TPU v7x, 256 devices: a whole 4x4x8 slice. The times are simulated.
256 devices in a mesh: src: 8 (over z_lo, core), brick: 32 (over x, y, z_hi).
Axes of the slice: x: 4, y: 4, z: 8 (z_hi: 2, z_lo: 4; z = z_hi * 4 + z_lo), core: 2. Of those that a mesh axis runs over, the one named last changes fastest.
Arguments:
- slowness: float32 [128, 64, 128], P('brick'), may hold values from 0.5 to 2
- source_x: int32 [16], P('src'), may hold values from 0 to 127
- source_y: int32 [16], P('src'), may hold values from 0 to 63
- source_z: int32 [16], P('src'), may hold values from 0 to 127
- station_x: int32 [2048], replicated, may hold values from 0 to 127
- station_y: int32 [2048], replicated, may hold values from 0 to 63
- station_z: int32 [2048], replicated, may hold values from 0 to 127
- observed: float32 [16, 2048], P('src'), may hold values from 0 to 4
Outputs:
- kernel: float32 [128, 64, 128], P('brick', 'src')
- arrivals: float32 [16, 2048], P('src', 'brick')
All inputs are finite; a program needn't handle non-finite values.
Results may differ from a plain program's by a relative error of at most 0.0003.
Values sent between devices are 32-bit elements; how exact they have to be, the bound alone decides.
No kernel may reach another device: no remote copies, remote signals or barrier semaphores. Data moves between devices by JAX's collectives and lax.ppermute only.
A program may use at most 128 MiB of HBM per device.

v0:
```python
import jax
import jax.numpy as jnp
from jax import lax
from jax.sharding import PartitionSpec as P

ITERS = 16


spacing = 0.015625
big_value = 1000000.0
start_slowness = 2.0


def extended(cells, sides, width):
    for axis, dim in sides:
        count = lax.axis_size(axis)
        ends = count - 1
        head = lax.slice_in_dim(cells, 0, width, axis=dim)
        tail = lax.slice_in_dim(cells, cells.shape[dim] - width, cells.shape[dim], axis=dim)
        cells = jnp.concatenate(
            [
                lax.ppermute(tail, axis, [(i, (i + 1) % count) for i in range(ends)]),
                cells,
                lax.ppermute(head, axis, [((i + 1) % count, i) for i in range(ends)]),
            ],
            axis=dim,
        )
    return cells


def neighbours(padded):
    return [
        padded[:, 2:, 1:-1, 1:-1],
        padded[:, :-2, 1:-1, 1:-1],
        padded[:, 1:-1, 2:, 1:-1],
        padded[:, 1:-1, :-2, 1:-1],
        padded[:, 1:-1, 1:-1, 2:],
        padded[:, 1:-1, 1:-1, :-2],
    ]


def per_device(slowness, source_x, source_y, source_z, station_x, station_y, station_z, observed):
    slabs = lax.axis_size("brick")
    slab_id = lax.axis_index("brick")
    cells_x, cells_y, cells_z = slowness.shape
    count = source_x.shape[0]
    grid_x = cells_x * slabs
    width = 1
    extent = cells_x + 2 * width
    first = slab_id * cells_x - width
    ext_x = first + jnp.arange(extent, dtype=jnp.int32)
    outside = ((ext_x < 0) | (ext_x >= grid_x))[None, :, None, None]
    slow_ext = extended(slowness, (("brick", 0),), width)[None]
    slow_pad = jnp.pad(slow_ext, ((0, 0), (1, 1), (1, 1), (1, 1)), constant_values=1.0)
    costs = [spacing * 0.5 * (slow_ext + other) for other in neighbours(slow_pad)]
    own_x = (slab_id * cells_x + jnp.arange(cells_x, dtype=jnp.int32)).astype(jnp.float32)
    pos_y = jnp.arange(cells_y, dtype=jnp.float32)[None, None, :, None]
    pos_z = jnp.arange(cells_z, dtype=jnp.float32)[None, None, None, :]
    dist = (
        (own_x[None, :, None, None] - source_x.astype(jnp.float32)[:, None, None, None]) ** 2
        + (pos_y - source_y.astype(jnp.float32)[:, None, None, None]) ** 2
        + (pos_z - source_z.astype(jnp.float32)[:, None, None, None]) ** 2
    )
    times = start_slowness * spacing * jnp.sqrt(dist)

    def forward_group(group, times):
        field = extended(times, (("brick", 1),), width)
        field = jnp.where(outside, big_value, field)
        padded = jnp.pad(field, ((0, 0), (1, 1), (1, 1), (1, 1)), constant_values=big_value)
        fresh = field
        for cost, other in zip(costs, neighbours(padded)):
            fresh = jnp.minimum(fresh, other + cost)
        field = jnp.where(outside, big_value, fresh)
        return field[:, width : width + cells_x]

    times = lax.fori_loop(0, ITERS // width, forward_group, times)
    times_ext = extended(times, (("brick", 1),), width)
    times_ext = jnp.where(outside, -big_value, times_ext)
    local_x = station_x - first
    inside_ext = (local_x >= 0) & (local_x < extent)
    owned = (local_x >= width) & (local_x < width + cells_x)
    flat = jnp.where(inside_ext, (local_x * cells_y + station_y) * cells_z + station_z, 0)
    values = times_ext.reshape(count, -1)[:, flat]
    arrive_part = jnp.where(owned[None, :], values, 0.0)
    arrivals = lax.psum_scatter(arrive_part, "brick", scatter_dimension=1, tiled=True)
    residual = jnp.where(inside_ext[None, :], values - observed, 0.0)
    source = jnp.zeros((count, extent * cells_y * cells_z), jnp.float32).at[:, flat].add(residual)
    source = source.reshape(count, extent, cells_y, cells_z)
    low_pad = jnp.pad(times_ext, ((0, 0), (1, 1), (1, 1), (1, 1)), constant_values=-big_value)
    weights = [jnp.maximum(other - times_ext, 0.0) / spacing for other in neighbours(low_pad)]
    denom = 1.0 + weights[0] + weights[1] + weights[2] + weights[3] + weights[4] + weights[5]

    def adjoint_group(group, field_own):
        field = extended(field_own, (("brick", 1),), width)
        padded = jnp.pad(field, ((0, 0), (1, 1), (1, 1), (1, 1)))
        acc = source
        for weight, other in zip(weights, neighbours(padded)):
            acc = acc + weight * other
        field = acc / denom
        return field[:, width : width + cells_x]

    adjoint = lax.fori_loop(
        0, ITERS // width, adjoint_group, jnp.zeros((count, cells_x, cells_y, cells_z), jnp.float32)
    )
    partial_sum = slowness * jnp.sum(adjoint, axis=0)
    kernel = lax.psum_scatter(partial_sum, "src", scatter_dimension=1, tiled=True)
    return (kernel, arrivals)


def solution(mesh):
    in_specs = (P("brick", None, None), P("src"), P("src"), P("src"), P(), P(), P(), P("src", None))
    out_specs = (P("brick", "src", None), P("src", "brick"))
    return jax.shard_map(
        per_device, mesh=mesh, in_specs=in_specs, out_specs=out_specs, check_vma=False
    )
```

profile of v0, /device:TPU:2, one launch (start us, length us, event | category | flops | bytes accessed | tf_op | source)
XLA Modules:
  0.0 761.3 jit_solution(2500943533203257311)
XLA Ops:
  8.0 9.1 %collective-permute-start.4 = (f32[1,64,128]{2,1,0:T(8,128)S(1)}, f32[1,64,128]{2,1,0:T(8,128)S(1)}, u32[]{:S(2)}, u32[]{:S(2)}) collective-permute-start(f32[1,64,128]{2,1,0:T(8,128)S(1)} %get-tuple-element.280), channel_id=1, source_target_pairs={{0,1},{1,2},{2,3},{3,4},{4,5},{5,6},{6,7},{7,8},{8,9},{9,10},{10,1... | collective-permute-start | bytes 98312 | tf_op jit(solution)/shard_map/ppermute | solution.py:22
  27.3 267.4 %while.24 = (s32[]{:T(128)}, f32[2,4,64,128]{3,2,1,0:T(8,128)S(1)}, f32[1,6,64,128]{3,2,1,0:T(8,128)S(1)}, f32[1,6,64,128]{3,2,1,0:T(8,128)S(1)}, f32[1,6,64,128...) while((s32[]{:T(128)}, f32[2,4,64,128]{3,2,1,0:T(8,128)S(1)}, ...), condition=%wide.region_1.2_spmd.clone, body=%wide.region_0.1_spmd.clone.sunk | while | flops 1245210 | bytes 8126673 | solution.py:76
  27.3 7.8 %collective-permute-start.2 = (f32[2,1,64,128]{3,2,1,0:T(8,128)S(1)}, f32[2,1,64,128]{3,2,1,0:T(8,128)S(1)}, u32[]{:S(2)}, u32[]{:S(2)}) collective-permute-start(f32[2,1,64,128]{3,2,1,0:T(8,128)S(1)} %get-tuple-element.424), channel_id=1, source_target_pairs={{1,0},{2,1},{3,2},{4,3},{5,4},{6,5},{7,6},{8,7},{9,8},{10,9},{11,1... | collective-permute-start | bytes 196616 | tf_op jit(solution)/shard_map/while/body/eval_jaxpr/ppermute | solution.py:24
  38.1 10.2 %collective-permute-done.3 = f32[2,1,64,128]{3,2,1,0:T(8,128)S(1)} collective-permute-done((f32[2,1,64,128]{3,2,1,0:T(8,128)S(1)}, f32[2,1,64,128]{3,2,1,0:T(8,128)S(1)}, u32[]{:S(2)}, u32[]{:S(2)}) %collective-permute-start.3) | collective-permute-done | bytes 65568 | tf_op jit(solution)/shard_map/while/body/eval_jaxpr/ppermute | solution.py:22
  51.1 7.8 %collective-permute-start.3 = (f32[2,1,64,128]{3,2,1,0:T(8,128)S(1)}, f32[2,1,64,128]{3,2,1,0:T(8,128)S(1)}, u32[]{:S(2)}, u32[]{:S(2)}) collective-permute-start(f32[2,1,64,128]{3,2,1,0:T(8,128)S(1)} %get-tuple-element.425), channel_id=1, source_target_pairs={{0,1},{1,2},{2,3},{3,4},{4,5},{5,6},{6,7},{7,8},{8,9},{9,10},{10,1... | collective-permute-start | bytes 196616 | tf_op jit(solution)/shard_map/while/body/eval_jaxpr/ppermute | solution.py:22
  68.8 6.1 collective-permute-start.3
  76.1 5.7 collective-permute-done.3
  84.6 7.8 %collective-permute-start.3 = (f32[2,1,64,128]{3,2,1,0:T(8,128)S(1)}, f32[2,1,64,128]{3,2,1,0:T(8,128)S(1)}, u32[]{:S(2)}, u32[]{:S(2)}) collective-permute-start(f32[2,1,64,128]{3,2,1,0:T(8,128)S(1)} %get-tuple-element.425), channel_id=1, source_target_pairs={{0,1},{1,2},{2,3},{3,4},{4,5},{5,6},{6,7},{7,8},{8,9},{9,10},{10,1... | collective-permute-start | bytes 196616 | tf_op jit(solution)/shard_map/while/body/eval_jaxpr/ppermute | solution.py:22
  101.4 7.4 collective-permute-start.3
  109.2 6.1 collective-permute-done.3
  118.0 7.8 %collective-permute-start.3 = (f32[2,1,64,128]{3,2,1,0:T(8,128)S(1)}, f32[2,1,64,128]{3,2,1,0:T(8,128)S(1)}, u32[]{:S(2)}, u32[]{:S(2)}) collective-permute-start(f32[2,1,64,128]{3,2,1,0:T(8,128)S(1)} %get-tuple-element.425), channel_id=1, source_target_pairs={{0,1},{1,2},{2,3},{3,4},{4,5},{5,6},{6,7},{7,8},{8,9},{9,10},{10,1... | collective-permute-start | bytes 196616 | tf_op jit(solution)/shard_map/while/body/eval_jaxpr/ppermute | solution.py:22
  135.8 5.8 collective-permute-start.3
  142.0 6.9 collective-permute-done.3
  151.6 7.8 %collective-permute-start.3 = (f32[2,1,64,128]{3,2,1,0:T(8,128)S(1)}, f32[2,1,64,128]{3,2,1,0:T(8,128)S(1)}, u32[]{:S(2)}, u32[]{:S(2)}) collective-permute-start(f32[2,1,64,128]{3,2,1,0:T(8,128)S(1)} %get-tuple-element.425), channel_id=1, source_target_pairs={{0,1},{1,2},{2,3},{3,4},{4,5},{5,6},{6,7},{7,8},{8,9},{9,10},{10,1... | collective-permute-start | bytes 196616 | tf_op jit(solution)/shard_map/while/body/eval_jaxpr/ppermute | solution.py:22
  168.1 7.8 %collective-permute-start.3 = (f32[2,1,64,128]{3,2,1,0:T(8,128)S(1)}, f32[2,1,64,128]{3,2,1,0:T(8,128)S(1)}, u32[]{:S(2)}, u32[]{:S(2)}) collective-permute-start(f32[2,1,64,128]{3,2,1,0:T(8,128)S(1)} %get-tuple-element.425), channel_id=1, source_target_pairs={{0,1},{1,2},{2,3},{3,4},{4,5},{5,6},{6,7},{7,8},{8,9},{9,10},{10,1... | collective-permute-start | bytes 196616 | tf_op jit(solution)/shard_map/while/body/eval_jaxpr/ppermute | solution.py:22
  185.3 7.8 %collective-permute-start.3 = (f32[2,1,64,128]{3,2,1,0:T(8,128)S(1)}, f32[2,1,64,128]{3,2,1,0:T(8,128)S(1)}, u32[]{:S(2)}, u32[]{:S(2)}) collective-permute-start(f32[2,1,64,128]{3,2,1,0:T(8,128)S(1)} %get-tuple-element.425), channel_id=1, source_target_pairs={{0,1},{1,2},{2,3},{3,4},{4,5},{5,6},{6,7},{7,8},{8,9},{9,10},{10,1... | collective-permute-start | bytes 196616 | tf_op jit(solution)/shard_map/while/body/eval_jaxpr/ppermute | solution.py:22
  201.1 7.8 %collective-permute-start.3 = (f32[2,1,64,128]{3,2,1,0:T(8,128)S(1)}, f32[2,1,64,128]{3,2,1,0:T(8,128)S(1)}, u32[]{:S(2)}, u32[]{:S(2)}) collective-permute-start(f32[2,1,64,128]{3,2,1,0:T(8,128)S(1)} %get-tuple-element.425), channel_id=1, source_target_pairs={{0,1},{1,2},{2,3},{3,4},{4,5},{5,6},{6,7},{7,8},{8,9},{9,10},{10,1... | collective-permute-start | bytes 196616 | tf_op jit(solution)/shard_map/while/body/eval_jaxpr/ppermute | solution.py:22
  217.0 7.8 %collective-permute-start.3 = (f32[2,1,64,128]{3,2,1,0:T(8,128)S(1)}, f32[2,1,64,128]{3,2,1,0:T(8,128)S(1)}, u32[]{:S(2)}, u32[]{:S(2)}) collective-permute-start(f32[2,1,64,128]{3,2,1,0:T(8,128)S(1)} %get-tuple-element.425), channel_id=1, source_target_pairs={{0,1},{1,2},{2,3},{3,4},{4,5},{5,6},{6,7},{7,8},{8,9},{9,10},{10,1... | collective-permute-start | bytes 196616 | tf_op jit(solution)/shard_map/while/body/eval_jaxpr/ppermute | solution.py:22
  232.8 7.8 %collective-permute-start.3 = (f32[2,1,64,128]{3,2,1,0:T(8,128)S(1)}, f32[2,1,64,128]{3,2,1,0:T(8,128)S(1)}, u32[]{:S(2)}, u32[]{:S(2)}) collective-permute-start(f32[2,1,64,128]{3,2,1,0:T(8,128)S(1)} %get-tuple-element.425), channel_id=1, source_target_pairs={{0,1},{1,2},{2,3},{3,4},{4,5},{5,6},{6,7},{7,8},{8,9},{9,10},{10,1... | collective-permute-start | bytes 196616 | tf_op jit(solution)/shard_map/while/body/eval_jaxpr/ppermute | solution.py:22
  249.3 7.8 %collective-permute-start.3 = (f32[2,1,64,128]{3,2,1,0:T(8,128)S(1)}, f32[2,1,64,128]{3,2,1,0:T(8,128)S(1)}, u32[]{:S(2)}, u32[]{:S(2)}) collective-permute-start(f32[2,1,64,128]{3,2,1,0:T(8,128)S(1)} %get-tuple-element.425), channel_id=1, source_target_pairs={{0,1},{1,2},{2,3},{3,4},{4,5},{5,6},{6,7},{7,8},{8,9},{9,10},{10,1... | collective-permute-start | bytes 196616 | tf_op jit(solution)/shard_map/while/body/eval_jaxpr/ppermute | solution.py:22
  265.1 7.8 %collective-permute-start.3 = (f32[2,1,64,128]{3,2,1,0:T(8,128)S(1)}, f32[2,1,64,128]{3,2,1,0:T(8,128)S(1)}, u32[]{:S(2)}, u32[]{:S(2)}) collective-permute-start(f32[2,1,64,128]{3,2,1,0:T(8,128)S(1)} %get-tuple-element.425), channel_id=1, source_target_pairs={{0,1},{1,2},{2,3},{3,4},{4,5},{5,6},{6,7},{7,8},{8,9},{9,10},{10,1... | collective-permute-start | bytes 196616 | tf_op jit(solution)/shard_map/while/body/eval_jaxpr/ppermute | solution.py:22
  280.9 7.8 %collective-permute-start.3 = (f32[2,1,64,128]{3,2,1,0:T(8,128)S(1)}, f32[2,1,64,128]{3,2,1,0:T(8,128)S(1)}, u32[]{:S(2)}, u32[]{:S(2)}) collective-permute-start(f32[2,1,64,128]{3,2,1,0:T(8,128)S(1)} %get-tuple-element.425), channel_id=1, source_target_pairs={{0,1},{1,2},{2,3},{3,4},{4,5},{5,6},{6,7},{7,8},{8,9},{9,10},{10,1... | collective-permute-start | bytes 196616 | tf_op jit(solution)/shard_map/while/body/eval_jaxpr/ppermute | solution.py:22
  300.3 7.2 collective-permute-start.7
  310.4 12.6 %copy.10 = f32[2,6,64,128]{0,3,2,1:T(8,128)} copy(f32[2,6,64,128]{3,2,1,0:T(8,128)S(1)} %constant_dynamic-update-slice_fusion) | data formatting | bytes 786432 | tf_op jit(solution)/shard_map/concatenate | solution.py:20
  323.2 27.4 %bitcast_select_fusion = f32[2,49152]{0,1:T(8,128)} fusion(f32[2,6,64,128]{0,3,2,1:T(8,128)} %copy.10, pred[49152]{0:T(1024)(128)(4,1)S(1)} %bitcast.46), kind=kLoop, calls=%fused_computation.50 | loop fusion | flops 98304 | bytes 835584 | tf_op jit(solution)/shard_map/jit(_where)/select_n | solution.py:78
  350.6 13.6 %gather_fusion = f32[2048,2]{1,0:T(8,128)S(1)} fusion(f32[2,49152]{0,1:T(8,128)} %bitcast_select_fusion, s32[2048]{0:T(1024)S(1)} %get-tuple-element.254), kind=kCustom, calls=%fused_computation | custom fusion | bytes 40960 | tf_op jit(solution)/shard_map/gather | solution.py:83
  364.2 25.3 %scatter_custom_fusion = f32[2,49152]{0,1:T(8,128)} fusion(s32[2048]{0:T(1024)} %get-tuple-element.255, f32[]{:T(128)} %constant.20.clone.1, f32[2,2048]{0,1:T(8,128)S(1)} %copy.11, f32[2048,2]{1,0:T(8,128)S(1)} %gather_fusion, pred[2048]{0:T(1024)(128)(4,1)S(1)} %get-tuple-element.283), kind=kCustom, calls=%fused_computation.51 | custom fusion | flops 12288 | bytes 429056 | tf_op jit(solution)/shard_map/scatter-add | solution.py:87
  389.5 14.7 %copy.12 = f32[2,6,64,128]{3,2,1,0:T(8,128)S(1)} copy(f32[2,6,64,128]{0,3,2,1:T(8,128)} %bitcast.39) | data formatting | bytes 786432 | tf_op jit(solution)/shard_map/while | solution.py:102
  406.9 286.0 %while.23 = (s32[]{:T(128)}, f32[2,4,64,128]{3,2,1,0:T(8,128)S(1)}, f32[2,6,64,128]{3,2,1,0:T(8,128)S(1)}, f32[2,6,64,128]{3,2,1,0:T(8,128)S(1)}, f32[2,6,64,128...) while((s32[]{:T(128)}, f32[2,4,64,128]{3,2,1,0:T(8,128)S(1)}, ...), condition=%wide.region_4.5_spmd, body=%wide.region_3.4_spmd.sunk | while | flops 3970434 | bytes 10772925 | solution.py:102
  407.6 10.2 %collective-permute-start = (f32[2,1,64,128]{3,2,1,0:T(8,128)}, f32[2,1,64,128]{3,2,1,0:T(8,128)S(1)}, u32[]{:S(2)}, u32[]{:S(2)}) collective-permute-start(f32[2,1,64,128]{3,2,1,0:T(8,128)} %get-tuple-element.407), channel_id=1, source_target_pairs={{1,0},{2,1},{3,2},{4,3},{5,4},{6,5},{7,6},{8,7},{9,8},{10,9},{11,1... | collective-permute-start | bytes 196616 | tf_op jit(solution)/shard_map/while/body/eval_jaxpr/ppermute | solution.py:24
  420.2 11.6 %collective-permute-done.1 = f32[2,1,64,128]{3,2,1,0:T(8,128)S(1)} collective-permute-done((f32[2,1,64,128]{3,2,1,0:T(8,128)}, f32[2,1,64,128]{3,2,1,0:T(8,128)S(1)}, u32[]{:S(2)}, u32[]{:S(2)}) %collective-permute-start.1) | collective-permute-done | bytes 65568 | tf_op jit(solution)/shard_map/while/body/eval_jaxpr/ppermute | solution.py:22
  435.5 7.8 %collective-permute-start.1 = (f32[2,1,64,128]{3,2,1,0:T(8,128)}, f32[2,1,64,128]{3,2,1,0:T(8,128)S(1)}, u32[]{:S(2)}, u32[]{:S(2)}) collective-permute-start(f32[2,1,64,128]{3,2,1,0:T(8,128)} %get-tuple-element.408), channel_id=1, source_target_pairs={{0,1},{1,2},{2,3},{3,4},{4,5},{5,6},{6,7},{7,8},{8,9},{9,10},{10,1... | collective-permute-start | bytes 196616 | tf_op jit(solution)/shard_map/while/body/eval_jaxpr/ppermute | solution.py:22
  443.9 5.8 collective-permute-done.1
  453.5 7.8 %collective-permute-start.1 = (f32[2,1,64,128]{3,2,1,0:T(8,128)}, f32[2,1,64,128]{3,2,1,0:T(8,128)S(1)}, u32[]{:S(2)}, u32[]{:S(2)}) collective-permute-start(f32[2,1,64,128]{3,2,1,0:T(8,128)} %get-tuple-element.408), channel_id=1, source_target_pairs={{0,1},{1,2},{2,3},{3,4},{4,5},{5,6},{6,7},{7,8},{8,9},{9,10},{10,1... | collective-permute-start | bytes 196616 | tf_op jit(solution)/shard_map/while/body/eval_jaxpr/ppermute | solution.py:22
  471.6 7.8 %collective-permute-start.1 = (f32[2,1,64,128]{3,2,1,0:T(8,128)}, f32[2,1,64,128]{3,2,1,0:T(8,128)S(1)}, u32[]{:S(2)}, u32[]{:S(2)}) collective-permute-start(f32[2,1,64,128]{3,2,1,0:T(8,128)} %get-tuple-element.408), channel_id=1, source_target_pairs={{0,1},{1,2},{2,3},{3,4},{4,5},{5,6},{6,7},{7,8},{8,9},{9,10},{10,1... | collective-permute-start | bytes 196616 | tf_op jit(solution)/shard_map/while/body/eval_jaxpr/ppermute | solution.py:22
  489.1 7.8 %collective-permute-start.1 = (f32[2,1,64,128]{3,2,1,0:T(8,128)}, f32[2,1,64,128]{3,2,1,0:T(8,128)S(1)}, u32[]{:S(2)}, u32[]{:S(2)}) collective-permute-start(f32[2,1,64,128]{3,2,1,0:T(8,128)} %get-tuple-element.408), channel_id=1, source_target_pairs={{0,1},{1,2},{2,3},{3,4},{4,5},{5,6},{6,7},{7,8},{8,9},{9,10},{10,1... | collective-permute-start | bytes 196616 | tf_op jit(solution)/shard_map/while/body/eval_jaxpr/ppermute | solution.py:22
  506.3 7.8 %collective-permute-start.1 = (f32[2,1,64,128]{3,2,1,0:T(8,128)}, f32[2,1,64,128]{3,2,1,0:T(8,128)S(1)}, u32[]{:S(2)}, u32[]{:S(2)}) collective-permute-start(f32[2,1,64,128]{3,2,1,0:T(8,128)} %get-tuple-element.408), channel_id=1, source_target_pairs={{0,1},{1,2},{2,3},{3,4},{4,5},{5,6},{6,7},{7,8},{8,9},{9,10},{10,1... | collective-permute-start | bytes 196616 | tf_op jit(solution)/shard_map/while/body/eval_jaxpr/ppermute | solution.py:22
  523.6 7.8 %collective-permute-start.1 = (f32[2,1,64,128]{3,2,1,0:T(8,128)}, f32[2,1,64,128]{3,2,1,0:T(8,128)S(1)}, u32[]{:S(2)}, u32[]{:S(2)}) collective-permute-start(f32[2,1,64,128]{3,2,1,0:T(8,128)} %get-tuple-element.408), channel_id=1, source_target_pairs={{0,1},{1,2},{2,3},{3,4},{4,5},{5,6},{6,7},{7,8},{8,9},{9,10},{10,1... | collective-permute-start | bytes 196616 | tf_op jit(solution)/shard_map/while/body/eval_jaxpr/ppermute | solution.py:22
  540.7 7.8 %collective-permute-start.1 = (f32[2,1,64,128]{3,2,1,0:T(8,128)}, f32[2,1,64,128]{3,2,1,0:T(8,128)S(1)}, u32[]{:S(2)}, u32[]{:S(2)}) collective-permute-start(f32[2,1,64,128]{3,2,1,0:T(8,128)} %get-tuple-element.408), channel_id=1, source_target_pairs={{0,1},{1,2},{2,3},{3,4},{4,5},{5,6},{6,7},{7,8},{8,9},{9,10},{10,1... | collective-permute-start | bytes 196616 | tf_op jit(solution)/shard_map/while/body/eval_jaxpr/ppermute | solution.py:22
  558.1 7.8 %collective-permute-start.1 = (f32[2,1,64,128]{3,2,1,0:T(8,128)}, f32[2,1,64,128]{3,2,1,0:T(8,128)S(1)}, u32[]{:S(2)}, u32[]{:S(2)}) collective-permute-start(f32[2,1,64,128]{3,2,1,0:T(8,128)} %get-tuple-element.408), channel_id=1, source_target_pairs={{0,1},{1,2},{2,3},{3,4},{4,5},{5,6},{6,7},{7,8},{8,9},{9,10},{10,1... | collective-permute-start | bytes 196616 | tf_op jit(solution)/shard_map/while/body/eval_jaxpr/ppermute | solution.py:22
  575.2 7.8 %collective-permute-start.1 = (f32[2,1,64,128]{3,2,1,0:T(8,128)}, f32[2,1,64,128]{3,2,1,0:T(8,128)S(1)}, u32[]{:S(2)}, u32[]{:S(2)}) collective-permute-start(f32[2,1,64,128]{3,2,1,0:T(8,128)} %get-tuple-element.408), channel_id=1, source_target_pairs={{0,1},{1,2},{2,3},{3,4},{4,5},{5,6},{6,7},{7,8},{8,9},{9,10},{10,1... | collective-permute-start | bytes 196616 | tf_op jit(solution)/shard_map/while/body/eval_jaxpr/ppermute | solution.py:22
  592.4 7.8 %collective-permute-start.1 = (f32[2,1,64,128]{3,2,1,0:T(8,128)}, f32[2,1,64,128]{3,2,1,0:T(8,128)S(1)}, u32[]{:S(2)}, u32[]{:S(2)}) collective-permute-start(f32[2,1,64,128]{3,2,1,0:T(8,128)} %get-tuple-element.408), channel_id=1, source_target_pairs={{0,1},{1,2},{2,3},{3,4},{4,5},{5,6},{6,7},{7,8},{8,9},{9,10},{10,1... | collective-permute-start | bytes 196616 | tf_op jit(solution)/shard_map/while/body/eval_jaxpr/ppermute | solution.py:22
  609.7 7.8 %collective-permute-start.1 = (f32[2,1,64,128]{3,2,1,0:T(8,128)}, f32[2,1,64,128]{3,2,1,0:T(8,128)S(1)}, u32[]{:S(2)}, u32[]{:S(2)}) collective-permute-start(f32[2,1,64,128]{3,2,1,0:T(8,128)} %get-tuple-element.408), channel_id=1, source_target_pairs={{0,1},{1,2},{2,3},{3,4},{4,5},{5,6},{6,7},{7,8},{8,9},{9,10},{10,1... | collective-permute-start | bytes 196616 | tf_op jit(solution)/shard_map/while/body/eval_jaxpr/ppermute | solution.py:22
  627.0 7.8 %collective-permute-start.1 = (f32[2,1,64,128]{3,2,1,0:T(8,128)}, f32[2,1,64,128]{3,2,1,0:T(8,128)S(1)}, u32[]{:S(2)}, u32[]{:S(2)}) collective-permute-start(f32[2,1,64,128]{3,2,1,0:T(8,128)} %get-tuple-element.408), channel_id=1, source_target_pairs={{0,1},{1,2},{2,3},{3,4},{4,5},{5,6},{6,7},{7,8},{8,9},{9,10},{10,1... | collective-permute-start | bytes 196616 | tf_op jit(solution)/shard_map/while/body/eval_jaxpr/ppermute | solution.py:22
  644.3 7.8 %collective-permute-start.1 = (f32[2,1,64,128]{3,2,1,0:T(8,128)}, f32[2,1,64,128]{3,2,1,0:T(8,128)S(1)}, u32[]{:S(2)}, u32[]{:S(2)}) collective-permute-start(f32[2,1,64,128]{3,2,1,0:T(8,128)} %get-tuple-element.408), channel_id=1, source_target_pairs={{0,1},{1,2},{2,3},{3,4},{4,5},{5,6},{6,7},{7,8},{8,9},{9,10},{10,1... | collective-permute-start | bytes 196616 | tf_op jit(solution)/shard_map/while/body/eval_jaxpr/ppermute | solution.py:22
  661.4 7.8 %collective-permute-start.1 = (f32[2,1,64,128]{3,2,1,0:T(8,128)}, f32[2,1,64,128]{3,2,1,0:T(8,128)S(1)}, u32[]{:S(2)}, u32[]{:S(2)}) collective-permute-start(f32[2,1,64,128]{3,2,1,0:T(8,128)} %get-tuple-element.408), channel_id=1, source_target_pairs={{0,1},{1,2},{2,3},{3,4},{4,5},{5,6},{6,7},{7,8},{8,9},{9,10},{10,1... | collective-permute-start | bytes 196616 | tf_op jit(solution)/shard_map/while/body/eval_jaxpr/ppermute | solution.py:22
  678.5 7.8 %collective-permute-start.1 = (f32[2,1,64,128]{3,2,1,0:T(8,128)}, f32[2,1,64,128]{3,2,1,0:T(8,128)S(1)}, u32[]{:S(2)}, u32[]{:S(2)}) collective-permute-start(f32[2,1,64,128]{3,2,1,0:T(8,128)} %get-tuple-element.408), channel_id=1, source_target_pairs={{0,1},{1,2},{2,3},{3,4},{4,5},{5,6},{6,7},{7,8},{8,9},{9,10},{10,1... | collective-permute-start | bytes 196616 | tf_op jit(solution)/shard_map/while/body/eval_jaxpr/ppermute | solution.py:22
  696.0 58.5 %reduce-scatter.3.cloned.1.call-done = f32[4,8,128]{2,1,0:T(8,128)} async-done(((f32[4,64,128]{2,1,0:T(8,128)}), f32[4,8,128]{2,1,0:T(8,128)}) %reduce-scatter.3.cloned.1.call-update) | async-done | bytes 16400 | tf_op jit(solution)/shard_map/reduce_scatter | solution.py:106
  (359 shorter events, 281.2 us)
Async XLA Ops:
  7.2 687.4 %reduce-scatter.5.cloned.1.call-start = ((), (), s32[]{:S(2)}) async-start(), calls=%async_computation.3 | async-start | bytes 1081344 | tf_op jit(solution)/shard_map/reduce_scatter | solution.py:85
  8.0 19.0 %collective-permute-start.4 = (f32[1,64,128]{2,1,0:T(8,128)S(1)}, f32[1,64,128]{2,1,0:T(8,128)S(1)}, u32[]{:S(2)}, u32[]{:S(2)}) collective-permute-start(f32[1,64,128]{2,1,0:T(8,128)S(1)} %get-tuple-element.280), channel_id=1, source_target_pairs={{0,1},{1,2},{2,3},{3,4},{4,5},{5,6},{6,7},{7,8},{8,9},{9,10},{10,1... | collective-permute-start | bytes 98312 | tf_op jit(solution)/shard_map/ppermute | solution.py:22
  35.2 13.2 %collective-permute-start.3 = (f32[2,1,64,128]{3,2,1,0:T(8,128)S(1)}, f32[2,1,64,128]{3,2,1,0:T(8,128)S(1)}, u32[]{:S(2)}, u32[]{:S(2)}) collective-permute-start(f32[2,1,64,128]{3,2,1,0:T(8,128)S(1)} %get-tuple-element.425), channel_id=1, source_target_pairs={{0,1},{1,2},{2,3},{3,4},{4,5},{5,6},{6,7},{7,8},{8,9},{9,10},{10,1... | collective-permute-start | bytes 196616 | tf_op jit(solution)/shard_map/while/body/eval_jaxpr/ppermute | solution.py:22
  49.1 10.8 %collective-permute-start.2 = (f32[2,1,64,128]{3,2,1,0:T(8,128)S(1)}, f32[2,1,64,128]{3,2,1,0:T(8,128)S(1)}, u32[]{:S(2)}, u32[]{:S(2)}) collective-permute-start(f32[2,1,64,128]{3,2,1,0:T(8,128)S(1)} %get-tuple-element.424), channel_id=1, source_target_pairs={{1,0},{2,1},{3,2},{4,3},{5,4},{6,5},{7,6},{8,7},{9,8},{10,9},{11,1... | collective-permute-start | bytes 196616 | tf_op jit(solution)/shard_map/while/body/eval_jaxpr/ppermute | solution.py:24
  51.1 13.3 %collective-permute-start.3 = (f32[2,1,64,128]{3,2,1,0:T(8,128)S(1)}, f32[2,1,64,128]{3,2,1,0:T(8,128)S(1)}, u32[]{:S(2)}, u32[]{:S(2)}) collective-permute-start(f32[2,1,64,128]{3,2,1,0:T(8,128)S(1)} %get-tuple-element.425), channel_id=1, source_target_pairs={{0,1},{1,2},{2,3},{3,4},{4,5},{5,6},{6,7},{7,8},{8,9},{9,10},{10,1... | collective-permute-start | bytes 196616 | tf_op jit(solution)/shard_map/while/body/eval_jaxpr/ppermute | solution.py:22
  65.1 11.0 %collective-permute-start.2 = (f32[2,1,64,128]{3,2,1,0:T(8,128)S(1)}, f32[2,1,64,128]{3,2,1,0:T(8,128)S(1)}, u32[]{:S(2)}, u32[]{:S(2)}) collective-permute-start(f32[2,1,64,128]{3,2,1,0:T(8,128)S(1)} %get-tuple-element.424), channel_id=1, source_target_pairs={{1,0},{2,1},{3,2},{4,3},{5,4},{6,5},{7,6},{8,7},{9,8},{10,9},{11,1... | collective-permute-start | bytes 196616 | tf_op jit(solution)/shard_map/while/body/eval_jaxpr/ppermute | solution.py:24
  68.8 13.1 %collective-permute-start.3 = (f32[2,1,64,128]{3,2,1,0:T(8,128)S(1)}, f32[2,1,64,128]{3,2,1,0:T(8,128)S(1)}, u32[]{:S(2)}, u32[]{:S(2)}) collective-permute-start(f32[2,1,64,128]{3,2,1,0:T(8,128)S(1)} %get-tuple-element.425), channel_id=1, source_target_pairs={{0,1},{1,2},{2,3},{3,4},{4,5},{5,6},{6,7},{7,8},{8,9},{9,10},{10,1... | collective-permute-start | bytes 196616 | tf_op jit(solution)/shard_map/while/body/eval_jaxpr/ppermute | solution.py:22
  84.6 13.7 %collective-permute-start.3 = (f32[2,1,64,128]{3,2,1,0:T(8,128)S(1)}, f32[2,1,64,128]{3,2,1,0:T(8,128)S(1)}, u32[]{:S(2)}, u32[]{:S(2)}) collective-permute-start(f32[2,1,64,128]{3,2,1,0:T(8,128)S(1)} %get-tuple-element.425), channel_id=1, source_target_pairs={{0,1},{1,2},{2,3},{3,4},{4,5},{5,6},{6,7},{7,8},{8,9},{9,10},{10,1... | collective-permute-start | bytes 196616 | tf_op jit(solution)/shard_map/while/body/eval_jaxpr/ppermute | solution.py:22
  101.4 14.0 %collective-permute-start.3 = (f32[2,1,64,128]{3,2,1,0:T(8,128)S(1)}, f32[2,1,64,128]{3,2,1,0:T(8,128)S(1)}, u32[]{:S(2)}, u32[]{:S(2)}) collective-permute-start(f32[2,1,64,128]{3,2,1,0:T(8,128)S(1)} %get-tuple-element.425), channel_id=1, source_target_pairs={{0,1},{1,2},{2,3},{3,4},{4,5},{5,6},{6,7},{7,8},{8,9},{9,10},{10,1... | collective-permute-start | bytes 196616 | tf_op jit(solution)/shard_map/while/body/eval_jaxpr/ppermute | solution.py:22
  118.0 13.1 %collective-permute-start.3 = (f32[2,1,64,128]{3,2,1,0:T(8,128)S(1)}, f32[2,1,64,128]{3,2,1,0:T(8,128)S(1)}, u32[]{:S(2)}, u32[]{:S(2)}) collective-permute-start(f32[2,1,64,128]{3,2,1,0:T(8,128)S(1)} %get-tuple-element.425), channel_id=1, source_target_pairs={{0,1},{1,2},{2,3},{3,4},{4,5},{5,6},{6,7},{7,8},{8,9},{9,10},{10,1... | collective-permute-start | bytes 196616 | tf_op jit(solution)/shard_map/while/body/eval_jaxpr/ppermute | solution.py:22
  135.8 13.1 %collective-permute-start.3 = (f32[2,1,64,128]{3,2,1,0:T(8,128)S(1)}, f32[2,1,64,128]{3,2,1,0:T(8,128)S(1)}, u32[]{:S(2)}, u32[]{:S(2)}) collective-permute-start(f32[2,1,64,128]{3,2,1,0:T(8,128)S(1)} %get-tuple-element.425), channel_id=1, source_target_pairs={{0,1},{1,2},{2,3},{3,4},{4,5},{5,6},{6,7},{7,8},{8,9},{9,10},{10,1... | collective-permute-start | bytes 196616 | tf_op jit(solution)/shard_map/while/body/eval_jaxpr/ppermute | solution.py:22
  151.6 13.8 %collective-permute-start.3 = (f32[2,1,64,128]{3,2,1,0:T(8,128)S(1)}, f32[2,1,64,128]{3,2,1,0:T(8,128)S(1)}, u32[]{:S(2)}, u32[]{:S(2)}) collective-permute-start(f32[2,1,64,128]{3,2,1,0:T(8,128)S(1)} %get-tuple-element.425), channel_id=1, source_target_pairs={{0,1},{1,2},{2,3},{3,4},{4,5},{5,6},{6,7},{7,8},{8,9},{9,10},{10,1... | collective-permute-start | bytes 196616 | tf_op jit(solution)/shard_map/while/body/eval_jaxpr/ppermute | solution.py:22
  166.2 11.5 %collective-permute-start.2 = (f32[2,1,64,128]{3,2,1,0:T(8,128)S(1)}, f32[2,1,64,128]{3,2,1,0:T(8,128)S(1)}, u32[]{:S(2)}, u32[]{:S(2)}) collective-permute-start(f32[2,1,64,128]{3,2,1,0:T(8,128)S(1)} %get-tuple-element.424), channel_id=1, source_target_pairs={{1,0},{2,1},{3,2},{4,3},{5,4},{6,5},{7,6},{8,7},{9,8},{10,9},{11,1... | collective-permute-start | bytes 196616 | tf_op jit(solution)/shard_map/while/body/eval_jaxpr/ppermute | solution.py:24
  168.1 14.4 %collective-permute-start.3 = (f32[2,1,64,128]{3,2,1,0:T(8,128)S(1)}, f32[2,1,64,128]{3,2,1,0:T(8,128)S(1)}, u32[]{:S(2)}, u32[]{:S(2)}) collective-permute-start(f32[2,1,64,128]{3,2,1,0:T(8,128)S(1)} %get-tuple-element.425), channel_id=1, source_target_pairs={{0,1},{1,2},{2,3},{3,4},{4,5},{5,6},{6,7},{7,8},{8,9},{9,10},{10,1... | collective-permute-start | bytes 196616 | tf_op jit(solution)/shard_map/while/body/eval_jaxpr/ppermute | solution.py:22
  185.3 13.1 %collective-permute-start.3 = (f32[2,1,64,128]{3,2,1,0:T(8,128)S(1)}, f32[2,1,64,128]{3,2,1,0:T(8,128)S(1)}, u32[]{:S(2)}, u32[]{:S(2)}) collective-permute-start(f32[2,1,64,128]{3,2,1,0:T(8,128)S(1)} %get-tuple-element.425), channel_id=1, source_target_pairs={{0,1},{1,2},{2,3},{3,4},{4,5},{5,6},{6,7},{7,8},{8,9},{9,10},{10,1... | collective-permute-start | bytes 196616 | tf_op jit(solution)/shard_map/while/body/eval_jaxpr/ppermute | solution.py:22
  201.1 13.2 %collective-permute-start.3 = (f32[2,1,64,128]{3,2,1,0:T(8,128)S(1)}, f32[2,1,64,128]{3,2,1,0:T(8,128)S(1)}, u32[]{:S(2)}, u32[]{:S(2)}) collective-permute-start(f32[2,1,64,128]{3,2,1,0:T(8,128)S(1)} %get-tuple-element.425), channel_id=1, source_target_pairs={{0,1},{1,2},{2,3},{3,4},{4,5},{5,6},{6,7},{7,8},{8,9},{9,10},{10,1... | collective-permute-start | bytes 196616 | tf_op jit(solution)/shard_map/while/body/eval_jaxpr/ppermute | solution.py:22
  217.0 13.1 %collective-permute-start.3 = (f32[2,1,64,128]{3,2,1,0:T(8,128)S(1)}, f32[2,1,64,128]{3,2,1,0:T(8,128)S(1)}, u32[]{:S(2)}, u32[]{:S(2)}) collective-permute-start(f32[2,1,64,128]{3,2,1,0:T(8,128)S(1)} %get-tuple-element.425), channel_id=1, source_target_pairs={{0,1},{1,2},{2,3},{3,4},{4,5},{5,6},{6,7},{7,8},{8,9},{9,10},{10,1... | collective-permute-start | bytes 196616 | tf_op jit(solution)/shard_map/while/body/eval_jaxpr/ppermute | solution.py:22
  232.8 13.8 %collective-permute-start.3 = (f32[2,1,64,128]{3,2,1,0:T(8,128)S(1)}, f32[2,1,64,128]{3,2,1,0:T(8,128)S(1)}, u32[]{:S(2)}, u32[]{:S(2)}) collective-permute-start(f32[2,1,64,128]{3,2,1,0:T(8,128)S(1)} %get-tuple-element.425), channel_id=1, source_target_pairs={{0,1},{1,2},{2,3},{3,4},{4,5},{5,6},{6,7},{7,8},{8,9},{9,10},{10,1... | collective-permute-start | bytes 196616 | tf_op jit(solution)/shard_map/while/body/eval_jaxpr/ppermute | solution.py:22
  249.3 13.1 %collective-permute-start.3 = (f32[2,1,64,128]{3,2,1,0:T(8,128)S(1)}, f32[2,1,64,128]{3,2,1,0:T(8,128)S(1)}, u32[]{:S(2)}, u32[]{:S(2)}) collective-permute-start(f32[2,1,64,128]{3,2,1,0:T(8,128)S(1)} %get-tuple-element.425), channel_id=1, source_target_pairs={{0,1},{1,2},{2,3},{3,4},{4,5},{5,6},{6,7},{7,8},{8,9},{9,10},{10,1... | collective-permute-start | bytes 196616 | tf_op jit(solution)/shard_map/while/body/eval_jaxpr/ppermute | solution.py:22
  265.1 13.1 %collective-permute-start.3 = (f32[2,1,64,128]{3,2,1,0:T(8,128)S(1)}, f32[2,1,64,128]{3,2,1,0:T(8,128)S(1)}, u32[]{:S(2)}, u32[]{:S(2)}) collective-permute-start(f32[2,1,64,128]{3,2,1,0:T(8,128)S(1)} %get-tuple-element.425), channel_id=1, source_target_pairs={{0,1},{1,2},{2,3},{3,4},{4,5},{5,6},{6,7},{7,8},{8,9},{9,10},{10,1... | collective-permute-start | bytes 196616 | tf_op jit(solution)/shard_map/while/body/eval_jaxpr/ppermute | solution.py:22
  280.9 13.1 %collective-permute-start.3 = (f32[2,1,64,128]{3,2,1,0:T(8,128)S(1)}, f32[2,1,64,128]{3,2,1,0:T(8,128)S(1)}, u32[]{:S(2)}, u32[]{:S(2)}) collective-permute-start(f32[2,1,64,128]{3,2,1,0:T(8,128)S(1)} %get-tuple-element.425), channel_id=1, source_target_pairs={{0,1},{1,2},{2,3},{3,4},{4,5},{5,6},{6,7},{7,8},{8,9},{9,10},{10,1... | collective-permute-start | bytes 196616 | tf_op jit(solution)/shard_map/while/body/eval_jaxpr/ppermute | solution.py:22
  294.7 13.1 %collective-permute-start.6 = (f32[2,1,64,128]{3,2,1,0:T(8,128)S(1)}, f32[2,1,64,128]{3,2,1,0:T(8,128)S(1)}, u32[]{:S(2)}, u32[]{:S(2)}) collective-permute-start(f32[2,1,64,128]{3,2,1,0:T(8,128)S(1)} %get-tuple-element.273), channel_id=1, source_target_pairs={{0,1},{1,2},{2,3},{3,4},{4,5},{5,6},{6,7},{7,8},{8,9},{9,10},{10,1... | collective-permute-start | bytes 196616 | tf_op jit(solution)/shard_map/ppermute | solution.py:22
  406.8 347.6 %reduce-scatter.3.cloned.1.call-start = ((), (), s32[]{:S(2)}) async-start(), calls=%async_computation.2 | async-start | bytes 147456 | tf_op jit(solution)/shard_map/reduce_scatter | solution.py:106
  407.6 12.6 %collective-permute-start = (f32[2,1,64,128]{3,2,1,0:T(8,128)}, f32[2,1,64,128]{3,2,1,0:T(8,128)S(1)}, u32[]{:S(2)}, u32[]{:S(2)}) collective-permute-start(f32[2,1,64,128]{3,2,1,0:T(8,128)} %get-tuple-element.407), channel_id=1, source_target_pairs={{1,0},{2,1},{3,2},{4,3},{5,4},{6,5},{7,6},{8,7},{9,8},{10,9},{11,1... | collective-permute-start | bytes 196616 | tf_op jit(solution)/shard_map/while/body/eval_jaxpr/ppermute | solution.py:24
  417.7 14.0 %collective-permute-start.1 = (f32[2,1,64,128]{3,2,1,0:T(8,128)}, f32[2,1,64,128]{3,2,1,0:T(8,128)S(1)}, u32[]{:S(2)}, u32[]{:S(2)}) collective-permute-start(f32[2,1,64,128]{3,2,1,0:T(8,128)} %get-tuple-element.408), channel_id=1, source_target_pairs={{0,1},{1,2},{2,3},{3,4},{4,5},{5,6},{6,7},{7,8},{8,9},{9,10},{10,1... | collective-permute-start | bytes 196616 | tf_op jit(solution)/shard_map/while/body/eval_jaxpr/ppermute | solution.py:22
  435.5 14.3 %collective-permute-start.1 = (f32[2,1,64,128]{3,2,1,0:T(8,128)}, f32[2,1,64,128]{3,2,1,0:T(8,128)S(1)}, u32[]{:S(2)}, u32[]{:S(2)}) collective-permute-start(f32[2,1,64,128]{3,2,1,0:T(8,128)} %get-tuple-element.408), channel_id=1, source_target_pairs={{0,1},{1,2},{2,3},{3,4},{4,5},{5,6},{6,7},{7,8},{8,9},{9,10},{10,1... | collective-permute-start | bytes 196616 | tf_op jit(solution)/shard_map/while/body/eval_jaxpr/ppermute | solution.py:22
  453.5 14.3 %collective-permute-start.1 = (f32[2,1,64,128]{3,2,1,0:T(8,128)}, f32[2,1,64,128]{3,2,1,0:T(8,128)S(1)}, u32[]{:S(2)}, u32[]{:S(2)}) collective-permute-start(f32[2,1,64,128]{3,2,1,0:T(8,128)} %get-tuple-element.408), channel_id=1, source_target_pairs={{0,1},{1,2},{2,3},{3,4},{4,5},{5,6},{6,7},{7,8},{8,9},{9,10},{10,1... | collective-permute-start | bytes 196616 | tf_op jit(solution)/shard_map/while/body/eval_jaxpr/ppermute | solution.py:22
  471.6 13.8 %collective-permute-start.1 = (f32[2,1,64,128]{3,2,1,0:T(8,128)}, f32[2,1,64,128]{3,2,1,0:T(8,128)S(1)}, u32[]{:S(2)}, u32[]{:S(2)}) collective-permute-start(f32[2,1,64,128]{3,2,1,0:T(8,128)} %get-tuple-element.408), channel_id=1, source_target_pairs={{0,1},{1,2},{2,3},{3,4},{4,5},{5,6},{6,7},{7,8},{8,9},{9,10},{10,1... | collective-permute-start | bytes 196616 | tf_op jit(solution)/shard_map/while/body/eval_jaxpr/ppermute | solution.py:22
  487.2 11.4 %collective-permute-start = (f32[2,1,64,128]{3,2,1,0:T(8,128)}, f32[2,1,64,128]{3,2,1,0:T(8,128)S(1)}, u32[]{:S(2)}, u32[]{:S(2)}) collective-permute-start(f32[2,1,64,128]{3,2,1,0:T(8,128)} %get-tuple-element.407), channel_id=1, source_target_pairs={{1,0},{2,1},{3,2},{4,3},{5,4},{6,5},{7,6},{8,7},{9,8},{10,9},{11,1... | collective-permute-start | bytes 196616 | tf_op jit(solution)/shard_map/while/body/eval_jaxpr/ppermute | solution.py:24
  489.1 13.5 %collective-permute-start.1 = (f32[2,1,64,128]{3,2,1,0:T(8,128)}, f32[2,1,64,128]{3,2,1,0:T(8,128)S(1)}, u32[]{:S(2)}, u32[]{:S(2)}) collective-permute-start(f32[2,1,64,128]{3,2,1,0:T(8,128)} %get-tuple-element.408), channel_id=1, source_target_pairs={{0,1},{1,2},{2,3},{3,4},{4,5},{5,6},{6,7},{7,8},{8,9},{9,10},{10,1... | collective-permute-start | bytes 196616 | tf_op jit(solution)/shard_map/while/body/eval_jaxpr/ppermute | solution.py:22
  504.4 12.1 %collective-permute-start = (f32[2,1,64,128]{3,2,1,0:T(8,128)}, f32[2,1,64,128]{3,2,1,0:T(8,128)S(1)}, u32[]{:S(2)}, u32[]{:S(2)}) collective-permute-start(f32[2,1,64,128]{3,2,1,0:T(8,128)} %get-tuple-element.407), channel_id=1, source_target_pairs={{1,0},{2,1},{3,2},{4,3},{5,4},{6,5},{7,6},{8,7},{9,8},{10,9},{11,1... | collective-permute-start | bytes 196616 | tf_op jit(solution)/shard_map/while/body/eval_jaxpr/ppermute | solution.py:24
  506.3 13.6 %collective-permute-start.1 = (f32[2,1,64,128]{3,2,1,0:T(8,128)}, f32[2,1,64,128]{3,2,1,0:T(8,128)S(1)}, u32[]{:S(2)}, u32[]{:S(2)}) collective-permute-start(f32[2,1,64,128]{3,2,1,0:T(8,128)} %get-tuple-element.408), channel_id=1, source_target_pairs={{0,1},{1,2},{2,3},{3,4},{4,5},{5,6},{6,7},{7,8},{8,9},{9,10},{10,1... | collective-permute-start | bytes 196616 | tf_op jit(solution)/shard_map/while/body/eval_jaxpr/ppermute | solution.py:22
  521.7 11.1 %collective-permute-start = (f32[2,1,64,128]{3,2,1,0:T(8,128)}, f32[2,1,64,128]{3,2,1,0:T(8,128)S(1)}, u32[]{:S(2)}, u32[]{:S(2)}) collective-permute-start(f32[2,1,64,128]{3,2,1,0:T(8,128)} %get-tuple-element.407), channel_id=1, source_target_pairs={{1,0},{2,1},{3,2},{4,3},{5,4},{6,5},{7,6},{8,7},{9,8},{10,9},{11,1... | collective-permute-start | bytes 196616 | tf_op jit(solution)/shard_map/while/body/eval_jaxpr/ppermute | solution.py:24
  523.6 13.4 %collective-permute-start.1 = (f32[2,1,64,128]{3,2,1,0:T(8,128)}, f32[2,1,64,128]{3,2,1,0:T(8,128)S(1)}, u32[]{:S(2)}, u32[]{:S(2)}) collective-permute-start(f32[2,1,64,128]{3,2,1,0:T(8,128)} %get-tuple-element.408), channel_id=1, source_target_pairs={{0,1},{1,2},{2,3},{3,4},{4,5},{5,6},{6,7},{7,8},{8,9},{9,10},{10,1... | collective-permute-start | bytes 196616 | tf_op jit(solution)/shard_map/while/body/eval_jaxpr/ppermute | solution.py:22
  538.8 11.4 %collective-permute-start = (f32[2,1,64,128]{3,2,1,0:T(8,128)}, f32[2,1,64,128]{3,2,1,0:T(8,128)S(1)}, u32[]{:S(2)}, u32[]{:S(2)}) collective-permute-start(f32[2,1,64,128]{3,2,1,0:T(8,128)} %get-tuple-element.407), channel_id=1, source_target_pairs={{1,0},{2,1},{3,2},{4,3},{5,4},{6,5},{7,6},{8,7},{9,8},{10,9},{11,1... | collective-permute-start | bytes 196616 | tf_op jit(solution)/shard_map/while/body/eval_jaxpr/ppermute | solution.py:24
  540.7 13.6 %collective-permute-start.1 = (f32[2,1,64,128]{3,2,1,0:T(8,128)}, f32[2,1,64,128]{3,2,1,0:T(8,128)S(1)}, u32[]{:S(2)}, u32[]{:S(2)}) collective-permute-start(f32[2,1,64,128]{3,2,1,0:T(8,128)} %get-tuple-element.408), channel_id=1, source_target_pairs={{0,1},{1,2},{2,3},{3,4},{4,5},{5,6},{6,7},{7,8},{8,9},{9,10},{10,1... | collective-permute-start | bytes 196616 | tf_op jit(solution)/shard_map/while/body/eval_jaxpr/ppermute | solution.py:22
  556.2 11.8 %collective-permute-start = (f32[2,1,64,128]{3,2,1,0:T(8,128)}, f32[2,1,64,128]{3,2,1,0:T(8,128)S(1)}, u32[]{:S(2)}, u32[]{:S(2)}) collective-permute-start(f32[2,1,64,128]{3,2,1,0:T(8,128)} %get-tuple-element.407), channel_id=1, source_target_pairs={{1,0},{2,1},{3,2},{4,3},{5,4},{6,5},{7,6},{8,7},{9,8},{10,9},{11,1... | collective-permute-start | bytes 196616 | tf_op jit(solution)/shard_map/while/body/eval_jaxpr/ppermute | solution.py:24
  558.1 13.4 %collective-permute-start.1 = (f32[2,1,64,128]{3,2,1,0:T(8,128)}, f32[2,1,64,128]{3,2,1,0:T(8,128)S(1)}, u32[]{:S(2)}, u32[]{:S(2)}) collective-permute-start(f32[2,1,64,128]{3,2,1,0:T(8,128)} %get-tuple-element.408), channel_id=1, source_target_pairs={{0,1},{1,2},{2,3},{3,4},{4,5},{5,6},{6,7},{7,8},{8,9},{9,10},{10,1... | collective-permute-start | bytes 196616 | tf_op jit(solution)/shard_map/while/body/eval_jaxpr/ppermute | solution.py:22
  573.3 11.0 %collective-permute-start = (f32[2,1,64,128]{3,2,1,0:T(8,128)}, f32[2,1,64,128]{3,2,1,0:T(8,128)S(1)}, u32[]{:S(2)}, u32[]{:S(2)}) collective-permute-start(f32[2,1,64,128]{3,2,1,0:T(8,128)} %get-tuple-element.407), channel_id=1, source_target_pairs={{1,0},{2,1},{3,2},{4,3},{5,4},{6,5},{7,6},{8,7},{9,8},{10,9},{11,1... | collective-permute-start | bytes 196616 | tf_op jit(solution)/shard_map/while/body/eval_jaxpr/ppermute | solution.py:24
  575.2 13.5 %collective-permute-start.1 = (f32[2,1,64,128]{3,2,1,0:T(8,128)}, f32[2,1,64,128]{3,2,1,0:T(8,128)S(1)}, u32[]{:S(2)}, u32[]{:S(2)}) collective-permute-start(f32[2,1,64,128]{3,2,1,0:T(8,128)} %get-tuple-element.408), channel_id=1, source_target_pairs={{0,1},{1,2},{2,3},{3,4},{4,5},{5,6},{6,7},{7,8},{8,9},{9,10},{10,1... | collective-permute-start | bytes 196616 | tf_op jit(solution)/shard_map/while/body/eval_jaxpr/ppermute | solution.py:22
  590.5 11.0 %collective-permute-start = (f32[2,1,64,128]{3,2,1,0:T(8,128)}, f32[2,1,64,128]{3,2,1,0:T(8,128)S(1)}, u32[]{:S(2)}, u32[]{:S(2)}) collective-permute-start(f32[2,1,64,128]{3,2,1,0:T(8,128)} %get-tuple-element.407), channel_id=1, source_target_pairs={{1,0},{2,1},{3,2},{4,3},{5,4},{6,5},{7,6},{8,7},{9,8},{10,9},{11,1... | collective-permute-start | bytes 196616 | tf_op jit(solution)/shard_map/while/body/eval_jaxpr/ppermute | solution.py:24
  592.4 13.5 %collective-permute-start.1 = (f32[2,1,64,128]{3,2,1,0:T(8,128)}, f32[2,1,64,128]{3,2,1,0:T(8,128)S(1)}, u32[]{:S(2)}, u32[]{:S(2)}) collective-permute-start(f32[2,1,64,128]{3,2,1,0:T(8,128)} %get-tuple-element.408), channel_id=1, source_target_pairs={{0,1},{1,2},{2,3},{3,4},{4,5},{5,6},{6,7},{7,8},{8,9},{9,10},{10,1... | collective-permute-start | bytes 196616 | tf_op jit(solution)/shard_map/while/body/eval_jaxpr/ppermute | solution.py:22
  609.7 13.6 %collective-permute-start.1 = (f32[2,1,64,128]{3,2,1,0:T(8,128)}, f32[2,1,64,128]{3,2,1,0:T(8,128)S(1)}, u32[]{:S(2)}, u32[]{:S(2)}) collective-permute-start(f32[2,1,64,128]{3,2,1,0:T(8,128)} %get-tuple-element.408), channel_id=1, source_target_pairs={{0,1},{1,2},{2,3},{3,4},{4,5},{5,6},{6,7},{7,8},{8,9},{9,10},{10,1... | collective-permute-start | bytes 196616 | tf_op jit(solution)/shard_map/while/body/eval_jaxpr/ppermute | solution.py:22
  625.1 11.3 %collective-permute-start = (f32[2,1,64,128]{3,2,1,0:T(8,128)}, f32[2,1,64,128]{3,2,1,0:T(8,128)S(1)}, u32[]{:S(2)}, u32[]{:S(2)}) collective-permute-start(f32[2,1,64,128]{3,2,1,0:T(8,128)} %get-tuple-element.407), channel_id=1, source_target_pairs={{1,0},{2,1},{3,2},{4,3},{5,4},{6,5},{7,6},{8,7},{9,8},{10,9},{11,1... | collective-permute-start | bytes 196616 | tf_op jit(solution)/shard_map/while/body/eval_jaxpr/ppermute | solution.py:24
  627.0 13.5 %collective-permute-start.1 = (f32[2,1,64,128]{3,2,1,0:T(8,128)}, f32[2,1,64,128]{3,2,1,0:T(8,128)S(1)}, u32[]{:S(2)}, u32[]{:S(2)}) collective-permute-start(f32[2,1,64,128]{3,2,1,0:T(8,128)} %get-tuple-element.408), channel_id=1, source_target_pairs={{0,1},{1,2},{2,3},{3,4},{4,5},{5,6},{6,7},{7,8},{8,9},{9,10},{10,1... | collective-permute-start | bytes 196616 | tf_op jit(solution)/shard_map/while/body/eval_jaxpr/ppermute | solution.py:22
  644.3 13.4 %collective-permute-start.1 = (f32[2,1,64,128]{3,2,1,0:T(8,128)}, f32[2,1,64,128]{3,2,1,0:T(8,128)S(1)}, u32[]{:S(2)}, u32[]{:S(2)}) collective-permute-start(f32[2,1,64,128]{3,2,1,0:T(8,128)} %get-tuple-element.408), channel_id=1, source_target_pairs={{0,1},{1,2},{2,3},{3,4},{4,5},{5,6},{6,7},{7,8},{8,9},{9,10},{10,1... | collective-permute-start | bytes 196616 | tf_op jit(solution)/shard_map/while/body/eval_jaxpr/ppermute | solution.py:22
  661.4 13.3 %collective-permute-start.1 = (f32[2,1,64,128]{3,2,1,0:T(8,128)}, f32[2,1,64,128]{3,2,1,0:T(8,128)S(1)}, u32[]{:S(2)}, u32[]{:S(2)}) collective-permute-start(f32[2,1,64,128]{3,2,1,0:T(8,128)} %get-tuple-element.408), channel_id=1, source_target_pairs={{0,1},{1,2},{2,3},{3,4},{4,5},{5,6},{6,7},{7,8},{8,9},{9,10},{10,1... | collective-permute-start | bytes 196616 | tf_op jit(solution)/shard_map/while/body/eval_jaxpr/ppermute | solution.py:22
  678.5 13.3 %collective-permute-start.1 = (f32[2,1,64,128]{3,2,1,0:T(8,128)}, f32[2,1,64,128]{3,2,1,0:T(8,128)S(1)}, u32[]{:S(2)}, u32[]{:S(2)}) collective-permute-start(f32[2,1,64,128]{3,2,1,0:T(8,128)} %get-tuple-element.408), channel_id=1, source_target_pairs={{0,1},{1,2},{2,3},{3,4},{4,5},{5,6},{6,7},{7,8},{8,9},{9,10},{10,1... | collective-permute-start | bytes 196616 | tf_op jit(solution)/shard_map/while/body/eval_jaxpr/ppermute | solution.py:22
  (25 other events, 272.7 us)
Sparse Core Ops, SparseCore 0:
  406.9 231.4 reduce-scatter.4
  694.7 59.7 reduce-scatter.2
where the time goes:
time: 764 us; the launch traced here: 761 us
  starting transfers between devices  340 us (45%)
  waiting for transfers between devices  256 us (34%)
  other arithmetic  90.9 us (12%)
  local copies, waits for them, and re-layouts  57.8 us (8%)
  between operations  14.2 us (2%)
    ppermute x34, starting transfers between devices, extended(): lax.ppermute(tail, axis, [(i, (i + 1) % count) for i in range(ends)])  249 us
    ppermute x34, waiting for transfers between devices, extended(): lax.ppermute(tail, axis, [(i, (i + 1) % count) for i in range(ends)])  168 us
    ppermute x34, starting transfers between devices, extended(): lax.ppermute(head, axis, [((i + 1) % count, i) for i in range(ends)])  91.2 us
    reduce_scatter x1, waiting for transfers between devices, per_device(): lax.psum_scatter(partial_sum, 'src', scatter_dimension=1, tiled=True)  58.5 us
    ppermute x34, waiting for transfers between devices, extended(): lax.ppermute(head, axis, [((i + 1) % count, i) for i in range(ends)])  28.6 us
    select_n x2, other arithmetic, per_device(): times_ext = jnp.where(outside, -big_value, times_ext)  27.5 us
    scatter-add x1, other arithmetic, per_device(): jnp.zeros((count, extent * cells_y * cells_z), jnp.float32).at[:, flat]  25.3 us
  transfers between devices with their start and end apart: 70, of which 67 were waited for; matrix products, arithmetic and copies ran while one was open for 5% of the time, Pallas kernels for 0%

commit v1 on v0

v1 whole, which is shorter than its diff:
```python
import jax
import jax.numpy as jnp
from jax import lax
from jax.experimental import pallas as pl
from jax.experimental.pallas import tpu as pltpu
from jax.sharding import Mesh, PartitionSpec as P

ITERS = 16
SPACING = 0.015625
BIG = 1000000.0
START = 2.0

LAYERS = 8
SEEN = 48
WIDE = SEEN + 2 * ITERS
ADJ = LAYERS + 2 * ITERS
NX, NY, NZ = 128, 64, 128


def iota(shape, dim):
    return lax.broadcasted_iota(jnp.int32, shape, dim)


def station_kernel(meta, sx, sy, sz, obs, count_out, seen_out, rhs):
    half, base = meta[0], meta[1]
    row = (sx[...] - base) * 64 + (sy[...] % 8) * 8 + sy[...] // 8
    seen = jnp.where(half == 0, obs[0:1, :], obs[1:2, :])
    hi = seen.astype(jnp.bfloat16).astype(jnp.float32)
    mid = (seen - hi).astype(jnp.bfloat16).astype(jnp.float32)
    low = seen - hi - mid
    there = iota((NZ, sx.shape[1]), 0) == sz[...]
    for part, value in enumerate((jnp.ones_like(seen), hi, mid, low)):
        rhs[part * NZ : (part + 1) * NZ, :] = jnp.where(there, value, 0.0).astype(jnp.bfloat16)
    chunk = 256

    def body(step, carry):
        match = iota((chunk, sx.shape[1]), 0) + step * chunk == row
        match = jnp.where(match, 1.0, 0.0).astype(jnp.bfloat16)
        got = lax.dot_general(
            match, rhs[...], (((1,), (1,)), ((), ())), preferred_element_type=jnp.float32
        )
        where = pl.ds(pl.multiple_of(step * chunk, chunk), chunk)
        count_out[where, :] = got[:, :NZ]
        seen_out[where, :] = got[:, NZ : 2 * NZ] + got[:, 2 * NZ : 3 * NZ] + got[:, 3 * NZ :]
        return carry

    lax.fori_loop(0, ADJ * 64 // chunk, body, 0)


def forward_kernel(meta, src_x, src_y, src_z, rows, lanes, mine, other, times_out, arrive_out, slow, even, odd, picked):
    half, core, offset, first = meta[0], meta[2], meta[3], meta[4]
    pos_x = src_x[half]
    pos_y = src_y[half]
    pos_z = src_z[half]
    row_y = iota((8, 8, NZ), 1) * 8 + iota((8, 8, NZ), 0) - pos_y
    row_z = iota((8, 8, NZ), 2) - pos_z
    dist_yz = (row_y * row_y + row_z * row_z).astype(jnp.float32)

    def load(layer, carry):
        a, b = mine[offset + layer], other[offset + layer]
        cells = jnp.concatenate([jnp.where(core == 0, a, b), jnp.where(core == 0, b, a)], axis=0)
        x = first + layer
        inside = (x >= 0) & (x < NX)
        dx = (x - pos_x).astype(jnp.float32)
        start = START * SPACING * jnp.sqrt(dist_yz + dx * dx)
        slow[layer] = jnp.where(inside, SPACING * cells, BIG)
        even[layer] = jnp.where(inside, start + (0.5 * SPACING) * cells, BIG)
        return carry

    lax.fori_loop(0, WIDE, load, 0, unroll=2)
    lane = iota((8, NZ), 1)
    sub = iota((8, NZ), 0)
    step = 2

    def sweep(before, after, k):
        def body(j, carry):
            layer = k + j * step
            near = before[pl.ds(layer - 1, step + 2)]
            here = near[1 : step + 1]
            best = jnp.minimum(near[:step], near[2:])
            left = jnp.where(lane == 0, BIG, pltpu.roll(here, 1, 3))
            right = jnp.where(lane == NZ - 1, BIG, pltpu.roll(here, NZ - 1, 3))
            best = jnp.minimum(best, jnp.minimum(left, right))
            down = jnp.where(sub == 0, BIG, pltpu.roll(here[:, 7:8], 1, 2))
            up = jnp.where(sub == 7, BIG, pltpu.roll(here[:, 0:1], 7, 2))
            below = jnp.concatenate([down, here[:, :7]], axis=1)
            above = jnp.concatenate([here[:, 1:], up], axis=1)
            best = jnp.minimum(best, jnp.minimum(below, above))
            after[pl.ds(layer, step)] = jnp.minimum(here, best + slow[pl.ds(layer, step)])
            return carry

        lax.fori_loop(0, (WIDE - 2 * k) // step, body, 0)

    for k in range(1, ITERS + 1):
        sweep(*((even, odd) if k % 2 else (odd, even)), k)

    def finish(layer, carry):
        x = first + ITERS + layer
        cells = even[ITERS + layer] - 0.5 * slow[ITERS + layer]
        cells = jnp.where((x >= 0) & (x < NX), cells, -BIG)
        times_out[pl.ds(pl.multiple_of(layer * 64, 64), 64), :] = cells.reshape(64, NZ)
        return carry

    lax.fori_loop(0, SEEN, finish, 0, unroll=2)
    one = iota((1, NZ), 1)

    def pick(j, carry):
        line = times_out[pl.ds(rows[j], 1), :]
        picked[pl.ds(j, 1), :] = jnp.where(one == lanes[j], line, 0.0)
        return carry

    lax.fori_loop(0, picked.shape[0], pick, 0, unroll=16)
    arrive_out[...] = lax.dot_general(
        jnp.ones((8, NZ), jnp.float32),
        picked[...],
        (((1,), (1,)), ((), ())),
        precision=lax.Precision.HIGHEST,
        preferred_element_type=jnp.float32,
    )


def adjoint_kernel(meta, times, count, seen, out, coef, even, odd):
    start = meta[5]
    lane = iota((8, NZ), 1)
    sub = iota((8, NZ), 0)

    def weights(layer, carry):
        here = times[start + layer]
        left = jnp.where(lane == 0, -BIG, pltpu.roll(here, 1, 2))
        right = jnp.where(lane == NZ - 1, -BIG, pltpu.roll(here, NZ - 1, 2))
        down = jnp.where(sub == 0, -BIG, pltpu.roll(here[7:8], 1, 1))
        up = jnp.where(sub == 7, -BIG, pltpu.roll(here[0:1], 7, 1))
        below = jnp.concatenate([down, here[:7]], axis=0)
        above = jnp.concatenate([here[1:], up], axis=0)
        others = (times[start + layer + 1], times[start + layer - 1], above, below, right, left)
        terms = [jnp.maximum(n - here, 0.0) * (1.0 / SPACING) for n in others]
        denom = 1.0 + terms[0] + terms[1] + terms[2] + terms[3] + terms[4] + terms[5]
        scale = 1.0 / denom
        for n, term in enumerate(terms):
            coef[n, layer] = term * scale
        first = (count[layer] * here - seen[layer]) * scale
        coef[6, layer] = first
        even[layer] = first
        return carry

    lax.fori_loop(1, ADJ - 1, weights, 0)
    step = 2

    def sweep(before, after, k):
        def body(j, carry):
            layer = k + j * step
            where = pl.ds(layer, step)
            near = before[pl.ds(layer - 1, step + 2)]
            here = near[1 : step + 1]
            left = pltpu.roll(here, 1, 3)
            right = pltpu.roll(here, NZ - 1, 3)
            below = jnp.concatenate([pltpu.roll(here[:, 7:8], 1, 2), here[:, :7]], axis=1)
            above = jnp.concatenate([here[:, 1:], pltpu.roll(here[:, 0:1], 7, 2)], axis=1)
            total = coef[6, where] + coef[0, where] * near[2:] + coef[1, where] * near[:step]
            total = total + coef[2, where] * above + coef[3, where] * below
            after[where] = total + (coef[4, where] * right + coef[5, where] * left)
            return carry

        lax.fori_loop(0, (ADJ - 2 * k) // step, body, 0)

    for k in range(2, ITERS + 1):
        sweep(*((odd, even) if k % 2 else (even, odd)), k)
    final = odd if ITERS % 2 == 0 else even
    for layer in range(LAYERS):
        for i in range(8):
            out[pl.ds(layer * 8 + i, 8, stride=64), :] = final[ITERS + layer, i]


def cycle(cells, axis, size, shift):
    return lax.ppermute(cells, axis, [(i, (i + shift) % size) for i in range(size)])


def gathered(cells, core, y, half):
    cells = cells.reshape(4, 8, 2, 4, NZ).transpose(0, 2, 3, 1, 4)
    part = lax.dynamic_index_in_dim(cells, core, 1, keepdims=False)
    partner = cycle(part, "half", 2, 1)
    slab = jnp.where(
        half == 0, jnp.concatenate([part, partner]), jnp.concatenate([partner, part])
    )
    line = jnp.zeros((4,) + slab.shape, jnp.float32)
    line = lax.dynamic_update_index_in_dim(line, slab, y, 0)
    for shift in (1, 3, 2):
        line = lax.dynamic_update_index_in_dim(line, cycle(slab, "y", 4, shift), (y - shift) % 4, 0)
    block = line.reshape((32,) + slab.shape[1:])
    before = lax.ppermute(block, "x", [(0, 1), (1, 2), (2, 3)])
    after = lax.ppermute(block, "x", [(1, 0), (2, 1), (3, 2)])
    mine = jnp.concatenate([before, block, after])
    return mine, cycle(mine, "core", 2, 1)


VMEM = pl.BlockSpec(memory_space=pltpu.VMEM)
SMEM = pl.BlockSpec(memory_space=pltpu.SMEM)


def f32(*shape):
    return jax.ShapeDtypeStruct(shape, jnp.float32)


def per_device(slowness, source_x, source_y, source_z, station_x, station_y, station_z, observed):
    core, x, y, half = (lax.axis_index(a) for a in ("core", "x", "y", "half"))
    group = lax.axis_index("zlo") * 2 + core
    slab = 4 * x + y
    back = jnp.where(y < 2, 16, 24)
    seen_first = slab * LAYERS - back
    slow_first = seen_first - ITERS
    meta = jnp.stack(
        [half, slab * LAYERS - ITERS, core, slow_first - 32 * (x - 1), slow_first, back - ITERS]
    ).astype(jnp.int32)

    stations = station_x.shape[0]
    params = pltpu.CompilerParams(vmem_limit_bytes=28 * 1024 * 1024)
    count, seen = pl.pallas_call(
        station_kernel,
        out_shape=(f32(ADJ * 64, NZ), f32(ADJ * 64, NZ)),
        in_specs=[SMEM, VMEM, VMEM, VMEM, VMEM],
        out_specs=(VMEM, VMEM),
        scratch_shapes=[pltpu.VMEM((4 * NZ, stations), jnp.bfloat16)],
        compiler_params=params,
        cost_estimate=pl.CostEstimate(
            flops=2 * ADJ * 64 * stations * 4 * NZ, bytes_accessed=2 * ADJ * 64 * NZ * 4, transcendentals=0
        ),
        name="stations",
    )(meta, station_x.reshape(1, -1), station_y.reshape(1, -1), station_z.reshape(1, -1), observed)

    def line_of(values):
        return lax.dynamic_index_in_dim(values.reshape(4, 4, stations // 16), y, 1, keepdims=False)

    at_x, at_y, at_z = line_of(station_x), line_of(station_y), line_of(station_z)
    owned = at_x // 32 == x
    rows = jnp.where(owned, (at_x - seen_first) * 64 + (at_y % 8) * 8 + at_y // 8, 0).reshape(-1)
    lanes = jnp.where(owned, at_z, -1).reshape(-1)

    mine, other = gathered(slowness, core, y, half)
    times, arrive = pl.pallas_call(
        forward_kernel,
        out_shape=(f32(SEEN * 64, NZ), f32(8, stations // 4)),
        in_specs=[SMEM] * 6 + [VMEM, VMEM],
        out_specs=(VMEM, VMEM),
        scratch_shapes=[
            pltpu.VMEM((WIDE, 8, 8, NZ), jnp.float32),
            pltpu.VMEM((WIDE, 8, 8, NZ), jnp.float32),
            pltpu.VMEM((WIDE, 8, 8, NZ), jnp.float32),
            pltpu.VMEM((stations // 4, NZ), jnp.float32),
        ],
        compiler_params=params,
        cost_estimate=pl.CostEstimate(
            flops=7 * ITERS * WIDE * 8192, bytes_accessed=WIDE * 8192 * 8, transcendentals=WIDE * 8192
        ),
        name="forward",
    )(meta, source_x, source_y, source_z, rows, lanes, mine, other)

    arrive = arrive[0].reshape(4, stations // 16)
    got = lax.dynamic_index_in_dim(arrive, x, 0)
    for shift in (1, 2, 3):
        piece = lax.dynamic_index_in_dim(arrive, (x + shift) % 4, 0)
        got = got + cycle(piece, "x", 4, shift)

    pieces = pl.pallas_call(
        adjoint_kernel,
        out_shape=f32(512, NZ),
        in_specs=[SMEM, VMEM, VMEM, VMEM],
        out_specs=VMEM,
        scratch_shapes=[
            pltpu.VMEM((7, ADJ, 8, 8, NZ), jnp.float32),
            pltpu.VMEM((ADJ, 8, 8, NZ), jnp.float32),
            pltpu.VMEM((ADJ, 8, 8, NZ), jnp.float32),
        ],
        compiler_params=params,
        cost_estimate=pl.CostEstimate(
            flops=12 * ITERS * ADJ * 8192, bytes_accessed=4 * ADJ * 8192 * 4, transcendentals=ADJ * 8192
        ),
        name="adjoint",
    )(
        meta,
        times.reshape(SEEN, 8, 8, NZ),
        count.reshape(ADJ, 8, 8, NZ),
        seen.reshape(ADJ, 8, 8, NZ),
    )
    summed = jnp.sum(
        lax.all_to_all(pieces.reshape(16, 4, 8, NZ), ("zlo", "core", "half"), 0, 0, tiled=True), axis=0
    )
    kernel = lax.dynamic_slice(slowness, (0, group * 8, 0), (4, 8, NZ)) * summed

    got = got.reshape(2, stations // 32)
    own = lax.dynamic_index_in_dim(got, half, 0)
    partner = cycle(lax.dynamic_index_in_dim(got, 1 - half, 0), "half", 2, 1)
    arrivals = jnp.where(half == 0, jnp.concatenate([own, partner]), jnp.concatenate([partner, own]))
    return kernel, arrivals


def solution(mesh):
    fine = Mesh(mesh.devices.reshape(4, 2, 4, 4, 2), ("zlo", "core", "x", "y", "half"))
    src, brick = ("zlo", "core"), ("x", "y", "half")
    in_specs = (P(brick, None, None), P(src), P(src), P(src), P(), P(), P(), P(src, None))
    out_specs = (P(brick, src, None), P(src, brick))
    return jax.shard_map(
        per_device, mesh=fine, in_specs=in_specs, out_specs=out_specs, check_vma=False
    )
```

time: 764 us -> 152 us (0.20)
  starting transfers between devices: 340 us -> 34.5 us
  waiting for transfers between devices: 256 us -> 23 us
  other arithmetic: 90.9 us -> 2.12 us
  Pallas kernels: 0 us -> 88.6 us
  local copies, waits for them, and re-layouts: 57.8 us -> 1.2 us
  between operations: 14.2 us -> 0.93 us
    ppermute x68 -> x11, starting transfers between devices: 340 us -> 27.9 us  [the longest x9 21.9 us: cycle(): lax.ppermute(cells, axis, [(i, (i + shift) % size) for i in range(size)])]
    ppermute x68 -> x11, waiting for transfers between devices: 197 us -> 23 us  [the longest x9 11.7 us: cycle(): lax.ppermute(cells, axis, [(i, (i + shift) % size) for i in range(size)])]
    pallas_call x0 -> x3, Pallas kernels: none -> 88.6 us  [the longest x1 57.5 us: per_device(): pl.pallas_call(forward_kernel, out_shape=(f32(SEEN * 64, NZ), f32(8, stat...]
    reduce_scatter x2 -> x0, waiting for transfers between devices: 58.5 us -> none  [the longest x1 58.5 us: per_device(): lax.psum_scatter(partial_sum, 'src', scatter_dimension=1, tiled=True)]
    select_n x35 -> x3, other arithmetic: 34.4 us -> 0.6 us  [the longest x1 0.57 us: per_device(): jnp.where(half == 0, jnp.concatenate([own, partner]), jnp.concatenate([pa...]
    scatter-add x1 -> x0, other arithmetic: 25.3 us -> none  [per_device(): jnp.zeros((count, extent * cells_y * cells_z), jnp.float32).at[:, flat]]
    while x1 -> x0, local copies, waits for them, and re-layouts: 14.7 us -> none  [per_device(): lax.fori_loop(0, ITERS // width, adjoint_group, jnp.zeros((count, cells_x...]
    gather x1 -> x0, local copies, waits for them, and re-layouts: 13.6 us -> none  [per_device(): values = times_ext.reshape(count, -1)[:, flat]]
  transfers between devices with their start and end apart: 70 -> 12, of which waited for: 67 -> 9; matrix products, arithmetic and copies ran while one was open for 5% -> 1% of each run, Pallas kernels for 0% -> 6%
where the time goes in v1:
time: 152 us; the launch traced here: 150 us
  Pallas kernels  88.6 us (58%)
  starting transfers between devices  34.5 us (23%)
  waiting for transfers between devices  23 us (15%)
  other arithmetic  2.12 us (1%)
    pallas_call x1, Pallas kernels, per_device(): pl.pallas_call(forward_kernel, out_shape=(f32(SEEN * 64, NZ), f32(8, stat...  57.5 us
    pallas_call x1, Pallas kernels, per_device(): pl.pallas_call(adjoint_kernel, out_shape=f32(512, NZ), in_specs=[SMEM, VM...  22.8 us
    ppermute x9, starting transfers between devices, cycle(): lax.ppermute(cells, axis, [(i, (i + shift) % size) for i in range(size)])  21.9 us
    ppermute x9, waiting for transfers between devices, cycle(): lax.ppermute(cells, axis, [(i, (i + shift) % size) for i in range(size)])  11.7 us
    pallas_call x1, Pallas kernels, per_device(): pl.pallas_call(station_kernel, out_shape=(f32(ADJ * 64, NZ), f32(ADJ * 64...  8.4 us
    ppermute x1, waiting for transfers between devices, gathered(): before = lax.ppermute(block, 'x', [(0, 1), (1, 2), (2, 3)])  8.1 us
    all_to_all x1, starting transfers between devices, per_device(): lax.all_to_all(pieces.reshape(16, 4, 8, NZ), ('zlo', 'core', 'half'), 0,...  6.59 us
    ppermute x1, starting transfers between devices, gathered(): before = lax.ppermute(block, 'x', [(0, 1), (1, 2), (2, 3)])  3.53 us
  transfers between devices with their start and end apart: 12, of which 9 were waited for; matrix products, arithmetic and copies ran while one was open for 1% of the time, Pallas kernels for 6%

profile of v1, /device:TPU:2, one launch (start us, length us, event | category | flops | bytes accessed | tf_op | source)
XLA Modules:
  0.0 150.4 jit_solution(15129260413779229688)
XLA Ops:
  0.6 0.8 constant_dynamic-slice_fusion.6
  1.5 7.3 %collective-permute-start = (f32[4,4,8,128]{3,2,1,0:T(8,128)S(1)}, f32[4,4,8,128]{3,2,1,0:T(8,128)S(1)}, u32[]{:S(2)}, u32[]{:S(2)}) collective-permute-start(f32[4,4,8,128]{3,2,1,0:T(8,128)S(1)} %bitcast.49), channel_id=1, source_target_pairs={{0,1},{1,0},{2,3},{3,2},{4,5},{5,4},{6,7},{7,6},{8,9},{9,8},{10,11... | collective-permute-start | bytes 196616 | tf_op jit(solution)/shard_map/ppermute | solution.py:175
  8.8 2.4 %collective-permute-done = f32[4,4,8,128]{3,2,1,0:T(8,128)S(1)} collective-permute-done((f32[4,4,8,128]{3,2,1,0:T(8,128)S(1)}, f32[4,4,8,128]{3,2,1,0:T(8,128)S(1)}, u32[]{:S(2)}, u32[]{:S(2)}) %collective-permute-start) | collective-permute-done | bytes 65568 | tf_op jit(solution)/shard_map/ppermute | solution.py:175
  11.2 1.7 %collective-permute-start.1 = (f32[8,4,8,128]{3,2,1,0:T(8,128)S(1)}, f32[8,4,8,128]{3,2,1,0:T(8,128)S(1)}, u32[]{:S(2)}, u32[]{:S(2)}) collective-permute-start(f32[8,4,8,128]{3,2,1,0:T(8,128)S(1)} %maximum_select_fusion.1), channel_id=1, source_target_pairs={{0,2},{2,4},{4,6},{6,0},{1,3},{3,5},{5,7},{7,1},{8,10},{10,12},{12... | collective-permute-start | bytes 393224 | tf_op jit(solution)/shard_map/ppermute | solution.py:175
  12.9 1.7 %collective-permute-start.2 = (f32[8,4,8,128]{3,2,1,0:T(8,128)S(1)}, f32[8,4,8,128]{3,2,1,0:T(8,128)S(1)}, u32[]{:S(2)}, u32[]{:S(2)}) collective-permute-start(f32[8,4,8,128]{3,2,1,0:T(8,128)S(1)} %maximum_select_fusion.1), channel_id=1, source_target_pairs={{0,6},{2,0},{4,2},{6,4},{1,7},{3,1},{5,3},{7,5},{8,14},{10,8},{12,... | collective-permute-start | bytes 393224 | tf_op jit(solution)/shard_map/ppermute | solution.py:175
  14.5 2.0 %collective-permute-start.3 = (f32[8,4,8,128]{3,2,1,0:T(8,128)S(1)}, f32[8,4,8,128]{3,2,1,0:T(8,128)S(1)}, u32[]{:S(2)}, u32[]{:S(2)}) collective-permute-start(f32[8,4,8,128]{3,2,1,0:T(8,128)S(1)} %maximum_select_fusion.1), channel_id=1, source_target_pairs={{0,4},{2,6},{4,0},{6,2},{1,5},{3,7},{5,1},{7,3},{8,12},{10,14},{12... | collective-permute-start | bytes 393224 | tf_op jit(solution)/shard_map/ppermute | solution.py:175
  16.6 1.3 collective-permute-done.1
  17.9 0.9 collective-permute-done.2
  18.9 2.5 %collective-permute-done.3 = f32[8,4,8,128]{3,2,1,0:T(8,128)S(1)} collective-permute-done((f32[8,4,8,128]{3,2,1,0:T(8,128)S(1)}, f32[8,4,8,128]{3,2,1,0:T(8,128)S(1)}, u32[]{:S(2)}, u32[]{:S(2)}) %collective-permute-start.3) | collective-permute-done | bytes 131104 | tf_op jit(solution)/shard_map/ppermute | solution.py:175
  21.4 0.0 copy-start.2
  21.4 0.0 copy-start
  21.4 0.0 copy-start.1
  21.4 0.0 copy-start.6
  21.4 3.5 %collective-permute-start.4 = (f32[32,4,8,128]{3,2,1,0:T(8,128)S(1)}, f32[32,4,8,128]{3,2,1,0:T(8,128)S(1)}, u32[]{:S(2)}, u32[]{:S(2)}) collective-permute-start(f32[32,4,8,128]{3,2,1,0:T(8,128)S(1)} %bitcast.46), channel_id=1, source_target_pairs={{0,8},{8,16},{16,24},{1,9},{9,17},{17,25},{2,10},{10,18},{18,26},{... | collective-permute-start | bytes 1572872 | tf_op jit(solution)/shard_map/ppermute | solution.py:190
  25.0 2.5 %collective-permute-start.5 = (f32[32,4,8,128]{3,2,1,0:T(8,128)S(1)}, f32[32,4,8,128]{3,2,1,0:T(8,128)S(1)}, u32[]{:S(2)}, u32[]{:S(2)}) collective-permute-start(f32[32,4,8,128]{3,2,1,0:T(8,128)S(1)} %bitcast.47), channel_id=1, source_target_pairs={{8,0},{16,8},{24,16},{9,1},{17,9},{25,17},{10,2},{18,10},{26,18},{... | collective-permute-start | bytes 1572872 | tf_op jit(solution)/shard_map/ppermute | solution.py:191
  27.5 8.1 %collective-permute-done.4 = f32[32,4,8,128]{3,2,1,0:T(8,128)S(1)} collective-permute-done((f32[32,4,8,128]{3,2,1,0:T(8,128)S(1)}, f32[32,4,8,128]{3,2,1,0:T(8,128)S(1)}, u32[]{:S(2)}, u32[]{:S(2)}) %collective-permute-start.4) | collective-permute-done | bytes 524320 | tf_op jit(solution)/shard_map/ppermute | solution.py:190
  35.6 3.1 %collective-permute-done.5 = f32[32,4,8,128]{3,2,1,0:T(8,128)S(1)} collective-permute-done((f32[32,4,8,128]{3,2,1,0:T(8,128)S(1)}, f32[32,4,8,128]{3,2,1,0:T(8,128)S(1)}, u32[]{:S(2)}, u32[]{:S(2)}) %collective-permute-start.5) | collective-permute-done | bytes 524320 | tf_op jit(solution)/shard_map/ppermute | solution.py:191
  38.7 0.1 pad_maximum_fusion.mine
  38.8 0.1 collective-permute-start.6
  38.9 0.1 stack.27.meta
  39.0 0.0 copy-done.2
  39.0 0.0 copy-done
  39.0 0.0 copy-done.1
  39.1 0.0 copy-done.6
  39.1 0.0 copy-start.3
  39.1 0.0 copy-start.4
  39.1 0.0 copy-start.5
  39.1 8.4 %stations.1 = (f32[2560,128]{1,0:T(8,128)S(1)}, f32[2560,128]{1,0:T(8,128)S(1)}) custom-call(s32[6]{0:T(128)S(1)} %stack.27.meta, s32[1,2048]{1,0:T(1,128)S(1)} %bitcast.45, s32[1,2048]{1,0:T(1,128)S(1)} %bitcast.43, s32[1,2048]{1,0:T(1,128)S(1)} %bitcast.41, f32[2,2048]{1,0:T(2,128)S(1)} %copy-done.6), custom_call_target="tpu_custom_call" | custom-call | flops 5368709120 | bytes 2621440 | tf_op jit(solution)/shard_map/stations/pallas_call | solution.py:217
  47.5 0.0 collective-permute-done.6.other
  47.5 0.0 copy-done.3
  47.6 0.0 copy-done.4
  47.6 0.0 copy-done.5
  47.6 57.5 %forward.1 = (f32[3072,128]{1,0:T(8,128)S(1)}, f32[8,512]{1,0:T(8,128)S(1)}) custom-call(s32[6]{0:T(128)S(1)} %stack.27.meta, s32[2]{0:T(128)S(1)} %copy-done.3, s32[2]{0:T(128)S(1)} %copy-done.4, s32[2]{0:T(128)S(1)} %copy-done.5, s32[512]{0:T(512)S(1)} %get-tuple-element.16.rows, s32[512]{0:T(512)S(1)} %get-tuple-element.15.lanes, ...), custom_call_target="tpu_custom_call" | custom-call | flops 73400320 | bytes 5242880 | tf_op jit(solution)/shard_map/forward/pallas_call | solution.py:239
  105.1 22.8 %adjoint.1 = f32[512,128]{1,0:T(8,128)} custom-call(s32[6]{0:T(128)S(1)} %stack.27.meta, f32[48,8,8,128]{3,2,1,0:T(8,128)S(1)} %bitcast.37, f32[40,8,8,128]{3,2,1,0:T(8,128)S(1)} %bitcast.38, f32[40,8,8,128]{3,2,1,0:T(8,128)S(1)} %bitcast.39), custom_call_target="tpu_custom_call" | custom-call | flops 62914560 | bytes 5242880 | tf_op jit(solution)/shard_map/adjoint/pallas_call | solution.py:263
  127.8 6.6 %all-to-all-start = ((f32[16,4,8,128]{3,2,1,0:T(8,128)}), f32[16,4,8,128]{3,2,1,0:T(8,128)S(1)}, u32[]{:S(2)}, u32[]{:S(2)}) async-start(f32[16,4,8,128]{3,2,1,0:T(8,128)} %bitcast.29), calls=%async_computation | async-start | bytes 524288 | tf_op jit(solution)/shard_map/all_to_all | solution.py:285
  134.5 1.3 collective-permute-start.7
  135.8 1.4 collective-permute-start.8
  137.2 0.7 collective-permute-start.9
  137.9 0.2 collective-permute-done.7
  138.1 2.7 %collective-permute-done.8 = f32[1,128]{1,0:T(1,128)S(1)} collective-permute-done((f32[1,128]{1,0:T(1,128)S(1)}, f32[1,128]{1,0:T(1,128)S(1)}, u32[]{:S(2)}, u32[]{:S(2)}) %collective-permute-start.8) | collective-permute-done | bytes 544 | tf_op jit(solution)/shard_map/ppermute | solution.py:175
  140.8 0.0 collective-permute-done.9
  140.8 0.1 reshape.118
  140.9 5.8 %collective-permute-start.10 = (f32[1,64]{1,0:T(1,128)S(1)}, f32[1,64]{1,0:T(1,128)S(1)}, u32[]{:S(2)}, u32[]{:S(2)}) collective-permute-start(f32[1,64]{1,0:T(1,128)S(1)} %get-tuple-element.18), channel_id=1, source_target_pairs={{0,1},{1,0},{2,3},{3,2},{4,5},{5,4},{6,7},{7,6},{8,9},{9,8},{10,11... | collective-permute-start | bytes 776 | tf_op jit(solution)/shard_map/ppermute | solution.py:175
  146.8 1.7 %collective-permute-done.10 = f32[1,64]{1,0:T(1,128)S(1)} collective-permute-done((f32[1,64]{1,0:T(1,128)S(1)}, f32[1,64]{1,0:T(1,128)S(1)}, u32[]{:S(2)}, u32[]{:S(2)}) %collective-permute-start.10) | collective-permute-done | bytes 288 | tf_op jit(solution)/shard_map/ppermute | solution.py:175
  148.4 0.6 maximum_select_fusion.2
  149.0 0.0 all-to-all-done
  149.0 1.3 dynamic-slice_multiply_fusion
  (15 shorter events, 0.2 us)
Async XLA Ops:
  1.5 9.7 %collective-permute-start = (f32[4,4,8,128]{3,2,1,0:T(8,128)S(1)}, f32[4,4,8,128]{3,2,1,0:T(8,128)S(1)}, u32[]{:S(2)}, u32[]{:S(2)}) collective-permute-start(f32[4,4,8,128]{3,2,1,0:T(8,128)S(1)} %bitcast.49), channel_id=1, source_target_pairs={{0,1},{1,0},{2,3},{3,2},{4,5},{5,4},{6,7},{7,6},{8,9},{9,8},{10,11... | collective-permute-start | bytes 196616 | tf_op jit(solution)/shard_map/ppermute | solution.py:175
  11.2 6.7 %collective-permute-start.1 = (f32[8,4,8,128]{3,2,1,0:T(8,128)S(1)}, f32[8,4,8,128]{3,2,1,0:T(8,128)S(1)}, u32[]{:S(2)}, u32[]{:S(2)}) collective-permute-start(f32[8,4,8,128]{3,2,1,0:T(8,128)S(1)} %maximum_select_fusion.1), channel_id=1, source_target_pairs={{0,2},{2,4},{4,6},{6,0},{1,3},{3,5},{5,7},{7,1},{8,10},{10,12},{12... | collective-permute-start | bytes 393224 | tf_op jit(solution)/shard_map/ppermute | solution.py:175
  12.9 6.0 %collective-permute-start.2 = (f32[8,4,8,128]{3,2,1,0:T(8,128)S(1)}, f32[8,4,8,128]{3,2,1,0:T(8,128)S(1)}, u32[]{:S(2)}, u32[]{:S(2)}) collective-permute-start(f32[8,4,8,128]{3,2,1,0:T(8,128)S(1)} %maximum_select_fusion.1), channel_id=1, source_target_pairs={{0,6},{2,0},{4,2},{6,4},{1,7},{3,1},{5,3},{7,5},{8,14},{10,8},{12,... | collective-permute-start | bytes 393224 | tf_op jit(solution)/shard_map/ppermute | solution.py:175
  14.5 6.8 %collective-permute-start.3 = (f32[8,4,8,128]{3,2,1,0:T(8,128)S(1)}, f32[8,4,8,128]{3,2,1,0:T(8,128)S(1)}, u32[]{:S(2)}, u32[]{:S(2)}) collective-permute-start(f32[8,4,8,128]{3,2,1,0:T(8,128)S(1)} %maximum_select_fusion.1), channel_id=1, source_target_pairs={{0,4},{2,6},{4,0},{6,2},{1,5},{3,7},{5,1},{7,3},{8,12},{10,14},{12... | collective-permute-start | bytes 393224 | tf_op jit(solution)/shard_map/ppermute | solution.py:175
  21.4 17.6 %copy-start.2 = (s32[2048]{0:T(1024)S(1)}, s32[2048]{0:T(1024)}, u32[]{:S(2)}) copy-start(s32[2048]{0:T(1024)} %param.12) | copy-start | bytes 24580
  21.4 17.6 %copy-start = (s32[2048]{0:T(1024)S(1)}, s32[2048]{0:T(1024)}, u32[]{:S(2)}) copy-start(s32[2048]{0:T(1024)} %param.14) | copy-start | bytes 24580
  21.4 17.6 %copy-start.1 = (s32[2048]{0:T(1024)S(1)}, s32[2048]{0:T(1024)}, u32[]{:S(2)}) copy-start(s32[2048]{0:T(1024)} %param.13) | copy-start | bytes 24580
  21.4 17.7 %copy-start.6 = (f32[2,2048]{1,0:T(2,128)S(1)}, f32[2,2048]{1,0:T(2,128)}, u32[]{:S(2)}) copy-start(f32[2,2048]{1,0:T(2,128)} %obs.1) | copy-start | bytes 49156
  21.4 14.1 %collective-permute-start.4 = (f32[32,4,8,128]{3,2,1,0:T(8,128)S(1)}, f32[32,4,8,128]{3,2,1,0:T(8,128)S(1)}, u32[]{:S(2)}, u32[]{:S(2)}) collective-permute-start(f32[32,4,8,128]{3,2,1,0:T(8,128)S(1)} %bitcast.46), channel_id=1, source_target_pairs={{0,8},{8,16},{16,24},{1,9},{9,17},{17,25},{2,10},{10,18},{18,26},{... | collective-permute-start | bytes 1572872 | tf_op jit(solution)/shard_map/ppermute | solution.py:190
  25.0 13.7 %collective-permute-start.5 = (f32[32,4,8,128]{3,2,1,0:T(8,128)S(1)}, f32[32,4,8,128]{3,2,1,0:T(8,128)S(1)}, u32[]{:S(2)}, u32[]{:S(2)}) collective-permute-start(f32[32,4,8,128]{3,2,1,0:T(8,128)S(1)} %bitcast.47), channel_id=1, source_target_pairs={{8,0},{16,8},{24,16},{9,1},{17,9},{25,17},{10,2},{18,10},{26,18},{... | collective-permute-start | bytes 1572872 | tf_op jit(solution)/shard_map/ppermute | solution.py:191
  38.8 8.7 %collective-permute-start.6 = (f32[96,4,8,128]{3,2,1,0:T(8,128)S(1)}, f32[96,4,8,128]{3,2,1,0:T(8,128)S(1)}, u32[]{:S(2)}, u32[]{:S(2)}) collective-permute-start(f32[96,4,8,128]{3,2,1,0:T(8,128)S(1)} %pad_maximum_fusion.mine), channel_id=1, source_target_pairs={{0,32},{32,0},{1,33},{33,1},{2,34},{34,2},{3,35},{35,3},{4,36},{36... | collective-permute-start | bytes 4718600 | tf_op jit(solution)/shard_map/ppermute | solution.py:175
  39.1 8.5 %copy-start.3 = (s32[2]{0:T(128)S(1)}, s32[2]{0:T(128)}, u32[]{:S(2)}) copy-start(s32[2]{0:T(128)} %src_x.1) | copy-start | bytes 28
  39.1 8.5 %copy-start.4 = (s32[2]{0:T(128)S(1)}, s32[2]{0:T(128)}, u32[]{:S(2)}) copy-start(s32[2]{0:T(128)} %src_y.1) | copy-start | bytes 28
  39.1 8.5 %copy-start.5 = (s32[2]{0:T(128)S(1)}, s32[2]{0:T(128)}, u32[]{:S(2)}) copy-start(s32[2]{0:T(128)} %src_z.1) | copy-start | bytes 28
  127.8 21.2 %all-to-all-start = ((f32[16,4,8,128]{3,2,1,0:T(8,128)}), f32[16,4,8,128]{3,2,1,0:T(8,128)S(1)}, u32[]{:S(2)}, u32[]{:S(2)}) async-start(f32[16,4,8,128]{3,2,1,0:T(8,128)} %bitcast.29), calls=%async_computation | async-start | bytes 524288 | tf_op jit(solution)/shard_map/all_to_all | solution.py:285
  134.5 3.6 %collective-permute-start.7 = (f32[1,128]{1,0:T(1,128)S(1)}, f32[1,128]{1,0:T(1,128)S(1)}, u32[]{:S(2)}, u32[]{:S(2)}) collective-permute-start(f32[1,128]{1,0:T(1,128)S(1)} %get-tuple-element.12), channel_id=1, source_target_pairs={{0,8},{8,16},{16,24},{24,0},{1,9},{9,17},{17,25},{25,1},{2,10},{10... | collective-permute-start | bytes 1544 | tf_op jit(solution)/shard_map/ppermute | solution.py:175
  135.8 5.0 %collective-permute-start.8 = (f32[1,128]{1,0:T(1,128)S(1)}, f32[1,128]{1,0:T(1,128)S(1)}, u32[]{:S(2)}, u32[]{:S(2)}) collective-permute-start(f32[1,128]{1,0:T(1,128)S(1)} %get-tuple-element.14), channel_id=1, source_target_pairs={{0,16},{8,24},{16,0},{24,8},{1,17},{9,25},{17,1},{25,9},{2,18},{10... | collective-permute-start | bytes 1544 | tf_op jit(solution)/shard_map/ppermute | solution.py:175
  137.2 3.6 %collective-permute-start.9 = (f32[1,128]{1,0:T(1,128)S(1)}, f32[1,128]{1,0:T(1,128)S(1)}, u32[]{:S(2)}, u32[]{:S(2)}) collective-permute-start(f32[1,128]{1,0:T(1,128)S(1)} %get-tuple-element.13), channel_id=1, source_target_pairs={{0,24},{8,0},{16,8},{24,16},{1,25},{9,1},{17,9},{25,17},{2,26},{10... | collective-permute-start | bytes 1544 | tf_op jit(solution)/shard_map/ppermute | solution.py:175
  140.9 7.5 %collective-permute-start.10 = (f32[1,64]{1,0:T(1,128)S(1)}, f32[1,64]{1,0:T(1,128)S(1)}, u32[]{:S(2)}, u32[]{:S(2)}) collective-permute-start(f32[1,64]{1,0:T(1,128)S(1)} %get-tuple-element.18), channel_id=1, source_target_pairs={{0,1},{1,0},{2,3},{3,2},{4,5},{5,4},{6,7},{7,6},{8,9},{9,8},{10,11... | collective-permute-start | bytes 776 | tf_op jit(solution)/shard_map/ppermute | solution.py:175

commit v2 on v1

v2 whole, which is shorter than its diff:
```python
import jax
import jax.numpy as jnp
from jax import lax
from jax.experimental import pallas as pl
from jax.experimental.pallas import tpu as pltpu
from jax.sharding import Mesh, PartitionSpec as P

ITERS = 16
SPACING = 0.015625
BIG = 1000000.0
START = 2.0

LAYERS = 8
SEEN = 48
WIDE = SEEN + 2 * ITERS
ADJ = LAYERS + 2 * ITERS
NX, NY, NZ = 128, 64, 128
HALF = NZ // 2


def iota(shape, dim):
    return lax.broadcasted_iota(jnp.int32, shape, dim)


def parts(values):
    hi = values.astype(jnp.bfloat16).astype(jnp.float32)
    mid = (values - hi).astype(jnp.bfloat16).astype(jnp.float32)
    return hi, mid, values - hi - mid


def moved(values, inverse):
    z, lane = iota((NZ, NZ), 0), iota((NZ, NZ), 1)
    if inverse:
        z, lane = lane, z
    match = jnp.where((z % 2) * HALF + z // 2 == lane, 1.0, 0.0).astype(jnp.bfloat16)
    got = [
        jnp.dot(part.astype(jnp.bfloat16), match, preferred_element_type=jnp.float32)
        for part in parts(values)
    ]
    return got[0] + got[1] + got[2]


def paired(first, second, low):
    axis = first.ndim - 1
    even = jnp.where(low, first, pltpu.roll(second, HALF, axis))
    odd = jnp.where(low, pltpu.roll(first, HALF, axis), second)
    return jnp.stack([even, odd])


def parted(even, odd, low):
    axis = even.ndim - 1
    first = jnp.where(low, even, pltpu.roll(odd, HALF, axis))
    second = jnp.where(low, pltpu.roll(even, HALF, axis), odd)
    return first, second


def beside(here, edge):
    lane = iota((8, NZ), 1) % HALF
    sub = iota((8, NZ), 0)

    def bounded(mask, values):
        return values if edge is None else jnp.where(mask, edge, values)

    even, odd = here[:, 0:1], here[:, 1:2]
    same = jnp.concatenate([odd, even], axis=1)
    left = bounded(lane == 0, pltpu.roll(odd, 1, 4))
    right = bounded(lane == HALF - 1, pltpu.roll(even, NZ - 1, 4))
    rolled = jnp.concatenate([left, right], axis=1)
    down = bounded(sub == 0, pltpu.roll(here[:, :, 7:8], 1, 3))
    up = bounded(sub == 7, pltpu.roll(here[:, :, 0:1], 7, 3))
    below = jnp.concatenate([down, here[:, :, :7]], axis=2)
    above = jnp.concatenate([here[:, :, 1:], up], axis=2)
    return same, rolled, below, above


def sweeps(first, last, count, step, even, odd, block):
    for k in range(first, last + 1):
        before, after = (even, odd) if k % 2 == first % 2 else (odd, even)
        whole, rest = divmod(count - k, step)

        def body(j, carry, before=before, after=after, k=k):
            block(before, after, k + j * step, step)
            return carry

        lax.fori_loop(0, whole, body, 0)
        if rest:
            block(before, after, count - rest, rest)
        after[count] = pltpu.roll(after[count - 1], HALF, 3)
    return after


def prepare_kernel(meta, cells, out):
    core = meta[2]
    rows = [
        cells[pl.ds(layer * NY + 4 * core + i, 8, stride=8), :] for layer in range(4) for i in range(4)
    ]
    out[...] = moved(jnp.concatenate(rows), False)


def station_kernel(meta, sx, sy, sz, obs, count_out, seen_out, rhs):
    half, base = meta[0], meta[1]
    x, y, z = sx[...] - base, sy[...], sz[...]
    layer = jnp.minimum(x, ADJ - 1 - x)
    row = (layer * 2 + z % 2) * NY + (y % 8) * 8 + y // 8
    row = jnp.where(layer >= 0, row, -1)
    lane = jnp.where(x < ADJ // 2, 0, HALF) + z // 2
    seen = jnp.where(half == 0, obs[0:1, :], obs[1:2, :])
    there = iota((NZ, sx.shape[1]), 0) == lane
    for part, value in enumerate((jnp.ones_like(seen),) + parts(seen)):
        rhs[part * NZ : (part + 1) * NZ, :] = jnp.where(there, value, 0.0).astype(jnp.bfloat16)
    chunk = 256

    def body(step, carry):
        match = iota((chunk, sx.shape[1]), 0) + step * chunk == row
        match = jnp.where(match, 1.0, 0.0).astype(jnp.bfloat16)
        got = lax.dot_general(
            match, rhs[...], (((1,), (1,)), ((), ())), preferred_element_type=jnp.float32
        )
        where = pl.ds(pl.multiple_of(step * chunk, chunk), chunk)
        count_out[where, :] = got[:, :NZ]
        seen_out[where, :] = got[:, NZ : 2 * NZ] + got[:, 2 * NZ : 3 * NZ] + got[:, 3 * NZ :]
        return carry

    lax.fori_loop(0, ADJ * NY // chunk, body, 0)


def forward_kernel(meta, src_x, src_y, src_z, rows, lanes, mine, other, times_out, arrive_out, slow, even, odd, table, picked):
    half, core, offset, first = meta[0], meta[2], meta[3], meta[4]
    shape = (2, 8, 8, NZ)
    low = iota((8, NZ), 1) < HALF
    dy = iota(shape, 2) * 8 + iota(shape, 1) - src_y[half]
    dz = iota(shape, 3) % HALF * 2 + iota(shape, 0) - src_z[half]
    dist_yz = (dy * dy + dz * dz).astype(jnp.float32)
    row_x = jnp.where(low, first, first + WIDE - 1)
    sign = jnp.where(low, 1, -1)

    def of_layer(layer):
        a, b = mine[offset + layer], other[offset + layer]
        return jnp.concatenate([jnp.where(core == 0, a, b), jnp.where(core == 0, b, a)], axis=0)

    def load(layer, carry):
        cells = paired(of_layer(layer), of_layer(WIDE - 1 - layer), low)
        x = row_x + sign * layer
        inside = (x >= 0) & (x < NX)
        dx = (x - src_x[half]).astype(jnp.float32)
        start = START * SPACING * jnp.sqrt(dist_yz + dx * dx)
        slow[layer] = jnp.where(inside, SPACING * cells, BIG)
        even[layer] = jnp.where(inside, start + (0.5 * SPACING) * cells, BIG)
        return carry

    lax.fori_loop(0, WIDE // 2, load, 0, unroll=4)

    def block(before, after, layer, step):
        near = before[pl.ds(layer - 1, step + 2)]
        here = near[1 : step + 1]
        best = jnp.minimum(near[:step], near[2:])
        same, rolled, below, above = beside(here, BIG)
        best = jnp.minimum(best, jnp.minimum(same, rolled))
        best = jnp.minimum(best, jnp.minimum(below, above))
        after[pl.ds(layer, step)] = jnp.minimum(here, best + slow[pl.ds(layer, step)])

    even[WIDE // 2] = pltpu.roll(even[WIDE // 2 - 1], HALF, 3)
    last = sweeps(1, ITERS, WIDE // 2, 16, even, odd, block)

    def finish(j, carry):
        layer = ITERS + j
        x = row_x + sign * layer
        cells = last[layer] - 0.5 * slow[layer]
        cells = jnp.where((x >= 0) & (x < NX), cells, -BIG)
        table[pl.ds(pl.multiple_of(j * 2 * NY, 2 * NY), 2 * NY), :] = cells.reshape(2 * NY, NZ)
        times_out[j], times_out[SEEN - 1 - j] = parted(cells[0], cells[1], low)
        return carry

    lax.fori_loop(0, SEEN // 2, finish, 0, unroll=4)
    one = iota((1, NZ), 1)

    def pick(j, carry):
        line = table[pl.ds(rows[j], 1), :]
        picked[pl.ds(j, 1), :] = jnp.where(one == lanes[j], line, 0.0)
        return carry

    lax.fori_loop(0, picked.shape[0], pick, 0, unroll=16)
    arrive_out[...] = lax.dot_general(
        jnp.ones((8, NZ), jnp.float32),
        picked[...],
        (((1,), (1,)), ((), ())),
        precision=lax.Precision.HIGHEST,
        preferred_element_type=jnp.float32,
    )


def adjoint_kernel(meta, times, count, seen, out, coef, even, odd, natural):
    start = meta[5]
    low = iota((8, NZ), 1) < HALF
    top = ADJ // 2

    def load(layer, carry):
        odd[layer] = paired(times[start + layer], times[start + ADJ - 1 - layer], low)
        return carry

    lax.fori_loop(0, top, load, 0, unroll=4)
    odd[top] = pltpu.roll(odd[top - 1], HALF, 3)

    def weights(layer, carry):
        here = odd[pl.ds(layer, 1)]
        others = (odd[pl.ds(layer + 1, 1)], odd[pl.ds(layer - 1, 1)]) + beside(here, -BIG)
        terms = [jnp.maximum(n - here, 0.0) * (1.0 / SPACING) for n in others]
        denom = 1.0 + terms[0] + terms[1] + terms[2] + terms[3] + terms[4] + terms[5]
        scale = 1.0 / denom
        for n, term in enumerate(terms):
            coef[n, pl.ds(layer, 1)] = term * scale
        first = (count[pl.ds(layer, 1)] * here - seen[pl.ds(layer, 1)]) * scale
        coef[6, pl.ds(layer, 1)] = first
        even[pl.ds(layer, 1)] = first
        return carry

    lax.fori_loop(1, top, weights, 0)
    even[top] = pltpu.roll(even[top - 1], HALF, 3)

    def block(before, after, layer, step):
        where = pl.ds(layer, step)
        near = before[pl.ds(layer - 1, step + 2)]
        same, rolled, below, above = beside(near[1 : step + 1], None)
        total = coef[6, where] + coef[0, where] * near[2:] + coef[1, where] * near[:step]
        total = total + coef[2, where] * same + coef[4, where] * below
        after[where] = total + (coef[3, where] * rolled + coef[5, where] * above)

    final = sweeps(2, ITERS, top, 8, even, odd, block)
    for j in range(LAYERS // 2):
        cells = final[ITERS + j]
        natural[j], natural[LAYERS - 1 - j] = parted(cells[0], cells[1], low)
    rows = moved(natural[...].reshape(LAYERS * NY, NZ), True)
    for layer in range(LAYERS):
        for i in range(8):
            at = (layer * 8 + i) * 8
            out[pl.ds(layer * 8 + i, 8, stride=64), :] = rows[at : at + 8]


def cycle(cells, axis, size, shift):
    return lax.ppermute(cells, axis, [(i, (i + shift) % size) for i in range(size)])


def gathered(part, y, half, beside_it):
    partner = cycle(part, "half", 2, 1)
    slab = jnp.where(
        half == 0, jnp.concatenate([part, partner]), jnp.concatenate([partner, part])
    )
    line = jnp.zeros((4,) + slab.shape, jnp.float32)
    line = lax.dynamic_update_index_in_dim(line, slab, y, 0)
    for shift in (1, 3, 2):
        line = lax.dynamic_update_index_in_dim(line, cycle(slab, "y", 4, shift), (y - shift) % 4, 0)
    block = line.reshape((32,) + slab.shape[1:])
    before = lax.ppermute(block, "x", [(0, 1), (1, 2), (2, 3)])
    after = lax.ppermute(block, "x", [(1, 0), (2, 1), (3, 2)])
    before, after, beside_it = lax.optimization_barrier((before, after, beside_it))
    mine = jnp.concatenate([before, block, after])
    return mine, cycle(mine, "core", 2, 1), beside_it


VMEM = pl.BlockSpec(memory_space=pltpu.VMEM)
SMEM = pl.BlockSpec(memory_space=pltpu.SMEM)


def f32(*shape):
    return jax.ShapeDtypeStruct(shape, jnp.float32)


def per_device(slowness, source_x, source_y, source_z, station_x, station_y, station_z, observed):
    core, x, y, half = (lax.axis_index(a) for a in ("core", "x", "y", "half"))
    group = lax.axis_index("zlo") * 2 + core
    slab = 4 * x + y
    back = jnp.where(y < 2, 16, 24)
    seen_first = slab * LAYERS - back
    slow_first = seen_first - ITERS
    meta = jnp.stack(
        [half, slab * LAYERS - ITERS, core, slow_first - 32 * (x - 1), slow_first, back - ITERS]
    ).astype(jnp.int32)

    stations = station_x.shape[0]
    params = pltpu.CompilerParams(vmem_limit_bytes=28 * 1024 * 1024)
    count, seen = pl.pallas_call(
        station_kernel,
        out_shape=(f32(ADJ * 64, NZ), f32(ADJ * 64, NZ)),
        in_specs=[SMEM, VMEM, VMEM, VMEM, VMEM],
        out_specs=(VMEM, VMEM),
        scratch_shapes=[pltpu.VMEM((4 * NZ, stations), jnp.bfloat16)],
        compiler_params=params,
        cost_estimate=pl.CostEstimate(
            flops=2 * ADJ * 64 * stations * 4 * NZ, bytes_accessed=2 * ADJ * 64 * NZ * 4, transcendentals=0
        ),
        name="stations",
    )(meta, station_x.reshape(1, -1), station_y.reshape(1, -1), station_z.reshape(1, -1), observed)

    def line_of(values):
        return lax.dynamic_index_in_dim(values.reshape(4, 4, stations // 16), y, 1, keepdims=False)

    at_x, at_y, at_z = line_of(station_x), line_of(station_y), line_of(station_z)
    owned = at_x // 32 == x
    seen_x = at_x - seen_first
    layer = jnp.minimum(seen_x, SEEN - 1 - seen_x)
    row = (layer * 2 + at_z % 2) * NY + (at_y % 8) * 8 + at_y // 8
    rows = jnp.where(owned, row, 0).reshape(-1)
    lanes = jnp.where(owned, jnp.where(seen_x < SEEN // 2, 0, HALF) + at_z // 2, -1).reshape(-1)

    part = pl.pallas_call(
        prepare_kernel,
        out_shape=f32(128, NZ),
        in_specs=[SMEM, VMEM],
        out_specs=VMEM,
        compiler_params=params,
        name="prepare",
    )(meta, slowness.reshape(-1, NZ))
    mine, other, (count, seen) = gathered(part.reshape(4, 4, 8, NZ), y, half, (count, seen))
    times, arrive = pl.pallas_call(
        forward_kernel,
        out_shape=(f32(SEEN, 8, 8, NZ), f32(8, stations // 4)),
        in_specs=[SMEM] * 6 + [VMEM, VMEM],
        out_specs=(VMEM, VMEM),
        scratch_shapes=[
            pltpu.VMEM((WIDE // 2, 2, 8, 8, NZ), jnp.float32),
            pltpu.VMEM((WIDE // 2 + 1, 2, 8, 8, NZ), jnp.float32),
            pltpu.VMEM((WIDE // 2 + 1, 2, 8, 8, NZ), jnp.float32),
            pltpu.VMEM((SEEN * NY, NZ), jnp.float32),
            pltpu.VMEM((stations // 4, NZ), jnp.float32),
        ],
        compiler_params=params,
        cost_estimate=pl.CostEstimate(
            flops=7 * ITERS * WIDE * 8192, bytes_accessed=WIDE * 8192 * 8, transcendentals=WIDE * 8192
        ),
        name="forward",
    )(meta, source_x, source_y, source_z, rows, lanes, mine, other)

    arrive = arrive[0].reshape(4, stations // 16)
    got = lax.dynamic_index_in_dim(arrive, x, 0)
    for shift in (1, 2, 3):
        piece = lax.dynamic_index_in_dim(arrive, (x + shift) % 4, 0)
        got = got + cycle(piece, "x", 4, shift)

    pieces = pl.pallas_call(
        adjoint_kernel,
        out_shape=f32(512, NZ),
        in_specs=[SMEM, VMEM, VMEM, VMEM],
        out_specs=VMEM,
        scratch_shapes=[
            pltpu.VMEM((7, ADJ // 2, 2, 8, 8, NZ), jnp.float32),
            pltpu.VMEM((ADJ // 2 + 1, 2, 8, 8, NZ), jnp.float32),
            pltpu.VMEM((ADJ // 2 + 1, 2, 8, 8, NZ), jnp.float32),
            pltpu.VMEM((LAYERS, 8, 8, NZ), jnp.float32),
        ],
        compiler_params=params,
        cost_estimate=pl.CostEstimate(
            flops=12 * ITERS * ADJ * 8192, bytes_accessed=4 * ADJ * 8192 * 4, transcendentals=ADJ * 8192
        ),
        name="adjoint",
    )(
        meta,
        times,
        count.reshape(ADJ // 2, 2, 8, 8, NZ),
        seen.reshape(ADJ // 2, 2, 8, 8, NZ),
    )
    summed = jnp.sum(
        lax.all_to_all(pieces.reshape(16, 4, 8, NZ), ("zlo", "core", "half"), 0, 0, tiled=True), axis=0
    )
    kernel = lax.dynamic_slice(slowness, (0, group * 8, 0), (4, 8, NZ)) * summed

    got = got.reshape(2, stations // 32)
    own = lax.dynamic_index_in_dim(got, half, 0)
    partner = cycle(lax.dynamic_index_in_dim(got, 1 - half, 0), "half", 2, 1)
    arrivals = jnp.where(half == 0, jnp.concatenate([own, partner]), jnp.concatenate([partner, own]))
    return kernel, arrivals


def solution(mesh):
    fine = Mesh(mesh.devices.reshape(4, 2, 4, 4, 2), ("zlo", "core", "x", "y", "half"))
    src, brick = ("zlo", "core"), ("x", "y", "half")
    in_specs = (P(brick, None, None), P(src), P(src), P(src), P(), P(), P(), P(src, None))
    out_specs = (P(brick, src, None), P(src, brick))
    return jax.shard_map(
        per_device, mesh=fine, in_specs=in_specs, out_specs=out_specs, check_vma=False
    )
```

time: 152 us -> 95.2 us (0.63)
  Pallas kernels: 88.6 us -> 37.2 us
  waiting for transfers between devices: 23 us -> 17.8 us
    pallas_call x1 -> x2, Pallas kernels: 57.5 us -> 17.9 us  [the longest x1 17.2 us: per_device(): pl.pallas_call(forward_kernel, out_shape=(f32(SEEN, 8, 8, NZ), f32(8, sta...]
    pallas_call x1, Pallas kernels: 22.8 us -> 10.9 us  [per_device(): pl.pallas_call(adjoint_kernel, out_shape=f32(512, NZ), in_specs=[SMEM, VM...]
    ppermute x1, waiting for transfers between devices: 8.1 us -> 0.01 us  [gathered(): before = lax.ppermute(block, 'x', [(0, 1), (1, 2), (2, 3)])]
    ppermute x9, waiting for transfers between devices: 11.7 us -> 15.1 us  [cycle(): lax.ppermute(cells, axis, [(i, (i + shift) % size) for i in range(size)])]
  transfers between devices with their start and end apart: 12 -> 12, of which waited for: 9 -> 9; matrix products, arithmetic and copies ran while one was open for 1% -> 1% of each run, Pallas kernels for 6% -> 9%
where the time goes in v2:
time: 95.2 us; the launch traced here: 93.8 us
  Pallas kernels  37.2 us (39%)
  starting transfers between devices  34.5 us (36%)
  waiting for transfers between devices  17.8 us (19%)
  other arithmetic  2.12 us (2%)
  local copies, waits for them, and re-layouts  1.24 us (1%)
    ppermute x9, starting transfers between devices, cycle(): lax.ppermute(cells, axis, [(i, (i + shift) % size) for i in range(size)])  22.1 us
    pallas_call x1, Pallas kernels, per_device(): pl.pallas_call(forward_kernel, out_shape=(f32(SEEN, 8, 8, NZ), f32(8, sta...  17.2 us
    ppermute x9, waiting for transfers between devices, cycle(): lax.ppermute(cells, axis, [(i, (i + shift) % size) for i in range(size)])  15.1 us
    pallas_call x1, Pallas kernels, per_device(): pl.pallas_call(adjoint_kernel, out_shape=f32(512, NZ), in_specs=[SMEM, VM...  10.9 us
    pallas_call x1, Pallas kernels, per_device(): pl.pallas_call(station_kernel, out_shape=(f32(ADJ * 64, NZ), f32(ADJ * 64...  8.41 us
    all_to_all x1, starting transfers between devices, per_device(): lax.all_to_all(pieces.reshape(16, 4, 8, NZ), ('zlo', 'core', 'half'), 0,...  6.51 us
    ppermute x1, starting transfers between devices, gathered(): before = lax.ppermute(block, 'x', [(0, 1), (1, 2), (2, 3)])  3.4 us
    ppermute x1, waiting for transfers between devices, gathered(): after = lax.ppermute(block, 'x', [(1, 0), (2, 1), (3, 2)])  2.75 us
  transfers between devices with their start and end apart: 12, of which 9 were waited for; matrix products, arithmetic and copies ran while one was open for 1% of the time, Pallas kernels for 9%

profile of v2, /device:TPU:2, one launch (start us, length us, event | category | flops | bytes accessed | tf_op | source)
XLA Modules:
  0.0 93.8 jit_solution(3664179604948309874)
XLA Ops:
  0.6 0.0 copy-start.3
  0.6 0.0 copy-start.1
  0.7 0.0 copy-start.2
  0.7 0.0 copy-start.7
  0.7 0.1 stack.27.meta
  0.8 0.0 copy-start
  0.8 0.9 copy-done
  1.7 0.7 prepare.1
  2.4 7.3 %collective-permute-start = (f32[4,4,8,128]{3,2,1,0:T(8,128)S(1)}, f32[4,4,8,128]{3,2,1,0:T(8,128)S(1)}, u32[]{:S(2)}, u32[]{:S(2)}) collective-permute-start(f32[4,4,8,128]{3,2,1,0:T(8,128)S(1)} %bitcast.32), channel_id=1, source_target_pairs={{0,1},{1,0},{2,3},{3,2},{4,5},{5,4},{6,7},{7,6},{8,9},{9,8},{10,11... | collective-permute-start | bytes 196616 | tf_op jit(solution)/shard_map/ppermute | solution.py:240
  9.7 2.4 %collective-permute-done = f32[4,4,8,128]{3,2,1,0:T(8,128)S(1)} collective-permute-done((f32[4,4,8,128]{3,2,1,0:T(8,128)S(1)}, f32[4,4,8,128]{3,2,1,0:T(8,128)S(1)}, u32[]{:S(2)}, u32[]{:S(2)}) %collective-permute-start) | collective-permute-done | bytes 65568 | tf_op jit(solution)/shard_map/ppermute | solution.py:240
  12.1 1.7 %collective-permute-start.1 = (f32[8,4,8,128]{3,2,1,0:T(8,128)S(1)}, f32[8,4,8,128]{3,2,1,0:T(8,128)S(1)}, u32[]{:S(2)}, u32[]{:S(2)}) collective-permute-start(f32[8,4,8,128]{3,2,1,0:T(8,128)S(1)} %maximum_select_fusion.1), channel_id=1, source_target_pairs={{0,2},{2,4},{4,6},{6,0},{1,3},{3,5},{5,7},{7,1},{8,10},{10,12},{12... | collective-permute-start | bytes 393224 | tf_op jit(solution)/shard_map/ppermute | solution.py:240
  13.8 1.7 %collective-permute-start.2 = (f32[8,4,8,128]{3,2,1,0:T(8,128)S(1)}, f32[8,4,8,128]{3,2,1,0:T(8,128)S(1)}, u32[]{:S(2)}, u32[]{:S(2)}) collective-permute-start(f32[8,4,8,128]{3,2,1,0:T(8,128)S(1)} %maximum_select_fusion.1), channel_id=1, source_target_pairs={{0,6},{2,0},{4,2},{6,4},{1,7},{3,1},{5,3},{7,5},{8,14},{10,8},{12,... | collective-permute-start | bytes 393224 | tf_op jit(solution)/shard_map/ppermute | solution.py:240
  15.4 2.0 %collective-permute-start.3 = (f32[8,4,8,128]{3,2,1,0:T(8,128)S(1)}, f32[8,4,8,128]{3,2,1,0:T(8,128)S(1)}, u32[]{:S(2)}, u32[]{:S(2)}) collective-permute-start(f32[8,4,8,128]{3,2,1,0:T(8,128)S(1)} %maximum_select_fusion.1), channel_id=1, source_target_pairs={{0,4},{2,6},{4,0},{6,2},{1,5},{3,7},{5,1},{7,3},{8,12},{10,14},{12... | collective-permute-start | bytes 393224 | tf_op jit(solution)/shard_map/ppermute | solution.py:240
  17.5 1.3 %collective-permute-done.1 = f32[8,4,8,128]{3,2,1,0:T(8,128)S(1)} collective-permute-done((f32[8,4,8,128]{3,2,1,0:T(8,128)S(1)}, f32[8,4,8,128]{3,2,1,0:T(8,128)S(1)}, u32[]{:S(2)}, u32[]{:S(2)}) %collective-permute-start.1) | collective-permute-done | bytes 131104 | tf_op jit(solution)/shard_map/ppermute | solution.py:240
  18.9 0.9 collective-permute-done.2
  19.8 2.5 %collective-permute-done.3 = f32[8,4,8,128]{3,2,1,0:T(8,128)S(1)} collective-permute-done((f32[8,4,8,128]{3,2,1,0:T(8,128)S(1)}, f32[8,4,8,128]{3,2,1,0:T(8,128)S(1)}, u32[]{:S(2)}, u32[]{:S(2)}) %collective-permute-start.3) | collective-permute-done | bytes 131104 | tf_op jit(solution)/shard_map/ppermute | solution.py:240
  22.3 3.4 %collective-permute-start.4 = (f32[32,4,8,128]{3,2,1,0:T(8,128)S(1)}, f32[32,4,8,128]{3,2,1,0:T(8,128)S(1)}, u32[]{:S(2)}, u32[]{:S(2)}) collective-permute-start(f32[32,4,8,128]{3,2,1,0:T(8,128)S(1)} %bitcast.42), channel_id=1, source_target_pairs={{0,8},{8,16},{16,24},{1,9},{9,17},{17,25},{2,10},{10,18},{18,26},{... | collective-permute-start | bytes 1572872 | tf_op jit(solution)/shard_map/ppermute | solution.py:253
  25.7 2.5 %collective-permute-start.5 = (f32[32,4,8,128]{3,2,1,0:T(8,128)S(1)}, f32[32,4,8,128]{3,2,1,0:T(8,128)S(1)}, u32[]{:S(2)}, u32[]{:S(2)}) collective-permute-start(f32[32,4,8,128]{3,2,1,0:T(8,128)S(1)} %bitcast.43), channel_id=1, source_target_pairs={{8,0},{16,8},{24,16},{9,1},{17,9},{25,17},{10,2},{18,10},{26,18},{... | collective-permute-start | bytes 1572872 | tf_op jit(solution)/shard_map/ppermute | solution.py:254
  28.2 0.0 copy-done.3
  28.2 0.0 copy-done.1
  28.2 0.0 copy-done.2
  28.2 0.0 copy-done.7
  28.2 8.4 %stations.1 = (f32[2560,128]{1,0:T(8,128)S(1)}, f32[2560,128]{1,0:T(8,128)S(1)}) custom-call(s32[6]{0:T(128)S(1)} %stack.27.meta, s32[1,2048]{1,0:T(1,128)S(1)} %bitcast.40, s32[1,2048]{1,0:T(1,128)S(1)} %bitcast.36, s32[1,2048]{1,0:T(1,128)S(1)} %bitcast.38, f32[2,2048]{1,0:T(2,128)S(1)} %copy-done.7), custom_call_target="tpu_custom_call" | custom-call | flops 5368709120 | bytes 2621440 | tf_op jit(solution)/shard_map/stations/pallas_call | solution.py:281
  36.6 0.0 collective-permute-done.4
  36.6 2.8 %collective-permute-done.5 = f32[32,4,8,128]{3,2,1,0:T(8,128)S(1)} collective-permute-done((f32[32,4,8,128]{3,2,1,0:T(8,128)S(1)}, f32[32,4,8,128]{3,2,1,0:T(8,128)S(1)}, u32[]{:S(2)}, u32[]{:S(2)}) %collective-permute-start.5) | collective-permute-done | bytes 524320 | tf_op jit(solution)/shard_map/ppermute | solution.py:254
  39.4 0.0 copy-start.4
  39.4 0.0 copy-start.5
  39.4 0.1 pad_maximum_fusion.mine
  39.5 0.3 collective-permute-start.6
  39.9 3.3 %collective-permute-done.6.other = f32[96,4,8,128]{3,2,1,0:T(8,128)S(1)} collective-permute-done((f32[96,4,8,128]{3,2,1,0:T(8,128)S(1)}, f32[96,4,8,128]{3,2,1,0:T(8,128)S(1)}, u32[]{:S(2)}, u32[]{:S(2)}) %collective-permute-start.6) | collective-permute-done | bytes 1572896 | tf_op jit(solution)/shard_map/ppermute | solution.py:240
  43.2 0.0 copy-done.4
  43.2 0.0 copy-done.5
  43.2 0.0 copy-done.6
  43.2 17.2 %forward.1 = (f32[48,8,8,128]{3,2,1,0:T(8,128)S(1)}, f32[8,512]{1,0:T(8,128)S(1)}) custom-call(s32[6]{0:T(128)S(1)} %stack.27.meta, s32[2]{0:T(128)S(1)} %copy-done.4, s32[2]{0:T(128)S(1)} %copy-done.5, s32[2]{0:T(128)S(1)} %copy-done.6, s32[512]{0:T(512)S(1)} %get-tuple-element.19.rows, s32[512]{0:T(512)S(1)} %get-tuple-element.18.lanes, ...), custom_call_target="tpu_custom_call" | custom-call | flops 73400320 | bytes 5242880 | tf_op jit(solution)/shard_map/forward/pallas_call | solution.py:314
  60.4 10.9 %adjoint.1 = f32[512,128]{1,0:T(8,128)} custom-call(s32[6]{0:T(128)S(1)} %stack.27.meta, f32[48,8,8,128]{3,2,1,0:T(8,128)S(1)} %get-tuple-element.14.times, f32[20,2,8,8,128]{4,3,2,1,0:T(8,128)S(1)} %bitcast.30, f32[20,2,8,8,128]{4,3,2,1,0:T(8,128)S(1)} %bitcast.31), custom_call_target="tpu_custom_call" | custom-call | flops 62914560 | bytes 5242880 | tf_op jit(solution)/shard_map/adjoint/pallas_call | solution.py:339
  71.3 6.5 %all-to-all-start = ((f32[16,4,8,128]{3,2,1,0:T(8,128)}), f32[16,4,8,128]{3,2,1,0:T(8,128)S(1)}, u32[]{:S(2)}, u32[]{:S(2)}) async-start(f32[16,4,8,128]{3,2,1,0:T(8,128)} %bitcast.25), calls=%async_computation | async-start | bytes 524288 | tf_op jit(solution)/shard_map/all_to_all | solution.py:362
  77.9 1.3 %collective-permute-start.7 = (f32[1,128]{1,0:T(1,128)S(1)}, f32[1,128]{1,0:T(1,128)S(1)}, u32[]{:S(2)}, u32[]{:S(2)}) collective-permute-start(f32[1,128]{1,0:T(1,128)S(1)} %get-tuple-element.20), channel_id=1, source_target_pairs={{0,8},{8,16},{16,24},{24,0},{1,9},{9,17},{17,25},{25,1},{2,10},{10... | collective-permute-start | bytes 1544 | tf_op jit(solution)/shard_map/ppermute | solution.py:240
  79.2 1.4 %collective-permute-start.8 = (f32[1,128]{1,0:T(1,128)S(1)}, f32[1,128]{1,0:T(1,128)S(1)}, u32[]{:S(2)}, u32[]{:S(2)}) collective-permute-start(f32[1,128]{1,0:T(1,128)S(1)} %get-tuple-element.22), channel_id=1, source_target_pairs={{0,16},{8,24},{16,0},{24,8},{1,17},{9,25},{17,1},{25,9},{2,18},{10... | collective-permute-start | bytes 1544 | tf_op jit(solution)/shard_map/ppermute | solution.py:240
  80.7 0.7 collective-permute-start.9
  81.4 0.2 collective-permute-done.7
  81.6 2.7 %collective-permute-done.8 = f32[1,128]{1,0:T(1,128)S(1)} collective-permute-done((f32[1,128]{1,0:T(1,128)S(1)}, f32[1,128]{1,0:T(1,128)S(1)}, u32[]{:S(2)}, u32[]{:S(2)}) %collective-permute-start.8) | collective-permute-done | bytes 544 | tf_op jit(solution)/shard_map/ppermute | solution.py:240
  84.3 0.0 collective-permute-done.9
  84.3 0.1 reshape.119
  84.4 5.8 %collective-permute-start.10 = (f32[1,64]{1,0:T(1,128)S(1)}, f32[1,64]{1,0:T(1,128)S(1)}, u32[]{:S(2)}, u32[]{:S(2)}) collective-permute-start(f32[1,64]{1,0:T(1,128)S(1)} %get-tuple-element.24), channel_id=1, source_target_pairs={{0,1},{1,0},{2,3},{3,2},{4,5},{5,4},{6,7},{7,6},{8,9},{9,8},{10,11... | collective-permute-start | bytes 776 | tf_op jit(solution)/shard_map/ppermute | solution.py:240
  90.2 1.7 %collective-permute-done.10 = f32[1,64]{1,0:T(1,128)S(1)} collective-permute-done((f32[1,64]{1,0:T(1,128)S(1)}, f32[1,64]{1,0:T(1,128)S(1)}, u32[]{:S(2)}, u32[]{:S(2)}) %collective-permute-start.10) | collective-permute-done | bytes 288 | tf_op jit(solution)/shard_map/ppermute | solution.py:240
  91.9 0.6 maximum_select_fusion.2
  92.5 0.0 all-to-all-done
  92.5 1.3 %dynamic-slice_multiply_fusion = f32[4,8,128]{2,1,0:T(8,128)} fusion(f32[4,8,128]{2,1,0:T(8,128)S(1)} %reduce_sum.9, f32[4,64,128]{2,1,0:T(8,128)} %param.8, s32[]{:T(128)S(6)} %select_n.139), kind=kLoop, calls=%fused_computation.7 | loop fusion | flops 4096 | bytes 49156 | tf_op jit(solution)/shard_map/mul | solution.py:364
  (15 shorter events, 0.2 us)
Async XLA Ops:
  0.6 27.5 %copy-start.3 = (s32[2048]{0:T(1024)S(1)}, s32[2048]{0:T(1024)}, u32[]{:S(2)}) copy-start(s32[2048]{0:T(1024)} %param.12) | copy-start | bytes 24580
  0.6 27.5 %copy-start.1 = (s32[2048]{0:T(1024)S(1)}, s32[2048]{0:T(1024)}, u32[]{:S(2)}) copy-start(s32[2048]{0:T(1024)} %param.13) | copy-start | bytes 24580
  0.7 27.5 %copy-start.2 = (s32[2048]{0:T(1024)S(1)}, s32[2048]{0:T(1024)}, u32[]{:S(2)}) copy-start(s32[2048]{0:T(1024)} %param.14) | copy-start | bytes 24580
  0.7 27.5 %copy-start.7 = (f32[2,2048]{1,0:T(2,128)S(1)}, f32[2,2048]{1,0:T(2,128)}, u32[]{:S(2)}) copy-start(f32[2,2048]{1,0:T(2,128)} %obs.1) | copy-start | bytes 49156
  0.8 0.9 copy-start
  2.4 9.7 %collective-permute-start = (f32[4,4,8,128]{3,2,1,0:T(8,128)S(1)}, f32[4,4,8,128]{3,2,1,0:T(8,128)S(1)}, u32[]{:S(2)}, u32[]{:S(2)}) collective-permute-start(f32[4,4,8,128]{3,2,1,0:T(8,128)S(1)} %bitcast.32), channel_id=1, source_target_pairs={{0,1},{1,0},{2,3},{3,2},{4,5},{5,4},{6,7},{7,6},{8,9},{9,8},{10,11... | collective-permute-start | bytes 196616 | tf_op jit(solution)/shard_map/ppermute | solution.py:240
  12.1 6.7 %collective-permute-start.1 = (f32[8,4,8,128]{3,2,1,0:T(8,128)S(1)}, f32[8,4,8,128]{3,2,1,0:T(8,128)S(1)}, u32[]{:S(2)}, u32[]{:S(2)}) collective-permute-start(f32[8,4,8,128]{3,2,1,0:T(8,128)S(1)} %maximum_select_fusion.1), channel_id=1, source_target_pairs={{0,2},{2,4},{4,6},{6,0},{1,3},{3,5},{5,7},{7,1},{8,10},{10,12},{12... | collective-permute-start | bytes 393224 | tf_op jit(solution)/shard_map/ppermute | solution.py:240
  13.8 6.0 %collective-permute-start.2 = (f32[8,4,8,128]{3,2,1,0:T(8,128)S(1)}, f32[8,4,8,128]{3,2,1,0:T(8,128)S(1)}, u32[]{:S(2)}, u32[]{:S(2)}) collective-permute-start(f32[8,4,8,128]{3,2,1,0:T(8,128)S(1)} %maximum_select_fusion.1), channel_id=1, source_target_pairs={{0,6},{2,0},{4,2},{6,4},{1,7},{3,1},{5,3},{7,5},{8,14},{10,8},{12,... | collective-permute-start | bytes 393224 | tf_op jit(solution)/shard_map/ppermute | solution.py:240
  15.4 6.8 %collective-permute-start.3 = (f32[8,4,8,128]{3,2,1,0:T(8,128)S(1)}, f32[8,4,8,128]{3,2,1,0:T(8,128)S(1)}, u32[]{:S(2)}, u32[]{:S(2)}) collective-permute-start(f32[8,4,8,128]{3,2,1,0:T(8,128)S(1)} %maximum_select_fusion.1), channel_id=1, source_target_pairs={{0,4},{2,6},{4,0},{6,2},{1,5},{3,7},{5,1},{7,3},{8,12},{10,14},{12... | collective-permute-start | bytes 393224 | tf_op jit(solution)/shard_map/ppermute | solution.py:240
  22.3 14.4 %collective-permute-start.4 = (f32[32,4,8,128]{3,2,1,0:T(8,128)S(1)}, f32[32,4,8,128]{3,2,1,0:T(8,128)S(1)}, u32[]{:S(2)}, u32[]{:S(2)}) collective-permute-start(f32[32,4,8,128]{3,2,1,0:T(8,128)S(1)} %bitcast.42), channel_id=1, source_target_pairs={{0,8},{8,16},{16,24},{1,9},{9,17},{17,25},{2,10},{10,18},{18,26},{... | collective-permute-start | bytes 1572872 | tf_op jit(solution)/shard_map/ppermute | solution.py:253
  25.7 13.7 %collective-permute-start.5 = (f32[32,4,8,128]{3,2,1,0:T(8,128)S(1)}, f32[32,4,8,128]{3,2,1,0:T(8,128)S(1)}, u32[]{:S(2)}, u32[]{:S(2)}) collective-permute-start(f32[32,4,8,128]{3,2,1,0:T(8,128)S(1)} %bitcast.43), channel_id=1, source_target_pairs={{8,0},{16,8},{24,16},{9,1},{17,9},{25,17},{10,2},{18,10},{26,18},{... | collective-permute-start | bytes 1572872 | tf_op jit(solution)/shard_map/ppermute | solution.py:254
  39.4 3.8 %copy-start.4 = (s32[2]{0:T(128)S(1)}, s32[2]{0:T(128)}, u32[]{:S(2)}) copy-start(s32[2]{0:T(128)} %src_x.1) | copy-start | bytes 28
  39.4 3.8 %copy-start.5 = (s32[2]{0:T(128)S(1)}, s32[2]{0:T(128)}, u32[]{:S(2)}) copy-start(s32[2]{0:T(128)} %src_y.1) | copy-start | bytes 28
  39.4 3.8 %copy-start.6 = (s32[2]{0:T(128)S(1)}, s32[2]{0:T(128)}, u32[]{:S(2)}) copy-start(s32[2]{0:T(128)} %src_z.1) | copy-start | bytes 28
  39.5 3.7 %collective-permute-start.6 = (f32[96,4,8,128]{3,2,1,0:T(8,128)S(1)}, f32[96,4,8,128]{3,2,1,0:T(8,128)S(1)}, u32[]{:S(2)}, u32[]{:S(2)}) collective-permute-start(f32[96,4,8,128]{3,2,1,0:T(8,128)S(1)} %pad_maximum_fusion.mine), channel_id=1, source_target_pairs={{0,32},{32,0},{1,33},{33,1},{2,34},{34,2},{3,35},{35,3},{4,36},{36... | collective-permute-start | bytes 4718600 | tf_op jit(solution)/shard_map/ppermute | solution.py:240
  71.3 21.1 %all-to-all-start = ((f32[16,4,8,128]{3,2,1,0:T(8,128)}), f32[16,4,8,128]{3,2,1,0:T(8,128)S(1)}, u32[]{:S(2)}, u32[]{:S(2)}) async-start(f32[16,4,8,128]{3,2,1,0:T(8,128)} %bitcast.25), calls=%async_computation | async-start | bytes 524288 | tf_op jit(solution)/shard_map/all_to_all | solution.py:362
  77.9 3.6 %collective-permute-start.7 = (f32[1,128]{1,0:T(1,128)S(1)}, f32[1,128]{1,0:T(1,128)S(1)}, u32[]{:S(2)}, u32[]{:S(2)}) collective-permute-start(f32[1,128]{1,0:T(1,128)S(1)} %get-tuple-element.20), channel_id=1, source_target_pairs={{0,8},{8,16},{16,24},{24,0},{1,9},{9,17},{17,25},{25,1},{2,10},{10... | collective-permute-start | bytes 1544 | tf_op jit(solution)/shard_map/ppermute | solution.py:240
  79.2 5.0 %collective-permute-start.8 = (f32[1,128]{1,0:T(1,128)S(1)}, f32[1,128]{1,0:T(1,128)S(1)}, u32[]{:S(2)}, u32[]{:S(2)}) collective-permute-start(f32[1,128]{1,0:T(1,128)S(1)} %get-tuple-element.22), channel_id=1, source_target_pairs={{0,16},{8,24},{16,0},{24,8},{1,17},{9,25},{17,1},{25,9},{2,18},{10... | collective-permute-start | bytes 1544 | tf_op jit(solution)/shard_map/ppermute | solution.py:240
  80.7 3.6 %collective-permute-start.9 = (f32[1,128]{1,0:T(1,128)S(1)}, f32[1,128]{1,0:T(1,128)S(1)}, u32[]{:S(2)}, u32[]{:S(2)}) collective-permute-start(f32[1,128]{1,0:T(1,128)S(1)} %get-tuple-element.21), channel_id=1, source_target_pairs={{0,24},{8,0},{16,8},{24,16},{1,25},{9,1},{17,9},{25,17},{2,26},{10... | collective-permute-start | bytes 1544 | tf_op jit(solution)/shard_map/ppermute | solution.py:240
  84.4 7.5 %collective-permute-start.10 = (f32[1,64]{1,0:T(1,128)S(1)}, f32[1,64]{1,0:T(1,128)S(1)}, u32[]{:S(2)}, u32[]{:S(2)}) collective-permute-start(f32[1,64]{1,0:T(1,128)S(1)} %get-tuple-element.24), channel_id=1, source_target_pairs={{0,1},{1,0},{2,3},{3,2},{4,5},{5,4},{6,7},{7,6},{8,9},{9,8},{10,11... | collective-permute-start | bytes 776 | tf_op jit(solution)/shard_map/ppermute | solution.py:240

commit v3 on v2

--- a/solution.py
+++ b/solution.py
@@ -54,8 +54,17 @@
     return first, second
 
 
-def beside(here, edge):
-    lane = iota((8, NZ), 1) % HALF
+def lane_of(values, index):
+    tiles = values.reshape(-1, 8, NZ)
+    tiles = [
+        jnp.take_along_axis(tiles[n], index, axis=1, mode="promise_in_bounds") for n in range(tiles.shape[0])
+    ]
+    return jnp.stack(tiles).reshape(values.shape)
+
+
+def beside(here, edge, repeat=False):
+    whole = iota((8, NZ), 1)
+    lane = whole % HALF
     sub = iota((8, NZ), 0)
 
     def bounded(mask, values):
@@ -63,8 +72,12 @@
 
     even, odd = here[:, 0:1], here[:, 1:2]
     same = jnp.concatenate([odd, even], axis=1)
-    left = bounded(lane == 0, pltpu.roll(odd, 1, 4))
-    right = bounded(lane == HALF - 1, pltpu.roll(even, NZ - 1, 4))
+    if repeat:
+        left = lane_of(odd, jnp.where(lane == 0, whole, whole - 1))
+        right = lane_of(even, jnp.where(lane == HALF - 1, whole, whole + 1))
+    else:
+        left = bounded(lane == 0, pltpu.roll(odd, 1, 4))
+        right = bounded(lane == HALF - 1, pltpu.roll(even, NZ - 1, 4))
     rolled = jnp.concatenate([left, right], axis=1)
     down = bounded(sub == 0, pltpu.roll(here[:, :, 7:8], 1, 3))
     up = bounded(sub == 7, pltpu.roll(here[:, :, 0:1], 7, 3))
@@ -154,13 +167,13 @@
         near = before[pl.ds(layer - 1, step + 2)]
         here = near[1 : step + 1]
         best = jnp.minimum(near[:step], near[2:])
-        same, rolled, below, above = beside(here, BIG)
+        same, rolled, below, above = beside(here, BIG, True)
         best = jnp.minimum(best, jnp.minimum(same, rolled))
         best = jnp.minimum(best, jnp.minimum(below, above))
         after[pl.ds(layer, step)] = jnp.minimum(here, best + slow[pl.ds(layer, step)])
 
     even[WIDE // 2] = pltpu.roll(even[WIDE // 2 - 1], HALF, 3)
-    last = sweeps(1, ITERS, WIDE // 2, 16, even, odd, block)
+    last = sweeps(1, ITERS, WIDE // 2, 20, even, odd, block)
 
     def finish(j, carry):
         layer = ITERS + j
@@ -201,20 +214,21 @@
     lax.fori_loop(0, top, load, 0, unroll=4)
     odd[top] = pltpu.roll(odd[top - 1], HALF, 3)
 
-    def weights(layer, carry):
-        here = odd[pl.ds(layer, 1)]
-        others = (odd[pl.ds(layer + 1, 1)], odd[pl.ds(layer - 1, 1)]) + beside(here, -BIG)
+    def weights(layer, size):
+        where = pl.ds(layer, size)
+        here = odd[where]
+        others = (odd[pl.ds(layer + 1, size)], odd[pl.ds(layer - 1, size)]) + beside(here, -BIG)
         terms = [jnp.maximum(n - here, 0.0) * (1.0 / SPACING) for n in others]
         denom = 1.0 + terms[0] + terms[1] + terms[2] + terms[3] + terms[4] + terms[5]
         scale = 1.0 / denom
         for n, term in enumerate(terms):
-            coef[n, pl.ds(layer, 1)] = term * scale
-        first = (count[pl.ds(layer, 1)] * here - seen[pl.ds(layer, 1)]) * scale
-        coef[6, pl.ds(layer, 1)] = first
-        even[pl.ds(layer, 1)] = first
-        return carry
-
-    lax.fori_loop(1, top, weights, 0)
+            coef[n, where] = term * scale
+        first = (count[where] * here - seen[where]) * scale
+        coef[6, where] = first
+        even[where] = first
+
+    lax.fori_loop(0, (top - 1) // 4, lambda j, carry: (weights(1 + 4 * j, 4), carry)[1], 0)
+    weights(top - 3, 3)
     even[top] = pltpu.roll(even[top - 1], HALF, 3)
 
     def block(before, after, layer, step):
@@ -330,11 +344,9 @@
         name="forward",
     )(meta, source_x, source_y, source_z, rows, lanes, mine, other)
 
-    arrive = arrive[0].reshape(4, stations // 16)
-    got = lax.dynamic_index_in_dim(arrive, x, 0)
-    for shift in (1, 2, 3):
-        piece = lax.dynamic_index_in_dim(arrive, (x + shift) % 4, 0)
-        got = got + cycle(piece, "x", 4, shift)
+    arrive = arrive[0].reshape(4, 2, stations // 32)
+    own = lax.dynamic_index_in_dim(arrive, half, 1, keepdims=False)
+    partner = cycle(lax.dynamic_index_in_dim(arrive, 1 - half, 1, keepdims=False), "half", 2, 1)
 
     pieces = pl.pallas_call(
         adjoint_kernel,
@@ -358,15 +370,17 @@
         count.reshape(ADJ // 2, 2, 8, 8, NZ),
         seen.reshape(ADJ // 2, 2, 8, 8, NZ),
     )
+    pieces, own, partner = lax.optimization_barrier((pieces, own, partner))
     summed = jnp.sum(
         lax.all_to_all(pieces.reshape(16, 4, 8, NZ), ("zlo", "core", "half"), 0, 0, tiled=True), axis=0
     )
     kernel = lax.dynamic_slice(slowness, (0, group * 8, 0), (4, 8, NZ)) * summed
 
-    got = got.reshape(2, stations // 32)
-    own = lax.dynamic_index_in_dim(got, half, 0)
-    partner = cycle(lax.dynamic_index_in_dim(got, 1 - half, 0), "half", 2, 1)
-    arrivals = jnp.where(half == 0, jnp.concatenate([own, partner]), jnp.concatenate([partner, own]))
+    known = jnp.where(half == 0, jnp.stack([own, partner], 1), jnp.stack([partner, own], 1))
+    arrivals = lax.dynamic_index_in_dim(known, x, 0, keepdims=False)
+    for shift in (1, 2, 3):
+        piece = lax.dynamic_index_in_dim(known, (x + shift) % 4, 0, keepdims=False)
+        arrivals = arrivals + cycle(piece, "x", 4, shift)
     return kernel, arrivals
 
 

time: 95.2 us -> 100 us (1.050)
  local copies, waits for them, and re-layouts: 1.24 us -> 6.49 us
  waiting for transfers between devices: 17.8 us -> 21.2 us
  starting transfers between devices: 34.5 us -> 32 us
    unnamed x16 -> x28, local copies, waits for them, and re-layouts: 0.93 us -> 6.16 us
    all_to_all x1, waiting for transfers between devices: 0.01 us -> 4.44 us  [per_device(): lax.all_to_all(pieces.reshape(16, 4, 8, NZ), ('zlo', 'core', 'half'), 0,...]
    all_to_all x1, starting transfers between devices: 6.51 us -> 4.81 us  [per_device(): lax.all_to_all(pieces.reshape(16, 4, 8, NZ), ('zlo', 'core', 'half'), 0,...]
    pallas_call x1, Pallas kernels: 10.9 us -> 9.84 us  [per_device(): pl.pallas_call(adjoint_kernel, out_shape=f32(512, NZ), in_specs=[SMEM, VM...]
    ppermute x9, waiting for transfers between devices: 15.1 us -> 14.1 us  [cycle(): lax.ppermute(cells, axis, [(i, (i + shift) % size) for i in range(size)])]
  transfers between devices with their start and end apart: 12 -> 12, of which waited for: 9 -> 9; matrix products, arithmetic and copies ran while one was open for 1% -> 1% of each run, Pallas kernels for 9% -> 18%
where the time goes in v3:
time: 100 us; the launch traced here: 99.4 us
  Pallas kernels  36.6 us (37%)
  starting transfers between devices  32 us (32%)
  waiting for transfers between devices  21.2 us (21%)
  local copies, waits for them, and re-layouts  6.49 us (6%)
  other arithmetic  2.11 us (2%)
    ppermute x9, starting transfers between devices, cycle(): lax.ppermute(cells, axis, [(i, (i + shift) % size) for i in range(size)])  21.4 us
    pallas_call x1, Pallas kernels, per_device(): pl.pallas_call(forward_kernel, out_shape=(f32(SEEN, 8, 8, NZ), f32(8, sta...  17.7 us
    ppermute x9, waiting for transfers between devices, cycle(): lax.ppermute(cells, axis, [(i, (i + shift) % size) for i in range(size)])  14.1 us
    pallas_call x1, Pallas kernels, per_device(): pl.pallas_call(adjoint_kernel, out_shape=f32(512, NZ), in_specs=[SMEM, VM...  9.84 us
    pallas_call x1, Pallas kernels, per_device(): pl.pallas_call(station_kernel, out_shape=(f32(ADJ * 64, NZ), f32(ADJ * 64...  8.41 us
    unnamed x28, local copies, waits for them, and re-layouts  6.16 us
    all_to_all x1, starting transfers between devices, per_device(): lax.all_to_all(pieces.reshape(16, 4, 8, NZ), ('zlo', 'core', 'half'), 0,...  4.81 us
    all_to_all x1, waiting for transfers between devices, per_device(): lax.all_to_all(pieces.reshape(16, 4, 8, NZ), ('zlo', 'core', 'half'), 0,...  4.44 us
  transfers between devices with their start and end apart: 12, of which 9 were waited for; matrix products, arithmetic and copies ran while one was open for 1% of the time, Pallas kernels for 18%

profile of v3, /device:TPU:2, one launch (start us, length us, event | category | flops | bytes accessed | tf_op | source)
XLA Modules:
  0.0 99.4 jit_solution(6407148128444568267)
XLA Ops:
  0.6 0.0 copy-start.9
  0.6 0.0 copy-start.7
  0.7 0.0 copy-start.8
  0.7 0.0 copy-start.13
  0.7 0.1 stack.41.meta
  0.8 0.9 copy-done.6
  1.7 0.7 prepare.1
  2.4 7.3 %collective-permute-start = (f32[4,4,8,128]{3,2,1,0:T(8,128)S(1)}, f32[4,4,8,128]{3,2,1,0:T(8,128)S(1)}, u32[]{:S(2)}, u32[]{:S(2)}) collective-permute-start(f32[4,4,8,128]{3,2,1,0:T(8,128)S(1)} %bitcast.49), channel_id=1, source_target_pairs={{0,1},{1,0},{2,3},{3,2},{4,5},{5,4},{6,7},{7,6},{8,9},{9,8},{10,11... | collective-permute-start | bytes 196616 | tf_op jit(solution)/shard_map/ppermute | solution.py:254
  9.7 2.4 %collective-permute-done = f32[4,4,8,128]{3,2,1,0:T(8,128)S(1)} collective-permute-done((f32[4,4,8,128]{3,2,1,0:T(8,128)S(1)}, f32[4,4,8,128]{3,2,1,0:T(8,128)S(1)}, u32[]{:S(2)}, u32[]{:S(2)}) %collective-permute-start) | collective-permute-done | bytes 65568 | tf_op jit(solution)/shard_map/ppermute | solution.py:254
  12.1 1.7 %collective-permute-start.1 = (f32[8,4,8,128]{3,2,1,0:T(8,128)S(1)}, f32[8,4,8,128]{3,2,1,0:T(8,128)S(1)}, u32[]{:S(2)}, u32[]{:S(2)}) collective-permute-start(f32[8,4,8,128]{3,2,1,0:T(8,128)S(1)} %maximum_select_fusion.1), channel_id=1, source_target_pairs={{0,2},{2,4},{4,6},{6,0},{1,3},{3,5},{5,7},{7,1},{8,10},{10,12},{12... | collective-permute-start | bytes 393224 | tf_op jit(solution)/shard_map/ppermute | solution.py:254
  13.8 1.7 %collective-permute-start.2 = (f32[8,4,8,128]{3,2,1,0:T(8,128)S(1)}, f32[8,4,8,128]{3,2,1,0:T(8,128)S(1)}, u32[]{:S(2)}, u32[]{:S(2)}) collective-permute-start(f32[8,4,8,128]{3,2,1,0:T(8,128)S(1)} %maximum_select_fusion.1), channel_id=1, source_target_pairs={{0,6},{2,0},{4,2},{6,4},{1,7},{3,1},{5,3},{7,5},{8,14},{10,8},{12,... | collective-permute-start | bytes 393224 | tf_op jit(solution)/shard_map/ppermute | solution.py:254
  15.4 2.0 %collective-permute-start.3 = (f32[8,4,8,128]{3,2,1,0:T(8,128)S(1)}, f32[8,4,8,128]{3,2,1,0:T(8,128)S(1)}, u32[]{:S(2)}, u32[]{:S(2)}) collective-permute-start(f32[8,4,8,128]{3,2,1,0:T(8,128)S(1)} %maximum_select_fusion.1), channel_id=1, source_target_pairs={{0,4},{2,6},{4,0},{6,2},{1,5},{3,7},{5,1},{7,3},{8,12},{10,14},{12... | collective-permute-start | bytes 393224 | tf_op jit(solution)/shard_map/ppermute | solution.py:254
  17.5 1.3 %collective-permute-done.1 = f32[8,4,8,128]{3,2,1,0:T(8,128)S(1)} collective-permute-done((f32[8,4,8,128]{3,2,1,0:T(8,128)S(1)}, f32[8,4,8,128]{3,2,1,0:T(8,128)S(1)}, u32[]{:S(2)}, u32[]{:S(2)}) %collective-permute-start.1) | collective-permute-done | bytes 131104 | tf_op jit(solution)/shard_map/ppermute | solution.py:254
  18.9 0.9 collective-permute-done.2
  19.8 2.5 %collective-permute-done.3 = f32[8,4,8,128]{3,2,1,0:T(8,128)S(1)} collective-permute-done((f32[8,4,8,128]{3,2,1,0:T(8,128)S(1)}, f32[8,4,8,128]{3,2,1,0:T(8,128)S(1)}, u32[]{:S(2)}, u32[]{:S(2)}) %collective-permute-start.3) | collective-permute-done | bytes 131104 | tf_op jit(solution)/shard_map/ppermute | solution.py:254
  22.3 3.4 %collective-permute-start.4 = (f32[32,4,8,128]{3,2,1,0:T(8,128)S(1)}, f32[32,4,8,128]{3,2,1,0:T(8,128)S(1)}, u32[]{:S(2)}, u32[]{:S(2)}) collective-permute-start(f32[32,4,8,128]{3,2,1,0:T(8,128)S(1)} %bitcast.59), channel_id=1, source_target_pairs={{0,8},{8,16},{16,24},{1,9},{9,17},{17,25},{2,10},{10,18},{18,26},{... | collective-permute-start | bytes 1572872 | tf_op jit(solution)/shard_map/ppermute | solution.py:267
  25.7 2.5 %collective-permute-start.5 = (f32[32,4,8,128]{3,2,1,0:T(8,128)S(1)}, f32[32,4,8,128]{3,2,1,0:T(8,128)S(1)}, u32[]{:S(2)}, u32[]{:S(2)}) collective-permute-start(f32[32,4,8,128]{3,2,1,0:T(8,128)S(1)} %bitcast.60), channel_id=1, source_target_pairs={{8,0},{16,8},{24,16},{9,1},{17,9},{25,17},{10,2},{18,10},{26,18},{... | collective-permute-start | bytes 1572872 | tf_op jit(solution)/shard_map/ppermute | solution.py:268
  28.2 0.0 copy-done.9
  28.2 0.0 copy-done.7
  28.2 0.0 copy-done.8
  28.2 0.0 copy-done.13
  28.2 8.4 %stations.1 = (f32[2560,128]{1,0:T(8,128)S(1)}, f32[2560,128]{1,0:T(8,128)S(1)}) custom-call(s32[6]{0:T(128)S(1)} %stack.41.meta, s32[1,2048]{1,0:T(1,128)S(1)} %bitcast.57, s32[1,2048]{1,0:T(1,128)S(1)} %bitcast.53, s32[1,2048]{1,0:T(1,128)S(1)} %bitcast.55, f32[2,2048]{1,0:T(2,128)S(1)} %copy-done.13), custom_call_target="tpu_custom_call" | custom-call | flops 5368709120 | bytes 2621440 | tf_op jit(solution)/shard_map/stations/pallas_call | solution.py:295
  36.7 0.0 collective-permute-done.4
  36.7 2.7 %collective-permute-done.5 = f32[32,4,8,128]{3,2,1,0:T(8,128)S(1)} collective-permute-done((f32[32,4,8,128]{3,2,1,0:T(8,128)S(1)}, f32[32,4,8,128]{3,2,1,0:T(8,128)S(1)}, u32[]{:S(2)}, u32[]{:S(2)}) %collective-permute-start.5) | collective-permute-done | bytes 524320 | tf_op jit(solution)/shard_map/ppermute | solution.py:268
  39.4 0.1 pad_maximum_fusion.mine
  39.6 0.1 collective-permute-start.6
  39.7 3.3 %collective-permute-done.6.other = f32[96,4,8,128]{3,2,1,0:T(8,128)S(1)} collective-permute-done((f32[96,4,8,128]{3,2,1,0:T(8,128)S(1)}, f32[96,4,8,128]{3,2,1,0:T(8,128)S(1)}, u32[]{:S(2)}, u32[]{:S(2)}) %collective-permute-start.6) | collective-permute-done | bytes 1572896 | tf_op jit(solution)/shard_map/ppermute | solution.py:254
  43.1 1.2 %copy-done = f32[96,4,8,128]{3,2,1,0:T(8,128)} copy-done((f32[96,4,8,128]{3,2,1,0:T(8,128)}, f32[96,4,8,128]{3,2,1,0:T(8,128)S(1)}, u32[]{:S(2)}) %copy-start) | copy-done | bytes 1572888
  44.2 0.0 copy-done.10
  44.2 0.0 copy-done.12
  44.2 1.4 %copy-done.1 = f32[96,4,8,128]{3,2,1,0:T(8,128)S(1)} copy-done((f32[96,4,8,128]{3,2,1,0:T(8,128)S(1)}, f32[96,4,8,128]{3,2,1,0:T(8,128)}, u32[]{:S(2)}) %copy-start.1) | copy-done | bytes 1572888
  45.6 17.7 %forward.1 = (f32[48,8,8,128]{3,2,1,0:T(8,128)S(1)}, f32[8,512]{1,0:T(8,128)S(1)}) custom-call(s32[6]{0:T(128)S(1)} %stack.41.meta, s32[2]{0:T(128)S(1)} %copy-done.10, s32[2]{0:T(128)S(1)} %copy-done.11, s32[2]{0:T(128)S(1)} %copy-done.12, s32[512]{0:T(512)S(1)} %get-tuple-element.30.rows, s32[512]{0:T(512)S(1)} %get-tuple-element.29.lanes, ...), custom_call_target="tpu_custom_call" | custom-call | flops 73400320 | bytes 5242880 | tf_op jit(solution)/shard_map/forward/pallas_call | solution.py:328
  63.3 0.1 reshape_squeeze.3
  63.4 5.1 %collective-permute-start.7 = (f32[4,64]{1,0:T(4,128)S(1)}, f32[4,64]{1,0:T(4,128)S(1)}, u32[]{:S(2)}, u32[]{:S(2)}) collective-permute-start(f32[4,64]{1,0:T(4,128)S(1)} %bitcast.67), channel_id=1, source_target_pairs={{0,1},{1,0},{2,3},{3,2},{4,5},{5,4},{6,7},{7,6},{8,9},{9,8},{10,11... | collective-permute-start | bytes 3080 | tf_op jit(solution)/shard_map/ppermute | solution.py:254
  68.5 1.3 %copy-done.3 = f32[2560,128]{1,0:T(8,128)S(1)} copy-done((f32[2560,128]{1,0:T(8,128)S(1)}, f32[2560,128]{1,0:T(8,128)}, u32[]{:S(2)}) %copy-start.3) | copy-done | bytes 1310744
  69.8 1.3 %copy-done.5 = f32[2560,128]{1,0:T(8,128)S(1)} copy-done((f32[2560,128]{1,0:T(8,128)S(1)}, f32[2560,128]{1,0:T(8,128)}, u32[]{:S(2)}) %copy-start.5) | copy-done | bytes 1310744
  71.1 9.8 %adjoint.1 = f32[512,128]{1,0:T(8,128)} custom-call(s32[6]{0:T(128)S(1)} %stack.41.meta, f32[48,8,8,128]{3,2,1,0:T(8,128)S(1)} %get-tuple-element.17.times, f32[20,2,8,8,128]{4,3,2,1,0:T(8,128)S(1)} %bitcast.47, f32[20,2,8,8,128]{4,3,2,1,0:T(8,128)S(1)} %bitcast.48), custom_call_target="tpu_custom_call" | custom-call | flops 62914560 | bytes 5242880 | tf_op jit(solution)/shard_map/adjoint/pallas_call | solution.py:351
  81.0 0.0 collective-permute-done.7
  81.0 4.8 %all-to-all-start = ((f32[16,4,8,128]{3,2,1,0:T(8,128)}), f32[16,4,8,128]{3,2,1,0:T(8,128)S(1)}, u32[]{:S(2)}, u32[]{:S(2)}) async-start(f32[16,4,8,128]{3,2,1,0:T(8,128)} %bitcast.27), calls=%async_computation | async-start | bytes 524288 | tf_op jit(solution)/shard_map/all_to_all | solution.py:375
  85.9 0.7 collective-permute-start.10
  86.5 1.5 %collective-permute-start.8 = (f32[2,64]{1,0:T(2,128)S(1)}, f32[2,64]{1,0:T(2,128)S(1)}, u32[]{:S(2)}, u32[]{:S(2)}) collective-permute-start(f32[2,64]{1,0:T(2,128)S(1)} %get-tuple-element.24), channel_id=1, source_target_pairs={{0,8},{8,16},{16,24},{24,0},{1,9},{9,17},{17,25},{25,1},{2,10},{10... | collective-permute-start | bytes 1544 | tf_op jit(solution)/shard_map/ppermute | solution.py:254
  88.0 1.5 %collective-permute-start.9 = (f32[2,64]{1,0:T(2,128)S(1)}, f32[2,64]{1,0:T(2,128)S(1)}, u32[]{:S(2)}, u32[]{:S(2)}) collective-permute-start(f32[2,64]{1,0:T(2,128)S(1)} %get-tuple-element.26), channel_id=1, source_target_pairs={{0,16},{8,24},{16,0},{24,8},{1,17},{9,25},{17,1},{25,9},{2,18},{10... | collective-permute-start | bytes 1544 | tf_op jit(solution)/shard_map/ppermute | solution.py:254
  89.5 0.0 collective-permute-done.10
  89.5 0.6 collective-permute-done.8
  90.1 3.0 %collective-permute-done.9 = f32[2,64]{1,0:T(2,128)S(1)} collective-permute-done((f32[2,64]{1,0:T(2,128)S(1)}, f32[2,64]{1,0:T(2,128)S(1)}, u32[]{:S(2)}, u32[]{:S(2)}) %collective-permute-start.9) | collective-permute-done | bytes 544 | tf_op jit(solution)/shard_map/ppermute | solution.py:254
  93.1 0.6 fusion.19
  93.6 4.4 %all-to-all-done = f32[16,4,8,128]{3,2,1,0:T(8,128)S(1)} async-done(((f32[16,4,8,128]{3,2,1,0:T(8,128)}), f32[16,4,8,128]{3,2,1,0:T(8,128)S(1)}, u32[]{:S(2)}, u32[]{:S(2)}) %all-to-all-start) | async-done | bytes 262176 | tf_op jit(solution)/shard_map/all_to_all | solution.py:375
  98.1 1.3 %dynamic-slice_multiply_fusion = f32[4,8,128]{2,1,0:T(8,128)} fusion(f32[4,8,128]{2,1,0:T(8,128)S(1)} %reduce_sum.9, f32[4,64,128]{2,1,0:T(8,128)} %param.8, s32[]{:T(128)S(6)} %select_n.139), kind=kLoop, calls=%fused_computation.7 | loop fusion | flops 4096 | bytes 49156 | tf_op jit(solution)/shard_map/mul | solution.py:377
  (27 shorter events, 0.3 us)
Async XLA Ops:
  0.6 27.5 %copy-start.9 = (s32[2048]{0:T(1024)S(1)}, s32[2048]{0:T(1024)}, u32[]{:S(2)}) copy-start(s32[2048]{0:T(1024)} %param.12) | copy-start | bytes 24580
  0.6 27.5 %copy-start.7 = (s32[2048]{0:T(1024)S(1)}, s32[2048]{0:T(1024)}, u32[]{:S(2)}) copy-start(s32[2048]{0:T(1024)} %param.13) | copy-start | bytes 24580
  0.7 27.5 %copy-start.8 = (s32[2048]{0:T(1024)S(1)}, s32[2048]{0:T(1024)}, u32[]{:S(2)}) copy-start(s32[2048]{0:T(1024)} %param.14) | copy-start | bytes 24580
  0.7 27.5 %copy-start.13 = (f32[2,2048]{1,0:T(2,128)S(1)}, f32[2,2048]{1,0:T(2,128)}, u32[]{:S(2)}) copy-start(f32[2,2048]{1,0:T(2,128)} %obs.1) | copy-start | bytes 49156
  0.8 0.9 copy-start.6
  2.4 9.7 %collective-permute-start = (f32[4,4,8,128]{3,2,1,0:T(8,128)S(1)}, f32[4,4,8,128]{3,2,1,0:T(8,128)S(1)}, u32[]{:S(2)}, u32[]{:S(2)}) collective-permute-start(f32[4,4,8,128]{3,2,1,0:T(8,128)S(1)} %bitcast.49), channel_id=1, source_target_pairs={{0,1},{1,0},{2,3},{3,2},{4,5},{5,4},{6,7},{7,6},{8,9},{9,8},{10,11... | collective-permute-start | bytes 196616 | tf_op jit(solution)/shard_map/ppermute | solution.py:254
  12.1 6.7 %collective-permute-start.1 = (f32[8,4,8,128]{3,2,1,0:T(8,128)S(1)}, f32[8,4,8,128]{3,2,1,0:T(8,128)S(1)}, u32[]{:S(2)}, u32[]{:S(2)}) collective-permute-start(f32[8,4,8,128]{3,2,1,0:T(8,128)S(1)} %maximum_select_fusion.1), channel_id=1, source_target_pairs={{0,2},{2,4},{4,6},{6,0},{1,3},{3,5},{5,7},{7,1},{8,10},{10,12},{12... | collective-permute-start | bytes 393224 | tf_op jit(solution)/shard_map/ppermute | solution.py:254
  13.8 6.0 %collective-permute-start.2 = (f32[8,4,8,128]{3,2,1,0:T(8,128)S(1)}, f32[8,4,8,128]{3,2,1,0:T(8,128)S(1)}, u32[]{:S(2)}, u32[]{:S(2)}) collective-permute-start(f32[8,4,8,128]{3,2,1,0:T(8,128)S(1)} %maximum_select_fusion.1), channel_id=1, source_target_pairs={{0,6},{2,0},{4,2},{6,4},{1,7},{3,1},{5,3},{7,5},{8,14},{10,8},{12,... | collective-permute-start | bytes 393224 | tf_op jit(solution)/shard_map/ppermute | solution.py:254
  15.4 6.8 %collective-permute-start.3 = (f32[8,4,8,128]{3,2,1,0:T(8,128)S(1)}, f32[8,4,8,128]{3,2,1,0:T(8,128)S(1)}, u32[]{:S(2)}, u32[]{:S(2)}) collective-permute-start(f32[8,4,8,128]{3,2,1,0:T(8,128)S(1)} %maximum_select_fusion.1), channel_id=1, source_target_pairs={{0,4},{2,6},{4,0},{6,2},{1,5},{3,7},{5,1},{7,3},{8,12},{10,14},{12... | collective-permute-start | bytes 393224 | tf_op jit(solution)/shard_map/ppermute | solution.py:254
  22.3 14.4 %collective-permute-start.4 = (f32[32,4,8,128]{3,2,1,0:T(8,128)S(1)}, f32[32,4,8,128]{3,2,1,0:T(8,128)S(1)}, u32[]{:S(2)}, u32[]{:S(2)}) collective-permute-start(f32[32,4,8,128]{3,2,1,0:T(8,128)S(1)} %bitcast.59), channel_id=1, source_target_pairs={{0,8},{8,16},{16,24},{1,9},{9,17},{17,25},{2,10},{10,18},{18,26},{... | collective-permute-start | bytes 1572872 | tf_op jit(solution)/shard_map/ppermute | solution.py:267
  25.7 13.7 %collective-permute-start.5 = (f32[32,4,8,128]{3,2,1,0:T(8,128)S(1)}, f32[32,4,8,128]{3,2,1,0:T(8,128)S(1)}, u32[]{:S(2)}, u32[]{:S(2)}) collective-permute-start(f32[32,4,8,128]{3,2,1,0:T(8,128)S(1)} %bitcast.60), channel_id=1, source_target_pairs={{8,0},{16,8},{24,16},{9,1},{17,9},{25,17},{10,2},{18,10},{26,18},{... | collective-permute-start | bytes 1572872 | tf_op jit(solution)/shard_map/ppermute | solution.py:268
  36.6 2.9 %copy-start.2 = (f32[2560,128]{1,0:T(8,128)}, f32[2560,128]{1,0:T(8,128)S(1)}, u32[]{:S(2)}) copy-start(f32[2560,128]{1,0:T(8,128)S(1)} %get-tuple-element.18) | copy-start | bytes 3932164
  36.6 2.9 %copy-start.4 = (f32[2560,128]{1,0:T(8,128)}, f32[2560,128]{1,0:T(8,128)S(1)}, u32[]{:S(2)}) copy-start(f32[2560,128]{1,0:T(8,128)S(1)} %get-tuple-element.19) | copy-start | bytes 3932164
  39.4 4.8 %copy-start.10 = (s32[2]{0:T(128)S(1)}, s32[2]{0:T(128)}, u32[]{:S(2)}) copy-start(s32[2]{0:T(128)} %src_x.1) | copy-start | bytes 28
  39.4 4.8 %copy-start.11 = (s32[2]{0:T(128)S(1)}, s32[2]{0:T(128)}, u32[]{:S(2)}) copy-start(s32[2]{0:T(128)} %src_y.1) | copy-start | bytes 28
  39.4 4.8 %copy-start.12 = (s32[2]{0:T(128)S(1)}, s32[2]{0:T(128)}, u32[]{:S(2)}) copy-start(s32[2]{0:T(128)} %src_z.1) | copy-start | bytes 28
  39.6 3.5 %collective-permute-start.6 = (f32[96,4,8,128]{3,2,1,0:T(8,128)S(1)}, f32[96,4,8,128]{3,2,1,0:T(8,128)S(1)}, u32[]{:S(2)}, u32[]{:S(2)}) collective-permute-start(f32[96,4,8,128]{3,2,1,0:T(8,128)S(1)} %pad_maximum_fusion.mine), channel_id=1, source_target_pairs={{0,32},{32,0},{1,33},{33,1},{2,34},{34,2},{3,35},{35,3},{4,36},{36... | collective-permute-start | bytes 4718600 | tf_op jit(solution)/shard_map/ppermute | solution.py:254
  43.1 1.2 %copy-start = (f32[96,4,8,128]{3,2,1,0:T(8,128)}, f32[96,4,8,128]{3,2,1,0:T(8,128)S(1)}, u32[]{:S(2)}) copy-start(f32[96,4,8,128]{3,2,1,0:T(8,128)S(1)} %collective-permute-done.6.other) | copy-start | bytes 4718596
  44.2 1.4 %copy-start.1 = (f32[96,4,8,128]{3,2,1,0:T(8,128)S(1)}, f32[96,4,8,128]{3,2,1,0:T(8,128)}, u32[]{:S(2)}) copy-start(f32[96,4,8,128]{3,2,1,0:T(8,128)} %copy-done) | copy-start | bytes 4718596
  63.4 17.5 %collective-permute-start.7 = (f32[4,64]{1,0:T(4,128)S(1)}, f32[4,64]{1,0:T(4,128)S(1)}, u32[]{:S(2)}, u32[]{:S(2)}) collective-permute-start(f32[4,64]{1,0:T(4,128)S(1)} %bitcast.67), channel_id=1, source_target_pairs={{0,1},{1,0},{2,3},{3,2},{4,5},{5,4},{6,7},{7,6},{8,9},{9,8},{10,11... | collective-permute-start | bytes 3080 | tf_op jit(solution)/shard_map/ppermute | solution.py:254
  68.5 1.3 %copy-start.3 = (f32[2560,128]{1,0:T(8,128)S(1)}, f32[2560,128]{1,0:T(8,128)}, u32[]{:S(2)}) copy-start(f32[2560,128]{1,0:T(8,128)} %copy-done.2) | copy-start | bytes 3932164
  69.8 1.3 %copy-start.5 = (f32[2560,128]{1,0:T(8,128)S(1)}, f32[2560,128]{1,0:T(8,128)}, u32[]{:S(2)}) copy-start(f32[2560,128]{1,0:T(8,128)} %copy-done.4) | copy-start | bytes 3932164
  81.0 17.1 %all-to-all-start = ((f32[16,4,8,128]{3,2,1,0:T(8,128)}), f32[16,4,8,128]{3,2,1,0:T(8,128)S(1)}, u32[]{:S(2)}, u32[]{:S(2)}) async-start(f32[16,4,8,128]{3,2,1,0:T(8,128)} %bitcast.27), calls=%async_computation | async-start | bytes 524288 | tf_op jit(solution)/shard_map/all_to_all | solution.py:375
  85.9 3.7 %collective-permute-start.10 = (f32[2,64]{1,0:T(2,128)S(1)}, f32[2,64]{1,0:T(2,128)S(1)}, u32[]{:S(2)}, u32[]{:S(2)}) collective-permute-start(f32[2,64]{1,0:T(2,128)S(1)} %get-tuple-element.25), channel_id=1, source_target_pairs={{0,24},{8,0},{16,8},{24,16},{1,25},{9,1},{17,9},{25,17},{2,26},{10... | collective-permute-start | bytes 1544 | tf_op jit(solution)/shard_map/ppermute | solution.py:254
  86.5 3.6 %collective-permute-start.8 = (f32[2,64]{1,0:T(2,128)S(1)}, f32[2,64]{1,0:T(2,128)S(1)}, u32[]{:S(2)}, u32[]{:S(2)}) collective-permute-start(f32[2,64]{1,0:T(2,128)S(1)} %get-tuple-element.24), channel_id=1, source_target_pairs={{0,8},{8,16},{16,24},{24,0},{1,9},{9,17},{17,25},{25,1},{2,10},{10... | collective-permute-start | bytes 1544 | tf_op jit(solution)/shard_map/ppermute | solution.py:254
  88.0 5.1 %collective-permute-start.9 = (f32[2,64]{1,0:T(2,128)S(1)}, f32[2,64]{1,0:T(2,128)S(1)}, u32[]{:S(2)}, u32[]{:S(2)}) collective-permute-start(f32[2,64]{1,0:T(2,128)S(1)} %get-tuple-element.26), channel_id=1, source_target_pairs={{0,16},{8,24},{16,0},{24,8},{1,17},{9,25},{17,1},{25,9},{2,18},{10... | collective-permute-start | bytes 1544 | tf_op jit(solution)/shard_map/ppermute | solution.py:254

commit v4 on v3

--- a/solution.py
+++ b/solution.py
@@ -137,7 +137,7 @@
     lax.fori_loop(0, ADJ * NY // chunk, body, 0)
 
 
-def forward_kernel(meta, src_x, src_y, src_z, rows, lanes, mine, other, times_out, arrive_out, slow, even, odd, table, picked):
+def forward_kernel(meta, src_x, src_y, src_z, rows, lanes, mine, other, times_out, own_out, partner_out, slow, even, odd, table, picked, cells_in, times, arrived):
     half, core, offset, first = meta[0], meta[2], meta[3], meta[4]
     shape = (2, 8, 8, NZ)
     low = iota((8, NZ), 1) < HALF
@@ -147,12 +147,18 @@
     row_x = jnp.where(low, first, first + WIDE - 1)
     sign = jnp.where(low, 1, -1)
 
-    def of_layer(layer):
-        a, b = mine[offset + layer], other[offset + layer]
-        return jnp.concatenate([jnp.where(core == 0, a, b), jnp.where(core == 0, b, a)], axis=0)
+    window = pl.ds(offset, WIDE)
+    copies = [
+        pltpu.make_async_copy(mine.at[window], cells_in.at[:, pl.ds(4 * core, 4)], arrived.at[0]),
+        pltpu.make_async_copy(other.at[window], cells_in.at[:, pl.ds(4 - 4 * core, 4)], arrived.at[1]),
+    ]
+    for copy in copies:
+        copy.start()
+    for copy in copies:
+        copy.wait()
 
     def load(layer, carry):
-        cells = paired(of_layer(layer), of_layer(WIDE - 1 - layer), low)
+        cells = paired(cells_in[layer], cells_in[WIDE - 1 - layer], low)
         x = row_x + sign * layer
         inside = (x >= 0) & (x < NX)
         dx = (x - src_x[half]).astype(jnp.float32)
@@ -173,7 +179,7 @@
         after[pl.ds(layer, step)] = jnp.minimum(here, best + slow[pl.ds(layer, step)])
 
     even[WIDE // 2] = pltpu.roll(even[WIDE // 2 - 1], HALF, 3)
-    last = sweeps(1, ITERS, WIDE // 2, 20, even, odd, block)
+    last = sweeps(1, ITERS, WIDE // 2, 16, even, odd, block)
 
     def finish(j, carry):
         layer = ITERS + j
@@ -181,10 +187,12 @@
         cells = last[layer] - 0.5 * slow[layer]
         cells = jnp.where((x >= 0) & (x < NX), cells, -BIG)
         table[pl.ds(pl.multiple_of(j * 2 * NY, 2 * NY), 2 * NY), :] = cells.reshape(2 * NY, NZ)
-        times_out[j], times_out[SEEN - 1 - j] = parted(cells[0], cells[1], low)
+        times[j], times[SEEN - 1 - j] = parted(cells[0], cells[1], low)
         return carry
 
     lax.fori_loop(0, SEEN // 2, finish, 0, unroll=4)
+    leaving = pltpu.make_async_copy(times, times_out, arrived.at[0])
+    leaving.start()
     one = iota((1, NZ), 1)
 
     def pick(j, carry):
@@ -193,26 +201,40 @@
         return carry
 
     lax.fori_loop(0, picked.shape[0], pick, 0, unroll=16)
-    arrive_out[...] = lax.dot_general(
+    arrive = lax.dot_general(
         jnp.ones((8, NZ), jnp.float32),
         picked[...],
         (((1,), (1,)), ((), ())),
         precision=lax.Precision.HIGHEST,
         preferred_element_type=jnp.float32,
     )
-
-
-def adjoint_kernel(meta, times, count, seen, out, coef, even, odd, natural):
-    start = meta[5]
+    own_out[...] = arrive[:, : arrive.shape[1] // 2]
+    partner_out[...] = arrive[:, arrive.shape[1] // 2 :]
+    leaving.wait()
+
+
+def adjoint_kernel(meta, times_in, count_in, seen_in, out, coef, even, odd, natural, count, seen, times, arrived):
+    entering = pltpu.make_async_copy(times_in.at[pl.ds(meta[5], ADJ)], times, arrived.at[2])
+    entering.start()
+    copies = [
+        pltpu.make_async_copy(count_in, count, arrived.at[0]),
+        pltpu.make_async_copy(seen_in, seen, arrived.at[1]),
+    ]
+    for copy in copies:
+        copy.start()
     low = iota((8, NZ), 1) < HALF
     top = ADJ // 2
 
+    entering.wait()
+
     def load(layer, carry):
-        odd[layer] = paired(times[start + layer], times[start + ADJ - 1 - layer], low)
+        odd[layer] = paired(times[layer], times[ADJ - 1 - layer], low)
         return carry
 
     lax.fori_loop(0, top, load, 0, unroll=4)
     odd[top] = pltpu.roll(odd[top - 1], HALF, 3)
+    for copy in copies:
+        copy.wait()
 
     def weights(layer, size):
         where = pl.ds(layer, size)
@@ -272,6 +294,8 @@
 
 
 VMEM = pl.BlockSpec(memory_space=pltpu.VMEM)
+ANY = pl.BlockSpec(memory_space=pl.ANY)
+HBM = pl.BlockSpec(memory_space=pltpu.HBM)
 SMEM = pl.BlockSpec(memory_space=pltpu.SMEM)
 
 
@@ -291,22 +315,14 @@
     ).astype(jnp.int32)
 
     stations = station_x.shape[0]
-    params = pltpu.CompilerParams(vmem_limit_bytes=28 * 1024 * 1024)
-    count, seen = pl.pallas_call(
-        station_kernel,
-        out_shape=(f32(ADJ * 64, NZ), f32(ADJ * 64, NZ)),
-        in_specs=[SMEM, VMEM, VMEM, VMEM, VMEM],
-        out_specs=(VMEM, VMEM),
-        scratch_shapes=[pltpu.VMEM((4 * NZ, stations), jnp.bfloat16)],
-        compiler_params=params,
-        cost_estimate=pl.CostEstimate(
-            flops=2 * ADJ * 64 * stations * 4 * NZ, bytes_accessed=2 * ADJ * 64 * NZ * 4, transcendentals=0
-        ),
-        name="stations",
-    )(meta, station_x.reshape(1, -1), station_y.reshape(1, -1), station_z.reshape(1, -1), observed)
+
+    def params(mib):
+        return pltpu.CompilerParams(vmem_limit_bytes=mib * 1024 * 1024)
 
     def line_of(values):
-        return lax.dynamic_index_in_dim(values.reshape(4, 4, stations // 16), y, 1, keepdims=False)
+        line = lax.dynamic_index_in_dim(values.reshape(4, 4, 2, stations // 32), y, 1, keepdims=False)
+        own, partner = line[:, 0], line[:, 1]
+        return jnp.where(half == 0, jnp.stack([own, partner]), jnp.stack([partner, own]))
 
     at_x, at_y, at_z = line_of(station_x), line_of(station_y), line_of(station_z)
     owned = at_x // 32 == x
@@ -315,51 +331,70 @@
     row = (layer * 2 + at_z % 2) * NY + (at_y % 8) * 8 + at_y // 8
     rows = jnp.where(owned, row, 0).reshape(-1)
     lanes = jnp.where(owned, jnp.where(seen_x < SEEN // 2, 0, HALF) + at_z // 2, -1).reshape(-1)
+    later, rows, lanes = lax.optimization_barrier((meta, rows, lanes))
+
+    count, seen = pl.pallas_call(
+        station_kernel,
+        out_shape=(f32(ADJ * 64, NZ), f32(ADJ * 64, NZ)),
+        in_specs=[SMEM, VMEM, VMEM, VMEM, VMEM],
+        out_specs=(VMEM, VMEM),
+        scratch_shapes=[pltpu.VMEM((4 * NZ, stations), jnp.bfloat16)],
+        compiler_params=params(20),
+        cost_estimate=pl.CostEstimate(
+            flops=2 * ADJ * 64 * stations * 4 * NZ, bytes_accessed=2 * ADJ * 64 * NZ * 4, transcendentals=0
+        ),
+        name="stations",
+    )(later, station_x.reshape(1, -1), station_y.reshape(1, -1), station_z.reshape(1, -1), observed)
 
     part = pl.pallas_call(
         prepare_kernel,
         out_shape=f32(128, NZ),
         in_specs=[SMEM, VMEM],
         out_specs=VMEM,
-        compiler_params=params,
+        compiler_params=params(8),
         name="prepare",
     )(meta, slowness.reshape(-1, NZ))
     mine, other, (count, seen) = gathered(part.reshape(4, 4, 8, NZ), y, half, (count, seen))
-    times, arrive = pl.pallas_call(
+    times, own, partner = pl.pallas_call(
         forward_kernel,
-        out_shape=(f32(SEEN, 8, 8, NZ), f32(8, stations // 4)),
-        in_specs=[SMEM] * 6 + [VMEM, VMEM],
-        out_specs=(VMEM, VMEM),
+        out_shape=(f32(SEEN, 8, 8, NZ), f32(8, stations // 8), f32(8, stations // 8)),
+        in_specs=[SMEM] * 6 + [ANY, ANY],
+        out_specs=(HBM, VMEM, VMEM),
         scratch_shapes=[
             pltpu.VMEM((WIDE // 2, 2, 8, 8, NZ), jnp.float32),
             pltpu.VMEM((WIDE // 2 + 1, 2, 8, 8, NZ), jnp.float32),
             pltpu.VMEM((WIDE // 2 + 1, 2, 8, 8, NZ), jnp.float32),
             pltpu.VMEM((SEEN * NY, NZ), jnp.float32),
             pltpu.VMEM((stations // 4, NZ), jnp.float32),
+            pltpu.VMEM((WIDE, 8, 8, NZ), jnp.float32),
+            pltpu.VMEM((SEEN, 8, 8, NZ), jnp.float32),
+            pltpu.SemaphoreType.DMA((2,)),
         ],
-        compiler_params=params,
+        compiler_params=params(28),
         cost_estimate=pl.CostEstimate(
             flops=7 * ITERS * WIDE * 8192, bytes_accessed=WIDE * 8192 * 8, transcendentals=WIDE * 8192
         ),
         name="forward",
     )(meta, source_x, source_y, source_z, rows, lanes, mine, other)
 
-    arrive = arrive[0].reshape(4, 2, stations // 32)
-    own = lax.dynamic_index_in_dim(arrive, half, 1, keepdims=False)
-    partner = cycle(lax.dynamic_index_in_dim(arrive, 1 - half, 1, keepdims=False), "half", 2, 1)
+    partner = cycle(partner, "half", 2, 1)
 
     pieces = pl.pallas_call(
         adjoint_kernel,
         out_shape=f32(512, NZ),
-        in_specs=[SMEM, VMEM, VMEM, VMEM],
+        in_specs=[SMEM, HBM, HBM, HBM],
         out_specs=VMEM,
         scratch_shapes=[
             pltpu.VMEM((7, ADJ // 2, 2, 8, 8, NZ), jnp.float32),
             pltpu.VMEM((ADJ // 2 + 1, 2, 8, 8, NZ), jnp.float32),
             pltpu.VMEM((ADJ // 2 + 1, 2, 8, 8, NZ), jnp.float32),
             pltpu.VMEM((LAYERS, 8, 8, NZ), jnp.float32),
+            pltpu.VMEM((ADJ // 2, 2, 8, 8, NZ), jnp.float32),
+            pltpu.VMEM((ADJ // 2, 2, 8, 8, NZ), jnp.float32),
+            pltpu.VMEM((ADJ, 8, 8, NZ), jnp.float32),
+            pltpu.SemaphoreType.DMA((3,)),
         ],
-        compiler_params=params,
+        compiler_params=params(56),
         cost_estimate=pl.CostEstimate(
             flops=12 * ITERS * ADJ * 8192, bytes_accessed=4 * ADJ * 8192 * 4, transcendentals=ADJ * 8192
         ),
@@ -376,6 +411,7 @@
     )
     kernel = lax.dynamic_slice(slowness, (0, group * 8, 0), (4, 8, NZ)) * summed
 
+    own, partner = own[0].reshape(4, stations // 32), partner[0].reshape(4, stations // 32)
     known = jnp.where(half == 0, jnp.stack([own, partner], 1), jnp.stack([partner, own], 1))
     arrivals = lax.dynamic_index_in_dim(known, x, 0, keepdims=False)
     for shift in (1, 2, 3):

time: 100 us -> 96.3 us (0.963)
  waiting for transfers between devices: 21.2 us -> 19.3 us
  local copies, waits for them, and re-layouts: 6.49 us -> 5.09 us
    unnamed x28 -> x24, local copies, waits for them, and re-layouts: 6.16 us -> 2.1 us
    ppermute x9, waiting for transfers between devices: 14.1 us -> 11.6 us  [cycle(): lax.ppermute(cells, axis, [(i, (i + shift) % size) for i in range(size)])]
    reshape x0 -> x3, local copies, waits for them, and re-layouts: none -> 2.33 us  [line_of(): values.reshape(4, 4, 2, stations // 32)]
    pallas_call x1, Pallas kernels: 17.7 us -> 15.9 us  [per_device(): pl.pallas_call(forward_kernel, out_shape=(f32(SEEN, 8, 8, NZ), f32(8, sta...]
    pallas_call x1, Pallas kernels: 9.84 us -> 11.4 us  [per_device(): pl.pallas_call(adjoint_kernel, out_shape=f32(512, NZ), in_specs=[SMEM, HB...]
  transfers between devices with their start and end apart: 12 -> 12, of which waited for: 9 -> 9; matrix products, arithmetic and copies ran while one was open for 1% -> 4% of each run, Pallas kernels for 18% -> 21%
where the time goes in v4:
time: 96.3 us; the launch traced here: 95.3 us
  Pallas kernels  36.4 us (38%)
  starting transfers between devices  31.5 us (33%)
  waiting for transfers between devices  19.3 us (20%)
  local copies, waits for them, and re-layouts  5.09 us (5%)
  other arithmetic  2.13 us (2%)
    ppermute x9, starting transfers between devices, cycle(): lax.ppermute(cells, axis, [(i, (i + shift) % size) for i in range(size)])  21 us
    pallas_call x1, Pallas kernels, per_device(): pl.pallas_call(forward_kernel, out_shape=(f32(SEEN, 8, 8, NZ), f32(8, sta...  15.9 us
    ppermute x9, waiting for transfers between devices, cycle(): lax.ppermute(cells, axis, [(i, (i + shift) % size) for i in range(size)])  11.6 us
    pallas_call x1, Pallas kernels, per_device(): pl.pallas_call(adjoint_kernel, out_shape=f32(512, NZ), in_specs=[SMEM, HB...  11.4 us
    pallas_call x1, Pallas kernels, per_device(): pl.pallas_call(station_kernel, out_shape=(f32(ADJ * 64, NZ), f32(ADJ * 64...  8.42 us
    all_to_all x1, starting transfers between devices, per_device(): lax.all_to_all(pieces.reshape(16, 4, 8, NZ), ('zlo', 'core', 'half'), 0,...  4.55 us
    all_to_all x1, waiting for transfers between devices, per_device(): lax.all_to_all(pieces.reshape(16, 4, 8, NZ), ('zlo', 'core', 'half'), 0,...  4.32 us
    ppermute x1, starting transfers between devices, gathered(): before = lax.ppermute(block, 'x', [(0, 1), (1, 2), (2, 3)])  3.4 us
  transfers between devices with their start and end apart: 12, of which 9 were waited for; matrix products, arithmetic and copies ran while one was open for 4% of the time, Pallas kernels for 21%

profile of v4, /device:TPU:2, one launch (start us, length us, event | category | flops | bytes accessed | tf_op | source)
XLA Modules:
  0.0 95.3 jit_solution(13375842289652892472)
XLA Ops:
  0.6 0.0 copy-start.5
  0.6 0.0 copy-start.4
  0.7 0.0 copy-start.6
  0.7 0.0 copy-start.11
  0.7 0.1 stack.51.meta
  0.8 0.9 copy-done.3
  1.7 0.7 prepare.1
  2.4 7.3 %collective-permute-start = (f32[4,4,8,128]{3,2,1,0:T(8,128)S(1)}, f32[4,4,8,128]{3,2,1,0:T(8,128)S(1)}, u32[]{:S(2)}, u32[]{:S(2)}) collective-permute-start(f32[4,4,8,128]{3,2,1,0:T(8,128)S(1)} %bitcast.63), channel_id=1, source_target_pairs={{0,1},{1,0},{2,3},{3,2},{4,5},{5,4},{6,7},{7,6},{8,9},{9,8},{10,11... | collective-permute-start | bytes 196616 | tf_op jit(solution)/shard_map/ppermute | solution.py:276
  9.7 0.8 reshape.116
  10.5 0.8 reshape.117
  11.3 0.8 reshape.115
  12.1 0.0 collective-permute-done
  12.1 1.7 %collective-permute-start.1 = (f32[8,4,8,128]{3,2,1,0:T(8,128)S(1)}, f32[8,4,8,128]{3,2,1,0:T(8,128)S(1)}, u32[]{:S(2)}, u32[]{:S(2)}) collective-permute-start(f32[8,4,8,128]{3,2,1,0:T(8,128)S(1)} %maximum_select_fusion.1), channel_id=1, source_target_pairs={{0,2},{2,4},{4,6},{6,0},{1,3},{3,5},{5,7},{7,1},{8,10},{10,12},{12... | collective-permute-start | bytes 393224 | tf_op jit(solution)/shard_map/ppermute | solution.py:276
  13.8 0.1 select_n.173
  13.9 0.1 select_n.170
  13.9 0.1 select_n.167
  14.0 1.7 %collective-permute-start.2 = (f32[8,4,8,128]{3,2,1,0:T(8,128)S(1)}, f32[8,4,8,128]{3,2,1,0:T(8,128)S(1)}, u32[]{:S(2)}, u32[]{:S(2)}) collective-permute-start(f32[8,4,8,128]{3,2,1,0:T(8,128)S(1)} %maximum_select_fusion.1), channel_id=1, source_target_pairs={{0,6},{2,0},{4,2},{6,4},{1,7},{3,1},{5,3},{7,5},{8,14},{10,8},{12,... | collective-permute-start | bytes 393224 | tf_op jit(solution)/shard_map/ppermute | solution.py:276
  15.7 2.0 %collective-permute-start.3 = (f32[8,4,8,128]{3,2,1,0:T(8,128)S(1)}, f32[8,4,8,128]{3,2,1,0:T(8,128)S(1)}, u32[]{:S(2)}, u32[]{:S(2)}) collective-permute-start(f32[8,4,8,128]{3,2,1,0:T(8,128)S(1)} %maximum_select_fusion.1), channel_id=1, source_target_pairs={{0,4},{2,6},{4,0},{6,2},{1,5},{3,7},{5,1},{7,3},{8,12},{10,14},{12... | collective-permute-start | bytes 393224 | tf_op jit(solution)/shard_map/ppermute | solution.py:276
  17.8 0.7 collective-permute-done.1
  18.4 1.6 %collective-permute-done.2 = f32[8,4,8,128]{3,2,1,0:T(8,128)S(1)} collective-permute-done((f32[8,4,8,128]{3,2,1,0:T(8,128)S(1)}, f32[8,4,8,128]{3,2,1,0:T(8,128)S(1)}, u32[]{:S(2)}, u32[]{:S(2)}) %collective-permute-start.2) | collective-permute-done | bytes 131104 | tf_op jit(solution)/shard_map/ppermute | solution.py:276
  20.1 2.3 %collective-permute-done.3 = f32[8,4,8,128]{3,2,1,0:T(8,128)S(1)} collective-permute-done((f32[8,4,8,128]{3,2,1,0:T(8,128)S(1)}, f32[8,4,8,128]{3,2,1,0:T(8,128)S(1)}, u32[]{:S(2)}, u32[]{:S(2)}) %collective-permute-start.3) | collective-permute-done | bytes 131104 | tf_op jit(solution)/shard_map/ppermute | solution.py:276
  22.4 3.4 %collective-permute-start.4 = (f32[32,4,8,128]{3,2,1,0:T(8,128)S(1)}, f32[32,4,8,128]{3,2,1,0:T(8,128)S(1)}, u32[]{:S(2)}, u32[]{:S(2)}) collective-permute-start(f32[32,4,8,128]{3,2,1,0:T(8,128)S(1)} %bitcast.70), channel_id=1, source_target_pairs={{0,8},{8,16},{16,24},{1,9},{9,17},{17,25},{2,10},{10,18},{18,26},{... | collective-permute-start | bytes 1572872 | tf_op jit(solution)/shard_map/ppermute | solution.py:289
  25.9 2.5 %collective-permute-start.5 = (f32[32,4,8,128]{3,2,1,0:T(8,128)S(1)}, f32[32,4,8,128]{3,2,1,0:T(8,128)S(1)}, u32[]{:S(2)}, u32[]{:S(2)}) collective-permute-start(f32[32,4,8,128]{3,2,1,0:T(8,128)S(1)} %bitcast.71), channel_id=1, source_target_pairs={{8,0},{16,8},{24,16},{9,1},{17,9},{25,17},{10,2},{18,10},{26,18},{... | collective-permute-start | bytes 1572872 | tf_op jit(solution)/shard_map/ppermute | solution.py:290
  28.4 0.0 copy-done.5
  28.4 0.0 copy-done.4
  28.4 8.4 %stations.1 = (f32[2560,128]{1,0:T(8,128)S(1)}, f32[2560,128]{1,0:T(8,128)S(1)}) custom-call(s32[6]{0:T(128)S(1)} %stack.51.meta, s32[1,2048]{1,0:T(1,128)S(1)} %bitcast.69, s32[1,2048]{1,0:T(1,128)S(1)} %bitcast.67, s32[1,2048]{1,0:T(1,128)S(1)} %bitcast.68, f32[2,2048]{1,0:T(2,128)S(1)} %copy-done.11), custom_call_target="tpu_custom_call" | custom-call | flops 5368709120 | bytes 2621440 | tf_op jit(solution)/shard_map/stations/pallas_call | solution.py:336
  36.9 0.2 collective-permute-done.4
  37.1 3.1 %collective-permute-done.5 = f32[32,4,8,128]{3,2,1,0:T(8,128)S(1)} collective-permute-done((f32[32,4,8,128]{3,2,1,0:T(8,128)S(1)}, f32[32,4,8,128]{3,2,1,0:T(8,128)S(1)}, u32[]{:S(2)}, u32[]{:S(2)}) %collective-permute-start.5) | collective-permute-done | bytes 524320 | tf_op jit(solution)/shard_map/ppermute | solution.py:290
  40.2 0.1 pad_maximum_fusion.mine
  40.4 0.3 collective-permute-start.6
  40.6 3.4 %collective-permute-done.6.other = f32[96,4,8,128]{3,2,1,0:T(8,128)S(1)} collective-permute-done((f32[96,4,8,128]{3,2,1,0:T(8,128)S(1)}, f32[96,4,8,128]{3,2,1,0:T(8,128)S(1)}, u32[]{:S(2)}, u32[]{:S(2)}) %collective-permute-start.6) | collective-permute-done | bytes 1572896 | tf_op jit(solution)/shard_map/ppermute | solution.py:276
  44.1 15.9 %forward.1 = (f32[48,8,8,128]{3,2,1,0:T(8,128)S(1)}, f32[8,256]{1,0:T(8,128)S(1)}, f32[8,256]{1,0:T(8,128)S(1)}) custom-call(s32[6]{0:T(128)S(1)} %stack.51.meta, s32[2]{0:T(128)S(1)} %copy-done.8, s32[2]{0:T(128)S(1)} %copy-done.9, s32[2]{0:T(128)S(1)} %copy-done.10, s32[512]{0:T(512)S(1)} %get-tuple-element.17.rows, s32[512]{0:T(512)S(1)} %get-tuple-element.18.lanes, ...), custom_call_target="tpu_custom_call" | custom-call | flops 73400320 | bytes 5242880 | tf_op jit(solution)/shard_map/forward/pallas_call | solution.py:358
  59.9 1.1 %copy-done = f32[48,8,8,128]{3,2,1,0:T(8,128)} copy-done((f32[48,8,8,128]{3,2,1,0:T(8,128)}, f32[48,8,8,128]{3,2,1,0:T(8,128)S(1)}, u32[]{:S(2)}) %copy-start) | copy-done | bytes 1572888
  61.1 4.5 %collective-permute-start.7 = (f32[8,256]{1,0:T(8,128)S(1)}, f32[8,256]{1,0:T(8,128)S(1)}, u32[]{:S(2)}, u32[]{:S(2)}) collective-permute-start(f32[8,256]{1,0:T(8,128)S(1)} %get-tuple-element.28), channel_id=1, source_target_pairs={{0,1},{1,0},{2,3},{3,2},{4,5},{5,4},{6,7},{7,6},{8,9},{9,8},{10,11... | collective-permute-start | bytes 24584 | tf_op jit(solution)/shard_map/ppermute | solution.py:276
  65.6 11.4 %adjoint.1 = f32[512,128]{1,0:T(8,128)} custom-call(s32[6]{0:T(128)} %copy-done.7, f32[48,8,8,128]{3,2,1,0:T(8,128)} %copy-done, f32[20,2,8,8,128]{4,3,2,1,0:T(8,128)} %bitcast.61, f32[20,2,8,8,128]{4,3,2,1,0:T(8,128)} %bitcast.62), custom_call_target="tpu_custom_call" | custom-call | flops 62914560 | bytes 5242880 | tf_op jit(solution)/shard_map/adjoint/pallas_call | solution.py:382
  77.1 0.0 collective-permute-done.7
  77.1 4.5 %all-to-all-start = ((f32[16,4,8,128]{3,2,1,0:T(8,128)}), f32[16,4,8,128]{3,2,1,0:T(8,128)S(1)}, u32[]{:S(2)}, u32[]{:S(2)}) async-start(f32[16,4,8,128]{3,2,1,0:T(8,128)} %bitcast.73), calls=%async_computation | async-start | bytes 524288 | tf_op jit(solution)/shard_map/all_to_all | solution.py:410
  81.7 0.1 stack_reshape_squeeze.8
  81.8 0.1 stack_reshape_squeeze.9
  81.9 0.6 collective-permute-start.10
  82.5 1.5 %collective-permute-start.8 = (f32[2,64]{1,0:T(2,128)S(1)}, f32[2,64]{1,0:T(2,128)S(1)}, u32[]{:S(2)}, u32[]{:S(2)}) collective-permute-start(f32[2,64]{1,0:T(2,128)S(1)} %get-tuple-element.32), channel_id=1, source_target_pairs={{0,8},{8,16},{16,24},{24,0},{1,9},{9,17},{17,25},{25,1},{2,10},{10... | collective-permute-start | bytes 1544 | tf_op jit(solution)/shard_map/ppermute | solution.py:276
  84.0 1.5 %collective-permute-start.9 = (f32[2,64]{1,0:T(2,128)S(1)}, f32[2,64]{1,0:T(2,128)S(1)}, u32[]{:S(2)}, u32[]{:S(2)}) collective-permute-start(f32[2,64]{1,0:T(2,128)S(1)} %get-tuple-element.34), channel_id=1, source_target_pairs={{0,16},{8,24},{16,0},{24,8},{1,17},{9,25},{17,1},{25,9},{2,18},{10... | collective-permute-start | bytes 1544 | tf_op jit(solution)/shard_map/ppermute | solution.py:276
  85.5 0.0 collective-permute-done.10
  85.5 0.6 collective-permute-done.8
  86.1 3.0 %collective-permute-done.9 = f32[2,64]{1,0:T(2,128)S(1)} collective-permute-done((f32[2,64]{1,0:T(2,128)S(1)}, f32[2,64]{1,0:T(2,128)S(1)}, u32[]{:S(2)}, u32[]{:S(2)}) %collective-permute-start.9) | collective-permute-done | bytes 544 | tf_op jit(solution)/shard_map/ppermute | solution.py:276
  89.1 0.6 fusion.19
  89.6 4.3 %all-to-all-done = f32[16,4,8,128]{3,2,1,0:T(8,128)S(1)} async-done(((f32[16,4,8,128]{3,2,1,0:T(8,128)}), f32[16,4,8,128]{3,2,1,0:T(8,128)S(1)}, u32[]{:S(2)}, u32[]{:S(2)}) %all-to-all-start) | async-done | bytes 262176 | tf_op jit(solution)/shard_map/all_to_all | solution.py:410
  94.0 1.3 %dynamic-slice_multiply_fusion = f32[4,8,128]{2,1,0:T(8,128)} fusion(f32[4,8,128]{2,1,0:T(8,128)S(1)} %reduce_sum.9, f32[4,64,128]{2,1,0:T(8,128)} %param.8, s32[]{:T(128)S(6)} %select_n.162), kind=kLoop, calls=%fused_computation.7 | loop fusion | flops 4096 | bytes 49156 | tf_op jit(solution)/shard_map/mul | solution.py:412
  (36 shorter events, 0.3 us)
Async XLA Ops:
  0.6 27.7 %copy-start.5 = (s32[2048]{0:T(1024)S(1)}, s32[2048]{0:T(1024)}, u32[]{:S(2)}) copy-start(s32[2048]{0:T(1024)} %param.14) | copy-start | bytes 24580
  0.6 27.7 %copy-start.4 = (s32[2048]{0:T(1024)S(1)}, s32[2048]{0:T(1024)}, u32[]{:S(2)}) copy-start(s32[2048]{0:T(1024)} %param.13) | copy-start | bytes 24580
  0.7 27.7 %copy-start.6 = (s32[2048]{0:T(1024)S(1)}, s32[2048]{0:T(1024)}, u32[]{:S(2)}) copy-start(s32[2048]{0:T(1024)} %param.12) | copy-start | bytes 24580
  0.7 27.7 %copy-start.11 = (f32[2,2048]{1,0:T(2,128)S(1)}, f32[2,2048]{1,0:T(2,128)}, u32[]{:S(2)}) copy-start(f32[2,2048]{1,0:T(2,128)} %obs.1) | copy-start | bytes 49156
  0.8 43.3 %copy-start.7 = (s32[6]{0:T(128)}, s32[6]{0:T(128)S(1)}, u32[]{:S(2)}) copy-start(s32[6]{0:T(128)S(1)} %stack.51.meta) | copy-start | bytes 76
  0.8 0.9 copy-start.3
  2.4 9.7 %collective-permute-start = (f32[4,4,8,128]{3,2,1,0:T(8,128)S(1)}, f32[4,4,8,128]{3,2,1,0:T(8,128)S(1)}, u32[]{:S(2)}, u32[]{:S(2)}) collective-permute-start(f32[4,4,8,128]{3,2,1,0:T(8,128)S(1)} %bitcast.63), channel_id=1, source_target_pairs={{0,1},{1,0},{2,3},{3,2},{4,5},{5,4},{6,7},{7,6},{8,9},{9,8},{10,11... | collective-permute-start | bytes 196616 | tf_op jit(solution)/shard_map/ppermute | solution.py:276
  12.1 6.3 %collective-permute-start.1 = (f32[8,4,8,128]{3,2,1,0:T(8,128)S(1)}, f32[8,4,8,128]{3,2,1,0:T(8,128)S(1)}, u32[]{:S(2)}, u32[]{:S(2)}) collective-permute-start(f32[8,4,8,128]{3,2,1,0:T(8,128)S(1)} %maximum_select_fusion.1), channel_id=1, source_target_pairs={{0,2},{2,4},{4,6},{6,0},{1,3},{3,5},{5,7},{7,1},{8,10},{10,12},{12... | collective-permute-start | bytes 393224 | tf_op jit(solution)/shard_map/ppermute | solution.py:276
  14.0 6.1 %collective-permute-start.2 = (f32[8,4,8,128]{3,2,1,0:T(8,128)S(1)}, f32[8,4,8,128]{3,2,1,0:T(8,128)S(1)}, u32[]{:S(2)}, u32[]{:S(2)}) collective-permute-start(f32[8,4,8,128]{3,2,1,0:T(8,128)S(1)} %maximum_select_fusion.1), channel_id=1, source_target_pairs={{0,6},{2,0},{4,2},{6,4},{1,7},{3,1},{5,3},{7,5},{8,14},{10,8},{12,... | collective-permute-start | bytes 393224 | tf_op jit(solution)/shard_map/ppermute | solution.py:276
  15.7 6.7 %collective-permute-start.3 = (f32[8,4,8,128]{3,2,1,0:T(8,128)S(1)}, f32[8,4,8,128]{3,2,1,0:T(8,128)S(1)}, u32[]{:S(2)}, u32[]{:S(2)}) collective-permute-start(f32[8,4,8,128]{3,2,1,0:T(8,128)S(1)} %maximum_select_fusion.1), channel_id=1, source_target_pairs={{0,4},{2,6},{4,0},{6,2},{1,5},{3,7},{5,1},{7,3},{8,12},{10,14},{12... | collective-permute-start | bytes 393224 | tf_op jit(solution)/shard_map/ppermute | solution.py:276
  22.4 14.6 %collective-permute-start.4 = (f32[32,4,8,128]{3,2,1,0:T(8,128)S(1)}, f32[32,4,8,128]{3,2,1,0:T(8,128)S(1)}, u32[]{:S(2)}, u32[]{:S(2)}) collective-permute-start(f32[32,4,8,128]{3,2,1,0:T(8,128)S(1)} %bitcast.70), channel_id=1, source_target_pairs={{0,8},{8,16},{16,24},{1,9},{9,17},{17,25},{2,10},{10,18},{18,26},{... | collective-permute-start | bytes 1572872 | tf_op jit(solution)/shard_map/ppermute | solution.py:289
  25.9 14.4 %collective-permute-start.5 = (f32[32,4,8,128]{3,2,1,0:T(8,128)S(1)}, f32[32,4,8,128]{3,2,1,0:T(8,128)S(1)}, u32[]{:S(2)}, u32[]{:S(2)}) collective-permute-start(f32[32,4,8,128]{3,2,1,0:T(8,128)S(1)} %bitcast.71), channel_id=1, source_target_pairs={{8,0},{16,8},{24,16},{9,1},{17,9},{25,17},{10,2},{18,10},{26,18},{... | collective-permute-start | bytes 1572872 | tf_op jit(solution)/shard_map/ppermute | solution.py:290
  36.8 3.5 %copy-start.1 = (f32[2560,128]{1,0:T(8,128)}, f32[2560,128]{1,0:T(8,128)S(1)}, u32[]{:S(2)}) copy-start(f32[2560,128]{1,0:T(8,128)S(1)} %get-tuple-element.25) | copy-start | bytes 3932164
  36.8 3.5 %copy-start.2 = (f32[2560,128]{1,0:T(8,128)}, f32[2560,128]{1,0:T(8,128)S(1)}, u32[]{:S(2)}) copy-start(f32[2560,128]{1,0:T(8,128)S(1)} %get-tuple-element.26) | copy-start | bytes 3932164
  40.2 3.8 %copy-start.8 = (s32[2]{0:T(128)S(1)}, s32[2]{0:T(128)}, u32[]{:S(2)}) copy-start(s32[2]{0:T(128)} %src_x.1) | copy-start | bytes 28
  40.2 3.8 %copy-start.9 = (s32[2]{0:T(128)S(1)}, s32[2]{0:T(128)}, u32[]{:S(2)}) copy-start(s32[2]{0:T(128)} %src_y.1) | copy-start | bytes 28
  40.2 3.8 %copy-start.10 = (s32[2]{0:T(128)S(1)}, s32[2]{0:T(128)}, u32[]{:S(2)}) copy-start(s32[2]{0:T(128)} %src_z.1) | copy-start | bytes 28
  40.4 3.7 %collective-permute-start.6 = (f32[96,4,8,128]{3,2,1,0:T(8,128)S(1)}, f32[96,4,8,128]{3,2,1,0:T(8,128)S(1)}, u32[]{:S(2)}, u32[]{:S(2)}) collective-permute-start(f32[96,4,8,128]{3,2,1,0:T(8,128)S(1)} %pad_maximum_fusion.mine), channel_id=1, source_target_pairs={{0,32},{32,0},{1,33},{33,1},{2,34},{34,2},{3,35},{35,3},{4,36},{36... | collective-permute-start | bytes 4718600 | tf_op jit(solution)/shard_map/ppermute | solution.py:276
  59.9 1.2 %copy-start = (f32[48,8,8,128]{3,2,1,0:T(8,128)}, f32[48,8,8,128]{3,2,1,0:T(8,128)S(1)}, u32[]{:S(2)}) copy-start(f32[48,8,8,128]{3,2,1,0:T(8,128)S(1)} %get-tuple-element.24.times_in) | copy-start | bytes 4718596
  61.1 16.0 %collective-permute-start.7 = (f32[8,256]{1,0:T(8,128)S(1)}, f32[8,256]{1,0:T(8,128)S(1)}, u32[]{:S(2)}, u32[]{:S(2)}) collective-permute-start(f32[8,256]{1,0:T(8,128)S(1)} %get-tuple-element.28), channel_id=1, source_target_pairs={{0,1},{1,0},{2,3},{3,2},{4,5},{5,4},{6,7},{7,6},{8,9},{9,8},{10,11... | collective-permute-start | bytes 24584 | tf_op jit(solution)/shard_map/ppermute | solution.py:276
  77.1 16.8 %all-to-all-start = ((f32[16,4,8,128]{3,2,1,0:T(8,128)}), f32[16,4,8,128]{3,2,1,0:T(8,128)S(1)}, u32[]{:S(2)}, u32[]{:S(2)}) async-start(f32[16,4,8,128]{3,2,1,0:T(8,128)} %bitcast.73), calls=%async_computation | async-start | bytes 524288 | tf_op jit(solution)/shard_map/all_to_all | solution.py:410
  81.9 3.6 %collective-permute-start.10 = (f32[2,64]{1,0:T(2,128)S(1)}, f32[2,64]{1,0:T(2,128)S(1)}, u32[]{:S(2)}, u32[]{:S(2)}) collective-permute-start(f32[2,64]{1,0:T(2,128)S(1)} %get-tuple-element.33), channel_id=1, source_target_pairs={{0,24},{8,0},{16,8},{24,16},{1,25},{9,1},{17,9},{25,17},{2,26},{10... | collective-permute-start | bytes 1544 | tf_op jit(solution)/shard_map/ppermute | solution.py:276
  82.5 3.6 %collective-permute-start.8 = (f32[2,64]{1,0:T(2,128)S(1)}, f32[2,64]{1,0:T(2,128)S(1)}, u32[]{:S(2)}, u32[]{:S(2)}) collective-permute-start(f32[2,64]{1,0:T(2,128)S(1)} %get-tuple-element.32), channel_id=1, source_target_pairs={{0,8},{8,16},{16,24},{24,0},{1,9},{9,17},{17,25},{25,1},{2,10},{10... | collective-permute-start | bytes 1544 | tf_op jit(solution)/shard_map/ppermute | solution.py:276
  84.0 5.1 %collective-permute-start.9 = (f32[2,64]{1,0:T(2,128)S(1)}, f32[2,64]{1,0:T(2,128)S(1)}, u32[]{:S(2)}, u32[]{:S(2)}) collective-permute-start(f32[2,64]{1,0:T(2,128)S(1)} %get-tuple-element.34), channel_id=1, source_target_pairs={{0,16},{8,24},{16,0},{24,8},{1,17},{9,25},{17,1},{25,9},{2,18},{10... | collective-permute-start | bytes 1544 | tf_op jit(solution)/shard_map/ppermute | solution.py:276

commit v5 on v3

--- a/solution.py
+++ b/solution.py
@@ -137,7 +137,7 @@
     lax.fori_loop(0, ADJ * NY // chunk, body, 0)
 
 
-def forward_kernel(meta, src_x, src_y, src_z, rows, lanes, mine, other, times_out, arrive_out, slow, even, odd, table, picked):
+def forward_kernel(meta, src_x, src_y, src_z, rows, lanes, mine, other, times_out, own_out, partner_out, slow, even, odd, table, picked):
     half, core, offset, first = meta[0], meta[2], meta[3], meta[4]
     shape = (2, 8, 8, NZ)
     low = iota((8, NZ), 1) < HALF
@@ -173,7 +173,7 @@
         after[pl.ds(layer, step)] = jnp.minimum(here, best + slow[pl.ds(layer, step)])
 
     even[WIDE // 2] = pltpu.roll(even[WIDE // 2 - 1], HALF, 3)
-    last = sweeps(1, ITERS, WIDE // 2, 20, even, odd, block)
+    last = sweeps(1, ITERS, WIDE // 2, 16, even, odd, block)
 
     def finish(j, carry):
         layer = ITERS + j
@@ -193,13 +193,15 @@
         return carry
 
     lax.fori_loop(0, picked.shape[0], pick, 0, unroll=16)
-    arrive_out[...] = lax.dot_general(
+    arrive = lax.dot_general(
         jnp.ones((8, NZ), jnp.float32),
         picked[...],
         (((1,), (1,)), ((), ())),
         precision=lax.Precision.HIGHEST,
         preferred_element_type=jnp.float32,
     )
+    own_out[...] = arrive[:, : arrive.shape[1] // 2]
+    partner_out[...] = arrive[:, arrive.shape[1] // 2 :]
 
 
 def adjoint_kernel(meta, times, count, seen, out, coef, even, odd, natural):
@@ -291,22 +293,14 @@
     ).astype(jnp.int32)
 
     stations = station_x.shape[0]
-    params = pltpu.CompilerParams(vmem_limit_bytes=28 * 1024 * 1024)
-    count, seen = pl.pallas_call(
-        station_kernel,
-        out_shape=(f32(ADJ * 64, NZ), f32(ADJ * 64, NZ)),
-        in_specs=[SMEM, VMEM, VMEM, VMEM, VMEM],
-        out_specs=(VMEM, VMEM),
-        scratch_shapes=[pltpu.VMEM((4 * NZ, stations), jnp.bfloat16)],
-        compiler_params=params,
-        cost_estimate=pl.CostEstimate(
-            flops=2 * ADJ * 64 * stations * 4 * NZ, bytes_accessed=2 * ADJ * 64 * NZ * 4, transcendentals=0
-        ),
-        name="stations",
-    )(meta, station_x.reshape(1, -1), station_y.reshape(1, -1), station_z.reshape(1, -1), observed)
+
+    def params(mib):
+        return pltpu.CompilerParams(vmem_limit_bytes=mib * 1024 * 1024)
 
     def line_of(values):
-        return lax.dynamic_index_in_dim(values.reshape(4, 4, stations // 16), y, 1, keepdims=False)
+        line = lax.dynamic_index_in_dim(values.reshape(4, 4, 2, stations // 32), y, 1, keepdims=False)
+        own, partner = line[:, 0], line[:, 1]
+        return jnp.where(half == 0, jnp.stack([own, partner]), jnp.stack([partner, own]))
 
     at_x, at_y, at_z = line_of(station_x), line_of(station_y), line_of(station_z)
     owned = at_x // 32 == x
@@ -315,21 +309,35 @@
     row = (layer * 2 + at_z % 2) * NY + (at_y % 8) * 8 + at_y // 8
     rows = jnp.where(owned, row, 0).reshape(-1)
     lanes = jnp.where(owned, jnp.where(seen_x < SEEN // 2, 0, HALF) + at_z // 2, -1).reshape(-1)
+    later, rows, lanes = lax.optimization_barrier((meta, rows, lanes))
+
+    count, seen = pl.pallas_call(
+        station_kernel,
+        out_shape=(f32(ADJ * 64, NZ), f32(ADJ * 64, NZ)),
+        in_specs=[SMEM, VMEM, VMEM, VMEM, VMEM],
+        out_specs=(VMEM, VMEM),
+        scratch_shapes=[pltpu.VMEM((4 * NZ, stations), jnp.bfloat16)],
+        compiler_params=params(28),
+        cost_estimate=pl.CostEstimate(
+            flops=2 * ADJ * 64 * stations * 4 * NZ, bytes_accessed=2 * ADJ * 64 * NZ * 4, transcendentals=0
+        ),
+        name="stations",
+    )(later, station_x.reshape(1, -1), station_y.reshape(1, -1), station_z.reshape(1, -1), observed)
 
     part = pl.pallas_call(
         prepare_kernel,
         out_shape=f32(128, NZ),
         in_specs=[SMEM, VMEM],
         out_specs=VMEM,
-        compiler_params=params,
+        compiler_params=params(28),
         name="prepare",
     )(meta, slowness.reshape(-1, NZ))
     mine, other, (count, seen) = gathered(part.reshape(4, 4, 8, NZ), y, half, (count, seen))
-    times, arrive = pl.pallas_call(
+    times, own, partner = pl.pallas_call(
         forward_kernel,
-        out_shape=(f32(SEEN, 8, 8, NZ), f32(8, stations // 4)),
+        out_shape=(f32(SEEN, 8, 8, NZ), f32(8, stations // 8), f32(8, stations // 8)),
         in_specs=[SMEM] * 6 + [VMEM, VMEM],
-        out_specs=(VMEM, VMEM),
+        out_specs=(VMEM, VMEM, VMEM),
         scratch_shapes=[
             pltpu.VMEM((WIDE // 2, 2, 8, 8, NZ), jnp.float32),
             pltpu.VMEM((WIDE // 2 + 1, 2, 8, 8, NZ), jnp.float32),
@@ -337,16 +345,12 @@
             pltpu.VMEM((SEEN * NY, NZ), jnp.float32),
             pltpu.VMEM((stations // 4, NZ), jnp.float32),
         ],
-        compiler_params=params,
+        compiler_params=params(28),
         cost_estimate=pl.CostEstimate(
             flops=7 * ITERS * WIDE * 8192, bytes_accessed=WIDE * 8192 * 8, transcendentals=WIDE * 8192
         ),
         name="forward",
     )(meta, source_x, source_y, source_z, rows, lanes, mine, other)
-
-    arrive = arrive[0].reshape(4, 2, stations // 32)
-    own = lax.dynamic_index_in_dim(arrive, half, 1, keepdims=False)
-    partner = cycle(lax.dynamic_index_in_dim(arrive, 1 - half, 1, keepdims=False), "half", 2, 1)
 
     pieces = pl.pallas_call(
         adjoint_kernel,
@@ -359,7 +363,7 @@
             pltpu.VMEM((ADJ // 2 + 1, 2, 8, 8, NZ), jnp.float32),
             pltpu.VMEM((LAYERS, 8, 8, NZ), jnp.float32),
         ],
-        compiler_params=params,
+        compiler_params=params(28),
         cost_estimate=pl.CostEstimate(
             flops=12 * ITERS * ADJ * 8192, bytes_accessed=4 * ADJ * 8192 * 4, transcendentals=ADJ * 8192
         ),
@@ -371,11 +375,13 @@
         seen.reshape(ADJ // 2, 2, 8, 8, NZ),
     )
     pieces, own, partner = lax.optimization_barrier((pieces, own, partner))
+    partner = cycle(partner, "half", 2, 1)
     summed = jnp.sum(
         lax.all_to_all(pieces.reshape(16, 4, 8, NZ), ("zlo", "core", "half"), 0, 0, tiled=True), axis=0
     )
     kernel = lax.dynamic_slice(slowness, (0, group * 8, 0), (4, 8, NZ)) * summed
 
+    own, partner = own[0].reshape(4, stations // 32), partner[0].reshape(4, stations // 32)
     known = jnp.where(half == 0, jnp.stack([own, partner], 1), jnp.stack([partner, own], 1))
     arrivals = lax.dynamic_index_in_dim(known, x, 0, keepdims=False)
     for shift in (1, 2, 3):

time: 100 us -> 93.4 us (0.934)
  local copies, waits for them, and re-layouts: 6.49 us -> 3.96 us
  Pallas kernels: 36.6 us -> 34.6 us
  waiting for transfers between devices: 21.2 us -> 19.3 us
    unnamed x28 -> x24, local copies, waits for them, and re-layouts: 6.16 us -> 0.97 us
    ppermute x9, waiting for transfers between devices: 14.1 us -> 11.5 us  [cycle(): lax.ppermute(cells, axis, [(i, (i + shift) % size) for i in range(size)])]
    reshape x0 -> x3, local copies, waits for them, and re-layouts: none -> 2.33 us  [line_of(): values.reshape(4, 4, 2, stations // 32)]
    pallas_call x1, Pallas kernels: 17.7 us -> 15.4 us  [per_device(): pl.pallas_call(forward_kernel, out_shape=(f32(SEEN, 8, 8, NZ), f32(8, sta...]
  transfers between devices with their start and end apart: 12 -> 12, of which waited for: 9 -> 9; matrix products, arithmetic and copies ran while one was open for 1% -> 4% of each run, Pallas kernels for 18% -> 9%
where the time goes in v5:
time: 93.4 us; the launch traced here: 92.4 us
  Pallas kernels  34.6 us (37%)
  starting transfers between devices  31.5 us (34%)
  waiting for transfers between devices  19.3 us (21%)
  local copies, waits for them, and re-layouts  3.96 us (4%)
  other arithmetic  2.12 us (2%)
  between operations  0.99 us (1%)
    ppermute x9, starting transfers between devices, cycle(): lax.ppermute(cells, axis, [(i, (i + shift) % size) for i in range(size)])  21.1 us
    pallas_call x1, Pallas kernels, per_device(): pl.pallas_call(forward_kernel, out_shape=(f32(SEEN, 8, 8, NZ), f32(8, sta...  15.4 us
    ppermute x9, waiting for transfers between devices, cycle(): lax.ppermute(cells, axis, [(i, (i + shift) % size) for i in range(size)])  11.5 us
    pallas_call x1, Pallas kernels, per_device(): pl.pallas_call(adjoint_kernel, out_shape=f32(512, NZ), in_specs=[SMEM, VM...  10.1 us
    pallas_call x1, Pallas kernels, per_device(): pl.pallas_call(station_kernel, out_shape=(f32(ADJ * 64, NZ), f32(ADJ * 64...  8.41 us
    all_to_all x1, starting transfers between devices, per_device(): lax.all_to_all(pieces.reshape(16, 4, 8, NZ), ('zlo', 'core', 'half'), 0,...  4.54 us
    all_to_all x1, waiting for transfers between devices, per_device(): lax.all_to_all(pieces.reshape(16, 4, 8, NZ), ('zlo', 'core', 'half'), 0,...  4.39 us
    ppermute x1, starting transfers between devices, gathered(): before = lax.ppermute(block, 'x', [(0, 1), (1, 2), (2, 3)])  3.4 us
  transfers between devices with their start and end apart: 12, of which 9 were waited for; matrix products, arithmetic and copies ran while one was open for 4% of the time, Pallas kernels for 9%

profile of v5, /device:TPU:2, one launch (start us, length us, event | category | flops | bytes accessed | tf_op | source)
XLA Modules:
  0.0 92.4 jit_solution(815529404515764767)
XLA Ops:
  0.6 0.0 copy-start.6
  0.6 0.0 copy-start.5
  0.7 0.0 copy-start.7
  0.7 0.1 stack.51.meta
  0.8 0.9 copy-done.4
  1.7 0.7 prepare.1
  2.4 7.3 %collective-permute-start = (f32[4,4,8,128]{3,2,1,0:T(8,128)S(1)}, f32[4,4,8,128]{3,2,1,0:T(8,128)S(1)}, u32[]{:S(2)}, u32[]{:S(2)}) collective-permute-start(f32[4,4,8,128]{3,2,1,0:T(8,128)S(1)} %bitcast.63), channel_id=1, source_target_pairs={{0,1},{1,0},{2,3},{3,2},{4,5},{5,4},{6,7},{7,6},{8,9},{9,8},{10,11... | collective-permute-start | bytes 196616 | tf_op jit(solution)/shard_map/ppermute | solution.py:256
  9.7 0.8 reshape.116
  10.5 0.8 reshape.117
  11.3 0.8 reshape.115
  12.1 0.0 collective-permute-done
  12.1 1.7 %collective-permute-start.1 = (f32[8,4,8,128]{3,2,1,0:T(8,128)S(1)}, f32[8,4,8,128]{3,2,1,0:T(8,128)S(1)}, u32[]{:S(2)}, u32[]{:S(2)}) collective-permute-start(f32[8,4,8,128]{3,2,1,0:T(8,128)S(1)} %maximum_select_fusion.1), channel_id=1, source_target_pairs={{0,2},{2,4},{4,6},{6,0},{1,3},{3,5},{5,7},{7,1},{8,10},{10,12},{12... | collective-permute-start | bytes 393224 | tf_op jit(solution)/shard_map/ppermute | solution.py:256
  13.8 0.1 select_n.173
  13.9 0.1 select_n.170
  13.9 0.1 select_n.167
  14.0 1.7 %collective-permute-start.2 = (f32[8,4,8,128]{3,2,1,0:T(8,128)S(1)}, f32[8,4,8,128]{3,2,1,0:T(8,128)S(1)}, u32[]{:S(2)}, u32[]{:S(2)}) collective-permute-start(f32[8,4,8,128]{3,2,1,0:T(8,128)S(1)} %maximum_select_fusion.1), channel_id=1, source_target_pairs={{0,6},{2,0},{4,2},{6,4},{1,7},{3,1},{5,3},{7,5},{8,14},{10,8},{12,... | collective-permute-start | bytes 393224 | tf_op jit(solution)/shard_map/ppermute | solution.py:256
  15.7 2.0 %collective-permute-start.3 = (f32[8,4,8,128]{3,2,1,0:T(8,128)S(1)}, f32[8,4,8,128]{3,2,1,0:T(8,128)S(1)}, u32[]{:S(2)}, u32[]{:S(2)}) collective-permute-start(f32[8,4,8,128]{3,2,1,0:T(8,128)S(1)} %maximum_select_fusion.1), channel_id=1, source_target_pairs={{0,4},{2,6},{4,0},{6,2},{1,5},{3,7},{5,1},{7,3},{8,12},{10,14},{12... | collective-permute-start | bytes 393224 | tf_op jit(solution)/shard_map/ppermute | solution.py:256
  17.8 0.7 collective-permute-done.1
  18.4 1.6 %collective-permute-done.2 = f32[8,4,8,128]{3,2,1,0:T(8,128)S(1)} collective-permute-done((f32[8,4,8,128]{3,2,1,0:T(8,128)S(1)}, f32[8,4,8,128]{3,2,1,0:T(8,128)S(1)}, u32[]{:S(2)}, u32[]{:S(2)}) %collective-permute-start.2) | collective-permute-done | bytes 131104 | tf_op jit(solution)/shard_map/ppermute | solution.py:256
  20.1 2.3 %collective-permute-done.3 = f32[8,4,8,128]{3,2,1,0:T(8,128)S(1)} collective-permute-done((f32[8,4,8,128]{3,2,1,0:T(8,128)S(1)}, f32[8,4,8,128]{3,2,1,0:T(8,128)S(1)}, u32[]{:S(2)}, u32[]{:S(2)}) %collective-permute-start.3) | collective-permute-done | bytes 131104 | tf_op jit(solution)/shard_map/ppermute | solution.py:256
  22.4 3.4 %collective-permute-start.4 = (f32[32,4,8,128]{3,2,1,0:T(8,128)S(1)}, f32[32,4,8,128]{3,2,1,0:T(8,128)S(1)}, u32[]{:S(2)}, u32[]{:S(2)}) collective-permute-start(f32[32,4,8,128]{3,2,1,0:T(8,128)S(1)} %bitcast.70), channel_id=1, source_target_pairs={{0,8},{8,16},{16,24},{1,9},{9,17},{17,25},{2,10},{10,18},{18,26},{... | collective-permute-start | bytes 1572872 | tf_op jit(solution)/shard_map/ppermute | solution.py:269
  25.9 2.5 %collective-permute-start.5 = (f32[32,4,8,128]{3,2,1,0:T(8,128)S(1)}, f32[32,4,8,128]{3,2,1,0:T(8,128)S(1)}, u32[]{:S(2)}, u32[]{:S(2)}) collective-permute-start(f32[32,4,8,128]{3,2,1,0:T(8,128)S(1)} %bitcast.71), channel_id=1, source_target_pairs={{8,0},{16,8},{24,16},{9,1},{17,9},{25,17},{10,2},{18,10},{26,18},{... | collective-permute-start | bytes 1572872 | tf_op jit(solution)/shard_map/ppermute | solution.py:270
  28.4 0.0 copy-done.6
  28.4 0.0 copy-done.5
  28.4 0.0 copy-done.7
  28.4 8.4 %stations.1 = (f32[2560,128]{1,0:T(8,128)S(1)}, f32[2560,128]{1,0:T(8,128)S(1)}) custom-call(s32[6]{0:T(128)S(1)} %stack.51.meta, s32[1,2048]{1,0:T(1,128)S(1)} %bitcast.69, s32[1,2048]{1,0:T(1,128)S(1)} %bitcast.67, s32[1,2048]{1,0:T(1,128)S(1)} %bitcast.68, f32[2,2048]{1,0:T(2,128)S(1)} %copy-done.11), custom_call_target="tpu_custom_call" | custom-call | flops 5368709120 | bytes 2621440 | tf_op jit(solution)/shard_map/stations/pallas_call | solution.py:314
  36.8 0.2 collective-permute-done.4
  37.1 3.1 %collective-permute-done.5 = f32[32,4,8,128]{3,2,1,0:T(8,128)S(1)} collective-permute-done((f32[32,4,8,128]{3,2,1,0:T(8,128)S(1)}, f32[32,4,8,128]{3,2,1,0:T(8,128)S(1)}, u32[]{:S(2)}, u32[]{:S(2)}) %collective-permute-start.5) | collective-permute-done | bytes 524320 | tf_op jit(solution)/shard_map/ppermute | solution.py:270
  40.2 0.1 pad_maximum_fusion.mine
  40.4 0.3 collective-permute-start.6
  40.7 3.3 %collective-permute-done.6.other = f32[96,4,8,128]{3,2,1,0:T(8,128)S(1)} collective-permute-done((f32[96,4,8,128]{3,2,1,0:T(8,128)S(1)}, f32[96,4,8,128]{3,2,1,0:T(8,128)S(1)}, u32[]{:S(2)}, u32[]{:S(2)}) %collective-permute-start.6) | collective-permute-done | bytes 1572896 | tf_op jit(solution)/shard_map/ppermute | solution.py:256
  44.0 15.4 %forward.1 = (f32[48,8,8,128]{3,2,1,0:T(8,128)S(1)}, f32[8,256]{1,0:T(8,128)S(1)}, f32[8,256]{1,0:T(8,128)S(1)}) custom-call(s32[6]{0:T(128)S(1)} %stack.51.meta, s32[2]{0:T(128)S(1)} %copy-done.8, s32[2]{0:T(128)S(1)} %copy-done.9, s32[2]{0:T(128)S(1)} %copy-done.10, s32[512]{0:T(512)S(1)} %get-tuple-element.17.rows, s32[512]{0:T(512)S(1)} %get-tuple-element.18.lanes, ...), custom_call_target="tpu_custom_call" | custom-call | flops 73400320 | bytes 5242880 | tf_op jit(solution)/shard_map/forward/pallas_call | solution.py:336
  59.5 0.0 copy-done.3
  59.5 10.1 %adjoint.1 = f32[512,128]{1,0:T(8,128)} custom-call(s32[6]{0:T(128)S(1)} %stack.51.meta, f32[48,8,8,128]{3,2,1,0:T(8,128)S(1)} %get-tuple-element.24.times, f32[20,2,8,8,128]{4,3,2,1,0:T(8,128)S(1)} %bitcast.61, f32[20,2,8,8,128]{4,3,2,1,0:T(8,128)S(1)} %bitcast.62), custom_call_target="tpu_custom_call" | custom-call | flops 62914560 | bytes 5242880 | tf_op jit(solution)/shard_map/adjoint/pallas_call | solution.py:355
  69.6 4.5 %collective-permute-start.7 = (f32[8,256]{1,0:T(8,128)S(1)}, f32[8,256]{1,0:T(8,128)S(1)}, u32[]{:S(2)}, u32[]{:S(2)}) collective-permute-start(f32[8,256]{1,0:T(8,128)S(1)} %get-tuple-element.31), channel_id=1, source_target_pairs={{0,1},{1,0},{2,3},{3,2},{4,5},{5,4},{6,7},{7,6},{8,9},{9,8},{10,11... | collective-permute-start | bytes 24584 | tf_op jit(solution)/shard_map/ppermute | solution.py:256
  74.2 0.1 stack_reshape_squeeze.8
  74.2 4.5 %all-to-all-start = ((f32[16,4,8,128]{3,2,1,0:T(8,128)}), f32[16,4,8,128]{3,2,1,0:T(8,128)S(1)}, u32[]{:S(2)}, u32[]{:S(2)}) async-start(f32[16,4,8,128]{3,2,1,0:T(8,128)} %bitcast.28), calls=%async_computation | async-start | bytes 524288 | tf_op jit(solution)/shard_map/all_to_all | solution.py:380
  78.8 0.0 collective-permute-done.7
  78.8 0.1 stack_reshape_squeeze.9
  78.9 0.6 collective-permute-start.10
  79.6 1.5 %collective-permute-start.8 = (f32[2,64]{1,0:T(2,128)S(1)}, f32[2,64]{1,0:T(2,128)S(1)}, u32[]{:S(2)}, u32[]{:S(2)}) collective-permute-start(f32[2,64]{1,0:T(2,128)S(1)} %get-tuple-element.32), channel_id=1, source_target_pairs={{0,8},{8,16},{16,24},{24,0},{1,9},{9,17},{17,25},{25,1},{2,10},{10... | collective-permute-start | bytes 1544 | tf_op jit(solution)/shard_map/ppermute | solution.py:256
  81.1 1.6 %collective-permute-start.9 = (f32[2,64]{1,0:T(2,128)S(1)}, f32[2,64]{1,0:T(2,128)S(1)}, u32[]{:S(2)}, u32[]{:S(2)}) collective-permute-start(f32[2,64]{1,0:T(2,128)S(1)} %get-tuple-element.34), channel_id=1, source_target_pairs={{0,16},{8,24},{16,0},{24,8},{1,17},{9,25},{17,1},{25,9},{2,18},{10... | collective-permute-start | bytes 1544 | tf_op jit(solution)/shard_map/ppermute | solution.py:256
  82.6 0.0 collective-permute-done.10
  82.6 0.5 collective-permute-done.8
  83.2 3.0 %collective-permute-done.9 = f32[2,64]{1,0:T(2,128)S(1)} collective-permute-done((f32[2,64]{1,0:T(2,128)S(1)}, f32[2,64]{1,0:T(2,128)S(1)}, u32[]{:S(2)}, u32[]{:S(2)}) %collective-permute-start.9) | collective-permute-done | bytes 544 | tf_op jit(solution)/shard_map/ppermute | solution.py:256
  86.1 0.6 fusion.19
  86.7 4.4 %all-to-all-done = f32[16,4,8,128]{3,2,1,0:T(8,128)S(1)} async-done(((f32[16,4,8,128]{3,2,1,0:T(8,128)}), f32[16,4,8,128]{3,2,1,0:T(8,128)S(1)}, u32[]{:S(2)}, u32[]{:S(2)}) %all-to-all-start) | async-done | bytes 262176 | tf_op jit(solution)/shard_map/all_to_all | solution.py:380
  91.1 1.3 %dynamic-slice_multiply_fusion = f32[4,8,128]{2,1,0:T(8,128)} fusion(f32[4,8,128]{2,1,0:T(8,128)S(1)} %reduce_sum.9, f32[4,64,128]{2,1,0:T(8,128)} %param.8, s32[]{:T(128)S(6)} %select_n.162), kind=kLoop, calls=%fused_computation.7 | loop fusion | flops 4096 | bytes 49156 | tf_op jit(solution)/shard_map/mul | solution.py:382
  (36 shorter events, 0.3 us)
Async XLA Ops:
  0.6 27.7 %copy-start.6 = (s32[2048]{0:T(1024)S(1)}, s32[2048]{0:T(1024)}, u32[]{:S(2)}) copy-start(s32[2048]{0:T(1024)} %param.14) | copy-start | bytes 24580
  0.6 27.7 %copy-start.5 = (s32[2048]{0:T(1024)S(1)}, s32[2048]{0:T(1024)}, u32[]{:S(2)}) copy-start(s32[2048]{0:T(1024)} %param.13) | copy-start | bytes 24580
  0.7 27.7 %copy-start.7 = (s32[2048]{0:T(1024)S(1)}, s32[2048]{0:T(1024)}, u32[]{:S(2)}) copy-start(s32[2048]{0:T(1024)} %param.12) | copy-start | bytes 24580
  0.7 27.7 %copy-start.11 = (f32[2,2048]{1,0:T(2,128)S(1)}, f32[2,2048]{1,0:T(2,128)}, u32[]{:S(2)}) copy-start(f32[2,2048]{1,0:T(2,128)} %obs.1) | copy-start | bytes 49156
  0.8 0.9 copy-start.4
  2.4 9.7 %collective-permute-start = (f32[4,4,8,128]{3,2,1,0:T(8,128)S(1)}, f32[4,4,8,128]{3,2,1,0:T(8,128)S(1)}, u32[]{:S(2)}, u32[]{:S(2)}) collective-permute-start(f32[4,4,8,128]{3,2,1,0:T(8,128)S(1)} %bitcast.63), channel_id=1, source_target_pairs={{0,1},{1,0},{2,3},{3,2},{4,5},{5,4},{6,7},{7,6},{8,9},{9,8},{10,11... | collective-permute-start | bytes 196616 | tf_op jit(solution)/shard_map/ppermute | solution.py:256
  12.1 6.3 %collective-permute-start.1 = (f32[8,4,8,128]{3,2,1,0:T(8,128)S(1)}, f32[8,4,8,128]{3,2,1,0:T(8,128)S(1)}, u32[]{:S(2)}, u32[]{:S(2)}) collective-permute-start(f32[8,4,8,128]{3,2,1,0:T(8,128)S(1)} %maximum_select_fusion.1), channel_id=1, source_target_pairs={{0,2},{2,4},{4,6},{6,0},{1,3},{3,5},{5,7},{7,1},{8,10},{10,12},{12... | collective-permute-start | bytes 393224 | tf_op jit(solution)/shard_map/ppermute | solution.py:256
  14.0 6.1 %collective-permute-start.2 = (f32[8,4,8,128]{3,2,1,0:T(8,128)S(1)}, f32[8,4,8,128]{3,2,1,0:T(8,128)S(1)}, u32[]{:S(2)}, u32[]{:S(2)}) collective-permute-start(f32[8,4,8,128]{3,2,1,0:T(8,128)S(1)} %maximum_select_fusion.1), channel_id=1, source_target_pairs={{0,6},{2,0},{4,2},{6,4},{1,7},{3,1},{5,3},{7,5},{8,14},{10,8},{12,... | collective-permute-start | bytes 393224 | tf_op jit(solution)/shard_map/ppermute | solution.py:256
  15.7 6.7 %collective-permute-start.3 = (f32[8,4,8,128]{3,2,1,0:T(8,128)S(1)}, f32[8,4,8,128]{3,2,1,0:T(8,128)S(1)}, u32[]{:S(2)}, u32[]{:S(2)}) collective-permute-start(f32[8,4,8,128]{3,2,1,0:T(8,128)S(1)} %maximum_select_fusion.1), channel_id=1, source_target_pairs={{0,4},{2,6},{4,0},{6,2},{1,5},{3,7},{5,1},{7,3},{8,12},{10,14},{12... | collective-permute-start | bytes 393224 | tf_op jit(solution)/shard_map/ppermute | solution.py:256
  22.4 14.6 %collective-permute-start.4 = (f32[32,4,8,128]{3,2,1,0:T(8,128)S(1)}, f32[32,4,8,128]{3,2,1,0:T(8,128)S(1)}, u32[]{:S(2)}, u32[]{:S(2)}) collective-permute-start(f32[32,4,8,128]{3,2,1,0:T(8,128)S(1)} %bitcast.70), channel_id=1, source_target_pairs={{0,8},{8,16},{16,24},{1,9},{9,17},{17,25},{2,10},{10,18},{18,26},{... | collective-permute-start | bytes 1572872 | tf_op jit(solution)/shard_map/ppermute | solution.py:269
  25.9 14.4 %collective-permute-start.5 = (f32[32,4,8,128]{3,2,1,0:T(8,128)S(1)}, f32[32,4,8,128]{3,2,1,0:T(8,128)S(1)}, u32[]{:S(2)}, u32[]{:S(2)}) collective-permute-start(f32[32,4,8,128]{3,2,1,0:T(8,128)S(1)} %bitcast.71), channel_id=1, source_target_pairs={{8,0},{16,8},{24,16},{9,1},{17,9},{25,17},{10,2},{18,10},{26,18},{... | collective-permute-start | bytes 1572872 | tf_op jit(solution)/shard_map/ppermute | solution.py:270
  36.8 3.5 %copy-start = (f32[2560,128]{1,0:T(8,128)}, f32[2560,128]{1,0:T(8,128)S(1)}, u32[]{:S(2)}) copy-start(f32[2560,128]{1,0:T(8,128)S(1)} %get-tuple-element.25) | copy-start | bytes 3932164
  36.8 3.5 %copy-start.2 = (f32[2560,128]{1,0:T(8,128)}, f32[2560,128]{1,0:T(8,128)S(1)}, u32[]{:S(2)}) copy-start(f32[2560,128]{1,0:T(8,128)S(1)} %get-tuple-element.26) | copy-start | bytes 3932164
  40.2 3.8 %copy-start.8 = (s32[2]{0:T(128)S(1)}, s32[2]{0:T(128)}, u32[]{:S(2)}) copy-start(s32[2]{0:T(128)} %src_x.1) | copy-start | bytes 28
  40.2 3.8 %copy-start.9 = (s32[2]{0:T(128)S(1)}, s32[2]{0:T(128)}, u32[]{:S(2)}) copy-start(s32[2]{0:T(128)} %src_y.1) | copy-start | bytes 28
  40.2 3.8 %copy-start.10 = (s32[2]{0:T(128)S(1)}, s32[2]{0:T(128)}, u32[]{:S(2)}) copy-start(s32[2]{0:T(128)} %src_z.1) | copy-start | bytes 28
  40.4 3.7 %collective-permute-start.6 = (f32[96,4,8,128]{3,2,1,0:T(8,128)S(1)}, f32[96,4,8,128]{3,2,1,0:T(8,128)S(1)}, u32[]{:S(2)}, u32[]{:S(2)}) collective-permute-start(f32[96,4,8,128]{3,2,1,0:T(8,128)S(1)} %pad_maximum_fusion.mine), channel_id=1, source_target_pairs={{0,32},{32,0},{1,33},{33,1},{2,34},{34,2},{3,35},{35,3},{4,36},{36... | collective-permute-start | bytes 4718600 | tf_op jit(solution)/shard_map/ppermute | solution.py:256
  40.7 18.8 %copy-start.1 = (f32[2560,128]{1,0:T(8,128)S(1)}, f32[2560,128]{1,0:T(8,128)}, u32[]{:S(2)}) copy-start(f32[2560,128]{1,0:T(8,128)} %copy-done) | copy-start | bytes 3932164
  40.7 18.8 %copy-start.3 = (f32[2560,128]{1,0:T(8,128)S(1)}, f32[2560,128]{1,0:T(8,128)}, u32[]{:S(2)}) copy-start(f32[2560,128]{1,0:T(8,128)} %copy-done.2) | copy-start | bytes 3932164
  69.6 9.2 %collective-permute-start.7 = (f32[8,256]{1,0:T(8,128)S(1)}, f32[8,256]{1,0:T(8,128)S(1)}, u32[]{:S(2)}, u32[]{:S(2)}) collective-permute-start(f32[8,256]{1,0:T(8,128)S(1)} %get-tuple-element.31), channel_id=1, source_target_pairs={{0,1},{1,0},{2,3},{3,2},{4,5},{5,4},{6,7},{7,6},{8,9},{9,8},{10,11... | collective-permute-start | bytes 24584 | tf_op jit(solution)/shard_map/ppermute | solution.py:256
  74.2 16.8 %all-to-all-start = ((f32[16,4,8,128]{3,2,1,0:T(8,128)}), f32[16,4,8,128]{3,2,1,0:T(8,128)S(1)}, u32[]{:S(2)}, u32[]{:S(2)}) async-start(f32[16,4,8,128]{3,2,1,0:T(8,128)} %bitcast.28), calls=%async_computation | async-start | bytes 524288 | tf_op jit(solution)/shard_map/all_to_all | solution.py:380
  78.9 3.7 %collective-permute-start.10 = (f32[2,64]{1,0:T(2,128)S(1)}, f32[2,64]{1,0:T(2,128)S(1)}, u32[]{:S(2)}, u32[]{:S(2)}) collective-permute-start(f32[2,64]{1,0:T(2,128)S(1)} %get-tuple-element.33), channel_id=1, source_target_pairs={{0,24},{8,0},{16,8},{24,16},{1,25},{9,1},{17,9},{25,17},{2,26},{10... | collective-permute-start | bytes 1544 | tf_op jit(solution)/shard_map/ppermute | solution.py:256
  79.6 3.6 %collective-permute-start.8 = (f32[2,64]{1,0:T(2,128)S(1)}, f32[2,64]{1,0:T(2,128)S(1)}, u32[]{:S(2)}, u32[]{:S(2)}) collective-permute-start(f32[2,64]{1,0:T(2,128)S(1)} %get-tuple-element.32), channel_id=1, source_target_pairs={{0,8},{8,16},{16,24},{24,0},{1,9},{9,17},{17,25},{25,1},{2,10},{10... | collective-permute-start | bytes 1544 | tf_op jit(solution)/shard_map/ppermute | solution.py:256
  81.1 5.1 %collective-permute-start.9 = (f32[2,64]{1,0:T(2,128)S(1)}, f32[2,64]{1,0:T(2,128)S(1)}, u32[]{:S(2)}, u32[]{:S(2)}) collective-permute-start(f32[2,64]{1,0:T(2,128)S(1)} %get-tuple-element.34), channel_id=1, source_target_pairs={{0,16},{8,24},{16,0},{24,8},{1,17},{9,25},{17,1},{25,9},{2,18},{10... | collective-permute-start | bytes 1544 | tf_op jit(solution)/shard_map/ppermute | solution.py:256

commit v6 on v5

--- a/solution.py
+++ b/solution.py
@@ -332,7 +332,10 @@
         compiler_params=params(28),
         name="prepare",
     )(meta, slowness.reshape(-1, NZ))
-    mine, other, (count, seen) = gathered(part.reshape(4, 4, 8, NZ), y, half, (count, seen))
+    piece_slow = lax.dynamic_slice(slowness, (0, group * 8, 0), (4, 8, NZ))
+    mine, other, (count, seen, piece_slow) = gathered(
+        part.reshape(4, 4, 8, NZ), y, half, (count, seen, piece_slow)
+    )
     times, own, partner = pl.pallas_call(
         forward_kernel,
         out_shape=(f32(SEEN, 8, 8, NZ), f32(8, stations // 8), f32(8, stations // 8)),
@@ -379,7 +382,7 @@
     summed = jnp.sum(
         lax.all_to_all(pieces.reshape(16, 4, 8, NZ), ("zlo", "core", "half"), 0, 0, tiled=True), axis=0
     )
-    kernel = lax.dynamic_slice(slowness, (0, group * 8, 0), (4, 8, NZ)) * summed
+    kernel = piece_slow * summed
 
     own, partner = own[0].reshape(4, stations // 32), partner[0].reshape(4, stations // 32)
     known = jnp.where(half == 0, jnp.stack([own, partner], 1), jnp.stack([partner, own], 1))

time: 93.4 us -> 92.6 us (level)
  waiting for transfers between devices: 19.3 us -> 18 us
  transfers between devices with their start and end apart: 12 -> 12, of which waited for: 9 -> 7; matrix products, arithmetic and copies ran while one was open for 4% -> 5% of each run, Pallas kernels for 9% -> 9%
where the time goes in v6:
time: 92.6 us; the launch traced here: 91.6 us
  Pallas kernels  34.6 us (37%)
  starting transfers between devices  31.9 us (34%)
  waiting for transfers between devices  18 us (19%)
  local copies, waits for them, and re-layouts  4.68 us (5%)
  other arithmetic  1.4 us (2%)
  between operations  1.03 us (1%)
    ppermute x9, starting transfers between devices, cycle(): lax.ppermute(cells, axis, [(i, (i + shift) % size) for i in range(size)])  21.4 us
    pallas_call x1, Pallas kernels, per_device(): pl.pallas_call(forward_kernel, out_shape=(f32(SEEN, 8, 8, NZ), f32(8, sta...  15.4 us
    ppermute x9, waiting for transfers between devices, cycle(): lax.ppermute(cells, axis, [(i, (i + shift) % size) for i in range(size)])  10.9 us
    pallas_call x1, Pallas kernels, per_device(): pl.pallas_call(adjoint_kernel, out_shape=f32(512, NZ), in_specs=[SMEM, VM...  10.1 us
    pallas_call x1, Pallas kernels, per_device(): pl.pallas_call(station_kernel, out_shape=(f32(ADJ * 64, NZ), f32(ADJ * 64...  8.41 us
    all_to_all x1, starting transfers between devices, per_device(): lax.all_to_all(pieces.reshape(16, 4, 8, NZ), ('zlo', 'core', 'half'), 0,...  4.6 us
    all_to_all x1, waiting for transfers between devices, per_device(): lax.all_to_all(pieces.reshape(16, 4, 8, NZ), ('zlo', 'core', 'half'), 0,...  4.39 us
    ppermute x1, starting transfers between devices, gathered(): before = lax.ppermute(block, 'x', [(0, 1), (1, 2), (2, 3)])  3.4 us
  transfers between devices with their start and end apart: 12, of which 7 were waited for; matrix products, arithmetic and copies ran while one was open for 5% of the time, Pallas kernels for 9%

profile of v6, /device:TPU:2, one launch (start us, length us, event | category | flops | bytes accessed | tf_op | source)
XLA Modules:
  0.0 91.6 jit_solution(4452773353656848849)
XLA Ops:
  0.6 0.0 copy-start.6
  0.6 0.0 copy-start.5
  0.7 0.0 copy-start.7
  0.7 0.1 stack.51.meta
  0.8 0.9 copy-done.4
  1.7 0.7 prepare.1
  2.4 7.3 %collective-permute-start = (f32[4,4,8,128]{3,2,1,0:T(8,128)S(1)}, f32[4,4,8,128]{3,2,1,0:T(8,128)S(1)}, u32[]{:S(2)}, u32[]{:S(2)}) collective-permute-start(f32[4,4,8,128]{3,2,1,0:T(8,128)S(1)} %bitcast.63), channel_id=1, source_target_pairs={{0,1},{1,0},{2,3},{3,2},{4,5},{5,4},{6,7},{7,6},{8,9},{9,8},{10,11... | collective-permute-start | bytes 196616 | tf_op jit(solution)/shard_map/ppermute | solution.py:256
  9.7 0.8 reshape.119
  10.5 0.8 reshape.120
  11.3 0.1 select_n.179
  11.4 0.1 select_n.182
  11.4 0.8 reshape.118
  12.2 0.1 select_n.176
  12.3 0.0 collective-permute-done
  12.3 1.7 %collective-permute-start.1 = (f32[8,4,8,128]{3,2,1,0:T(8,128)S(1)}, f32[8,4,8,128]{3,2,1,0:T(8,128)S(1)}, u32[]{:S(2)}, u32[]{:S(2)}) collective-permute-start(f32[8,4,8,128]{3,2,1,0:T(8,128)S(1)} %maximum_select_fusion.1), channel_id=1, source_target_pairs={{0,2},{2,4},{4,6},{6,0},{1,3},{3,5},{5,7},{7,1},{8,10},{10,12},{12... | collective-permute-start | bytes 393224 | tf_op jit(solution)/shard_map/ppermute | solution.py:256
  14.1 1.7 %collective-permute-start.2 = (f32[8,4,8,128]{3,2,1,0:T(8,128)S(1)}, f32[8,4,8,128]{3,2,1,0:T(8,128)S(1)}, u32[]{:S(2)}, u32[]{:S(2)}) collective-permute-start(f32[8,4,8,128]{3,2,1,0:T(8,128)S(1)} %maximum_select_fusion.1), channel_id=1, source_target_pairs={{0,6},{2,0},{4,2},{6,4},{1,7},{3,1},{5,3},{7,5},{8,14},{10,8},{12,... | collective-permute-start | bytes 393224 | tf_op jit(solution)/shard_map/ppermute | solution.py:256
  15.8 2.0 %collective-permute-start.3 = (f32[8,4,8,128]{3,2,1,0:T(8,128)S(1)}, f32[8,4,8,128]{3,2,1,0:T(8,128)S(1)}, u32[]{:S(2)}, u32[]{:S(2)}) collective-permute-start(f32[8,4,8,128]{3,2,1,0:T(8,128)S(1)} %maximum_select_fusion.1), channel_id=1, source_target_pairs={{0,4},{2,6},{4,0},{6,2},{1,5},{3,7},{5,1},{7,3},{8,12},{10,14},{12... | collective-permute-start | bytes 393224 | tf_op jit(solution)/shard_map/ppermute | solution.py:256
  17.9 0.8 collective-permute-done.1
  18.7 1.5 %collective-permute-done.2 = f32[8,4,8,128]{3,2,1,0:T(8,128)S(1)} collective-permute-done((f32[8,4,8,128]{3,2,1,0:T(8,128)S(1)}, f32[8,4,8,128]{3,2,1,0:T(8,128)S(1)}, u32[]{:S(2)}, u32[]{:S(2)}) %collective-permute-start.2) | collective-permute-done | bytes 131104 | tf_op jit(solution)/shard_map/ppermute | solution.py:256
  20.2 2.4 %collective-permute-done.3 = f32[8,4,8,128]{3,2,1,0:T(8,128)S(1)} collective-permute-done((f32[8,4,8,128]{3,2,1,0:T(8,128)S(1)}, f32[8,4,8,128]{3,2,1,0:T(8,128)S(1)}, u32[]{:S(2)}, u32[]{:S(2)}) %collective-permute-start.3) | collective-permute-done | bytes 131104 | tf_op jit(solution)/shard_map/ppermute | solution.py:256
  22.7 3.4 %collective-permute-start.4 = (f32[32,4,8,128]{3,2,1,0:T(8,128)S(1)}, f32[32,4,8,128]{3,2,1,0:T(8,128)S(1)}, u32[]{:S(2)}, u32[]{:S(2)}) collective-permute-start(f32[32,4,8,128]{3,2,1,0:T(8,128)S(1)} %bitcast.70), channel_id=1, source_target_pairs={{0,8},{8,16},{16,24},{1,9},{9,17},{17,25},{2,10},{10,18},{18,26},{... | collective-permute-start | bytes 1572872 | tf_op jit(solution)/shard_map/ppermute | solution.py:269
  26.1 2.5 %collective-permute-start.5 = (f32[32,4,8,128]{3,2,1,0:T(8,128)S(1)}, f32[32,4,8,128]{3,2,1,0:T(8,128)S(1)}, u32[]{:S(2)}, u32[]{:S(2)}) collective-permute-start(f32[32,4,8,128]{3,2,1,0:T(8,128)S(1)} %bitcast.71), channel_id=1, source_target_pairs={{8,0},{16,8},{24,16},{9,1},{17,9},{25,17},{10,2},{18,10},{26,18},{... | collective-permute-start | bytes 1572872 | tf_op jit(solution)/shard_map/ppermute | solution.py:270
  28.6 0.7 constant_dynamic-slice_fusion.4
  29.3 0.0 copy-done.6
  29.3 8.4 %stations.1 = (f32[2560,128]{1,0:T(8,128)S(1)}, f32[2560,128]{1,0:T(8,128)S(1)}) custom-call(s32[6]{0:T(128)S(1)} %stack.51.meta, s32[1,2048]{1,0:T(1,128)S(1)} %bitcast.69, s32[1,2048]{1,0:T(1,128)S(1)} %bitcast.67, s32[1,2048]{1,0:T(1,128)S(1)} %bitcast.68, f32[2,2048]{1,0:T(2,128)S(1)} %copy-done.11), custom_call_target="tpu_custom_call" | custom-call | flops 5368709120 | bytes 2621440 | tf_op jit(solution)/shard_map/stations/pallas_call | solution.py:314
  37.7 0.0 collective-permute-done.4
  37.8 2.8 %collective-permute-done.5 = f32[32,4,8,128]{3,2,1,0:T(8,128)S(1)} collective-permute-done((f32[32,4,8,128]{3,2,1,0:T(8,128)S(1)}, f32[32,4,8,128]{3,2,1,0:T(8,128)S(1)}, u32[]{:S(2)}, u32[]{:S(2)}) %collective-permute-start.5) | collective-permute-done | bytes 524320 | tf_op jit(solution)/shard_map/ppermute | solution.py:270
  40.5 0.1 pad_maximum_fusion.mine
  40.7 0.3 collective-permute-start.6
  41.0 3.3 %collective-permute-done.6.other = f32[96,4,8,128]{3,2,1,0:T(8,128)S(1)} collective-permute-done((f32[96,4,8,128]{3,2,1,0:T(8,128)S(1)}, f32[96,4,8,128]{3,2,1,0:T(8,128)S(1)}, u32[]{:S(2)}, u32[]{:S(2)}) %collective-permute-start.6) | collective-permute-done | bytes 1572896 | tf_op jit(solution)/shard_map/ppermute | solution.py:256
  44.4 15.4 %forward.1 = (f32[48,8,8,128]{3,2,1,0:T(8,128)S(1)}, f32[8,256]{1,0:T(8,128)S(1)}, f32[8,256]{1,0:T(8,128)S(1)}) custom-call(s32[6]{0:T(128)S(1)} %stack.51.meta, s32[2]{0:T(128)S(1)} %copy-done.8, s32[2]{0:T(128)S(1)} %copy-done.9, s32[2]{0:T(128)S(1)} %copy-done.10, s32[512]{0:T(512)S(1)} %get-tuple-element.22.rows, s32[512]{0:T(512)S(1)} %get-tuple-element.23.lanes, ...), custom_call_target="tpu_custom_call" | custom-call | flops 73400320 | bytes 5242880 | tf_op jit(solution)/shard_map/forward/pallas_call | solution.py:339
  59.8 0.0 copy-done.1
  59.8 0.0 copy-done.3
  59.8 10.1 %adjoint.1 = f32[512,128]{1,0:T(8,128)} custom-call(s32[6]{0:T(128)S(1)} %stack.51.meta, f32[48,8,8,128]{3,2,1,0:T(8,128)S(1)} %get-tuple-element.26.times, f32[20,2,8,8,128]{4,3,2,1,0:T(8,128)S(1)} %bitcast.61, f32[20,2,8,8,128]{4,3,2,1,0:T(8,128)S(1)} %bitcast.62), custom_call_target="tpu_custom_call" | custom-call | flops 62914560 | bytes 5242880 | tf_op jit(solution)/shard_map/adjoint/pallas_call | solution.py:358
  69.9 4.1 %collective-permute-start.7 = (f32[8,256]{1,0:T(8,128)S(1)}, f32[8,256]{1,0:T(8,128)S(1)}, u32[]{:S(2)}, u32[]{:S(2)}) collective-permute-start(f32[8,256]{1,0:T(8,128)S(1)} %get-tuple-element.33), channel_id=1, source_target_pairs={{0,1},{1,0},{2,3},{3,2},{4,5},{5,4},{6,7},{7,6},{8,9},{9,8},{10,11... | collective-permute-start | bytes 24584 | tf_op jit(solution)/shard_map/ppermute | solution.py:256
  74.0 0.1 stack_reshape_squeeze.8
  74.1 4.6 %all-to-all-start = ((f32[16,4,8,128]{3,2,1,0:T(8,128)}), f32[16,4,8,128]{3,2,1,0:T(8,128)S(1)}, u32[]{:S(2)}, u32[]{:S(2)}) async-start(f32[16,4,8,128]{3,2,1,0:T(8,128)} %bitcast.28), calls=%async_computation | async-start | bytes 524288 | tf_op jit(solution)/shard_map/all_to_all | solution.py:383
  78.7 0.0 collective-permute-done.7
  78.7 0.1 stack_reshape_squeeze.9
  78.9 0.6 collective-permute-start.10
  79.5 1.5 %collective-permute-start.8 = (f32[2,64]{1,0:T(2,128)S(1)}, f32[2,64]{1,0:T(2,128)S(1)}, u32[]{:S(2)}, u32[]{:S(2)}) collective-permute-start(f32[2,64]{1,0:T(2,128)S(1)} %get-tuple-element.34), channel_id=1, source_target_pairs={{0,8},{8,16},{16,24},{24,0},{1,9},{9,17},{17,25},{25,1},{2,10},{10... | collective-permute-start | bytes 1544 | tf_op jit(solution)/shard_map/ppermute | solution.py:256
  81.0 2.3 %collective-permute-start.9 = (f32[2,64]{1,0:T(2,128)S(1)}, f32[2,64]{1,0:T(2,128)S(1)}, u32[]{:S(2)}, u32[]{:S(2)}) collective-permute-start(f32[2,64]{1,0:T(2,128)S(1)} %get-tuple-element.36), channel_id=1, source_target_pairs={{0,16},{8,24},{16,0},{24,8},{1,17},{9,25},{17,1},{25,9},{2,18},{10... | collective-permute-start | bytes 1544 | tf_op jit(solution)/shard_map/ppermute | solution.py:256
  83.2 0.0 collective-permute-done.10
  83.2 0.0 collective-permute-done.8
  83.2 2.8 %collective-permute-done.9 = f32[2,64]{1,0:T(2,128)S(1)} collective-permute-done((f32[2,64]{1,0:T(2,128)S(1)}, f32[2,64]{1,0:T(2,128)S(1)}, u32[]{:S(2)}, u32[]{:S(2)}) %collective-permute-start.9) | collective-permute-done | bytes 544 | tf_op jit(solution)/shard_map/ppermute | solution.py:256
  86.0 0.6 fusion.19
  86.6 4.4 %all-to-all-done = f32[16,4,8,128]{3,2,1,0:T(8,128)S(1)} async-done(((f32[16,4,8,128]{3,2,1,0:T(8,128)}), f32[16,4,8,128]{3,2,1,0:T(8,128)S(1)}, u32[]{:S(2)}, u32[]{:S(2)}) %all-to-all-start) | async-done | bytes 262176 | tf_op jit(solution)/shard_map/all_to_all | solution.py:383
  91.0 0.6 mul.48
  (37 shorter events, 0.3 us)
Async XLA Ops:
  0.6 28.7 %copy-start.6 = (s32[2048]{0:T(1024)S(1)}, s32[2048]{0:T(1024)}, u32[]{:S(2)}) copy-start(s32[2048]{0:T(1024)} %param.14) | copy-start | bytes 24580
  0.6 28.6 %copy-start.5 = (s32[2048]{0:T(1024)S(1)}, s32[2048]{0:T(1024)}, u32[]{:S(2)}) copy-start(s32[2048]{0:T(1024)} %param.13) | copy-start | bytes 24580
  0.7 28.6 %copy-start.7 = (s32[2048]{0:T(1024)S(1)}, s32[2048]{0:T(1024)}, u32[]{:S(2)}) copy-start(s32[2048]{0:T(1024)} %param.12) | copy-start | bytes 24580
  0.7 28.6 %copy-start.11 = (f32[2,2048]{1,0:T(2,128)S(1)}, f32[2,2048]{1,0:T(2,128)}, u32[]{:S(2)}) copy-start(f32[2,2048]{1,0:T(2,128)} %obs.1) | copy-start | bytes 49156
  0.8 0.9 copy-start.4
  2.4 9.9 %collective-permute-start = (f32[4,4,8,128]{3,2,1,0:T(8,128)S(1)}, f32[4,4,8,128]{3,2,1,0:T(8,128)S(1)}, u32[]{:S(2)}, u32[]{:S(2)}) collective-permute-start(f32[4,4,8,128]{3,2,1,0:T(8,128)S(1)} %bitcast.63), channel_id=1, source_target_pairs={{0,1},{1,0},{2,3},{3,2},{4,5},{5,4},{6,7},{7,6},{8,9},{9,8},{10,11... | collective-permute-start | bytes 196616 | tf_op jit(solution)/shard_map/ppermute | solution.py:256
  12.3 6.3 %collective-permute-start.1 = (f32[8,4,8,128]{3,2,1,0:T(8,128)S(1)}, f32[8,4,8,128]{3,2,1,0:T(8,128)S(1)}, u32[]{:S(2)}, u32[]{:S(2)}) collective-permute-start(f32[8,4,8,128]{3,2,1,0:T(8,128)S(1)} %maximum_select_fusion.1), channel_id=1, source_target_pairs={{0,2},{2,4},{4,6},{6,0},{1,3},{3,5},{5,7},{7,1},{8,10},{10,12},{12... | collective-permute-start | bytes 393224 | tf_op jit(solution)/shard_map/ppermute | solution.py:256
  14.1 6.1 %collective-permute-start.2 = (f32[8,4,8,128]{3,2,1,0:T(8,128)S(1)}, f32[8,4,8,128]{3,2,1,0:T(8,128)S(1)}, u32[]{:S(2)}, u32[]{:S(2)}) collective-permute-start(f32[8,4,8,128]{3,2,1,0:T(8,128)S(1)} %maximum_select_fusion.1), channel_id=1, source_target_pairs={{0,6},{2,0},{4,2},{6,4},{1,7},{3,1},{5,3},{7,5},{8,14},{10,8},{12,... | collective-permute-start | bytes 393224 | tf_op jit(solution)/shard_map/ppermute | solution.py:256
  15.8 6.8 %collective-permute-start.3 = (f32[8,4,8,128]{3,2,1,0:T(8,128)S(1)}, f32[8,4,8,128]{3,2,1,0:T(8,128)S(1)}, u32[]{:S(2)}, u32[]{:S(2)}) collective-permute-start(f32[8,4,8,128]{3,2,1,0:T(8,128)S(1)} %maximum_select_fusion.1), channel_id=1, source_target_pairs={{0,4},{2,6},{4,0},{6,2},{1,5},{3,7},{5,1},{7,3},{8,12},{10,14},{12... | collective-permute-start | bytes 393224 | tf_op jit(solution)/shard_map/ppermute | solution.py:256
  22.7 15.1 %collective-permute-start.4 = (f32[32,4,8,128]{3,2,1,0:T(8,128)S(1)}, f32[32,4,8,128]{3,2,1,0:T(8,128)S(1)}, u32[]{:S(2)}, u32[]{:S(2)}) collective-permute-start(f32[32,4,8,128]{3,2,1,0:T(8,128)S(1)} %bitcast.70), channel_id=1, source_target_pairs={{0,8},{8,16},{16,24},{1,9},{9,17},{17,25},{2,10},{10,18},{18,26},{... | collective-permute-start | bytes 1572872 | tf_op jit(solution)/shard_map/ppermute | solution.py:269
  26.1 14.4 %collective-permute-start.5 = (f32[32,4,8,128]{3,2,1,0:T(8,128)S(1)}, f32[32,4,8,128]{3,2,1,0:T(8,128)S(1)}, u32[]{:S(2)}, u32[]{:S(2)}) collective-permute-start(f32[32,4,8,128]{3,2,1,0:T(8,128)S(1)} %bitcast.71), channel_id=1, source_target_pairs={{8,0},{16,8},{24,16},{9,1},{17,9},{25,17},{10,2},{18,10},{26,18},{... | collective-permute-start | bytes 1572872 | tf_op jit(solution)/shard_map/ppermute | solution.py:270
  37.7 2.9 %copy-start = (f32[2560,128]{1,0:T(8,128)}, f32[2560,128]{1,0:T(8,128)S(1)}, u32[]{:S(2)}) copy-start(f32[2560,128]{1,0:T(8,128)S(1)} %get-tuple-element.27) | copy-start | bytes 3932164
  37.7 2.9 %copy-start.2 = (f32[2560,128]{1,0:T(8,128)}, f32[2560,128]{1,0:T(8,128)S(1)}, u32[]{:S(2)}) copy-start(f32[2560,128]{1,0:T(8,128)S(1)} %get-tuple-element.28) | copy-start | bytes 3932164
  40.5 3.8 %copy-start.8 = (s32[2]{0:T(128)S(1)}, s32[2]{0:T(128)}, u32[]{:S(2)}) copy-start(s32[2]{0:T(128)} %src_x.1) | copy-start | bytes 28
  40.5 3.8 %copy-start.9 = (s32[2]{0:T(128)S(1)}, s32[2]{0:T(128)}, u32[]{:S(2)}) copy-start(s32[2]{0:T(128)} %src_y.1) | copy-start | bytes 28
  40.5 3.8 %copy-start.10 = (s32[2]{0:T(128)S(1)}, s32[2]{0:T(128)}, u32[]{:S(2)}) copy-start(s32[2]{0:T(128)} %src_z.1) | copy-start | bytes 28
  40.7 3.7 %collective-permute-start.6 = (f32[96,4,8,128]{3,2,1,0:T(8,128)S(1)}, f32[96,4,8,128]{3,2,1,0:T(8,128)S(1)}, u32[]{:S(2)}, u32[]{:S(2)}) collective-permute-start(f32[96,4,8,128]{3,2,1,0:T(8,128)S(1)} %pad_maximum_fusion.mine), channel_id=1, source_target_pairs={{0,32},{32,0},{1,33},{33,1},{2,34},{34,2},{3,35},{35,3},{4,36},{36... | collective-permute-start | bytes 4718600 | tf_op jit(solution)/shard_map/ppermute | solution.py:256
  41.0 18.8 %copy-start.1 = (f32[2560,128]{1,0:T(8,128)S(1)}, f32[2560,128]{1,0:T(8,128)}, u32[]{:S(2)}) copy-start(f32[2560,128]{1,0:T(8,128)} %copy-done) | copy-start | bytes 3932164
  41.0 18.8 %copy-start.3 = (f32[2560,128]{1,0:T(8,128)S(1)}, f32[2560,128]{1,0:T(8,128)}, u32[]{:S(2)}) copy-start(f32[2560,128]{1,0:T(8,128)} %copy-done.2) | copy-start | bytes 3932164
  69.9 8.8 %collective-permute-start.7 = (f32[8,256]{1,0:T(8,128)S(1)}, f32[8,256]{1,0:T(8,128)S(1)}, u32[]{:S(2)}, u32[]{:S(2)}) collective-permute-start(f32[8,256]{1,0:T(8,128)S(1)} %get-tuple-element.33), channel_id=1, source_target_pairs={{0,1},{1,0},{2,3},{3,2},{4,5},{5,4},{6,7},{7,6},{8,9},{9,8},{10,11... | collective-permute-start | bytes 24584 | tf_op jit(solution)/shard_map/ppermute | solution.py:256
  74.1 16.9 %all-to-all-start = ((f32[16,4,8,128]{3,2,1,0:T(8,128)}), f32[16,4,8,128]{3,2,1,0:T(8,128)S(1)}, u32[]{:S(2)}, u32[]{:S(2)}) async-start(f32[16,4,8,128]{3,2,1,0:T(8,128)} %bitcast.28), calls=%async_computation | async-start | bytes 524288 | tf_op jit(solution)/shard_map/all_to_all | solution.py:383
  78.9 4.4 %collective-permute-start.10 = (f32[2,64]{1,0:T(2,128)S(1)}, f32[2,64]{1,0:T(2,128)S(1)}, u32[]{:S(2)}, u32[]{:S(2)}) collective-permute-start(f32[2,64]{1,0:T(2,128)S(1)} %get-tuple-element.35), channel_id=1, source_target_pairs={{0,24},{8,0},{16,8},{24,16},{1,25},{9,1},{17,9},{25,17},{2,26},{10... | collective-permute-start | bytes 1544 | tf_op jit(solution)/shard_map/ppermute | solution.py:256
  79.5 3.7 %collective-permute-start.8 = (f32[2,64]{1,0:T(2,128)S(1)}, f32[2,64]{1,0:T(2,128)S(1)}, u32[]{:S(2)}, u32[]{:S(2)}) collective-permute-start(f32[2,64]{1,0:T(2,128)S(1)} %get-tuple-element.34), channel_id=1, source_target_pairs={{0,8},{8,16},{16,24},{24,0},{1,9},{9,17},{17,25},{25,1},{2,10},{10... | collective-permute-start | bytes 1544 | tf_op jit(solution)/shard_map/ppermute | solution.py:256
  81.0 5.1 %collective-permute-start.9 = (f32[2,64]{1,0:T(2,128)S(1)}, f32[2,64]{1,0:T(2,128)S(1)}, u32[]{:S(2)}, u32[]{:S(2)}) collective-permute-start(f32[2,64]{1,0:T(2,128)S(1)} %get-tuple-element.36), channel_id=1, source_target_pairs={{0,16},{8,24},{16,0},{24,8},{1,17},{9,25},{17,1},{25,9},{2,18},{10... | collective-permute-start | bytes 1544 | tf_op jit(solution)/shard_map/ppermute | solution.py:256
